TPU v7x, 128 devices: a whole 4x4x4 slice. The times are simulated.
128 devices in a mesh: ctx: 16 (over x_hi, z, core), tp: 8 (over y, x_lo).
Axes of the slice: x: 4 (x_hi: 2, x_lo: 2; x = x_hi * 2 + x_lo), y: 4, z: 4, core: 2. Of those that a mesh axis runs over, the one named last changes fastest.
Arguments:
- tokens: bfloat16 [8192, 2048], P('ctx'), may hold values from -6 to 6
- cotangent: bfloat16 [8192, 2048], P('ctx'), may hold values from -6 to 6
- segment_ids: int32 [8192], replicated, may hold values from 0 to 2, as said below
- first_gain: float32 [2048], replicated, may hold values from 0.25 to 1.75
- first_shift: float32 [2048], replicated, may hold values from -3 to 3
- second_gain: float32 [2048], replicated, may hold values from 0.25 to 1.75
- second_shift: float32 [2048], replicated, may hold values from -3 to 3
- w_qkv: bfloat16 [2048, 3, 2048], P(None, None, 'tp'), may hold values from -0.125 to 0.125
- qkv_bias: float32 [3, 2048], P(None, 'tp'), may hold values from -3 to 3
- w_out: bfloat16 [2048, 2048], P('tp'), may hold values from -2 to 2
- w_gate_up: bfloat16 [2048, 2, 5632], P(None, None, 'tp'), may hold values from -0.125 to 0.125
- w_down: bfloat16 [5632, 2048], P('tp'), may hold values from -0.078125 to 0.078125
Outputs:
- layer_out: bfloat16 [8192, 2048], P('ctx')
- grad_tokens: bfloat16 [8192, 2048], P('ctx')
- grad_first_gain: float32 [2048], replicated
- grad_first_shift: float32 [2048], replicated
- grad_second_gain: float32 [2048], replicated
- grad_second_shift: float32 [2048], replicated
- grad_w_qkv: float32 [2048, 3, 2048], P('ctx', None, 'tp')
- grad_qkv_bias: float32 [3, 2048], P(None, 'tp')
- grad_w_out: float32 [2048, 2048], P('tp', 'ctx')
- grad_w_gate_up: float32 [2048, 2, 5632], P('ctx', None, 'tp')
- grad_w_down: float32 [5632, 2048], P('tp', 'ctx')
Inputs may be any that keep to these rules, and one draw needn't show every extreme that they name: `segment_ids`: ids never fall from one token to the next, every id appears, document 0 ends within the first 512 tokens and document 2 begins within the last 512 tokens.
All inputs are finite; a program needn't handle non-finite values.
Results may differ from a plain program's by a relative error of at most 0.029.
Values may be sent and summed in bfloat16 or wider, within the bound.
No kernel may reach another device: no remote copies, remote signals or barrier semaphores. Data moves between devices by JAX's collectives and lax.ppermute only.
A program may use at most 192 MiB of HBM per device.

v0:
```python
import functools

import jax
import jax.numpy as jnp
from jax import lax
from jax.experimental import pallas as pl
from jax.experimental.pallas import tpu as pltpu
from jax.sharding import Mesh
from jax.sharding import PartitionSpec as P

HDIM = 64
DOCS = 3
BLOCK = 512
HALF = 256
LOW = jnp.bfloat16
WIDE = jnp.float32
CTX = ("xh", "zh", "zl", "core")
TP = ("y", "xl")
SPREAD = ("xh", "zh")
Z = ("zh", "zl")


def size_of(a):
    return a.size * jnp.dtype(a.dtype).itemsize


def gathered_order(place):
    x, y = place[3], place[4]
    row = [lax.rem(y + k, 4) * 2 for k in range(4)]
    other = 1 - x
    return [
        row[0] + x, row[0] + other,
        row[3] + x, row[1] + x, row[2] + x,
        row[3] + other, row[1] + other, row[2] + other,
    ]


def deal_rows(place, rows, outs):
    tp = place[4] * 2 + place[3]
    for k, out in enumerate(outs):
        out[...] = rows[pl.ds(pl.multiple_of((tp ^ k) * 64, 64), 64), :]


def kernel_call(
    body, outs, inputs, *, small=(), small_outs=(), scalars=(), scratch=(), late=0, flops=0, exps=0, mib=12, quick=False, moved=0
):
    inputs = [a if isinstance(a, (tuple, list)) else (a, 0, a.shape[0]) for a in inputs]
    flat = [x for a in inputs for x in (a if isinstance(a, list) else a[:1])]
    counts = [len(x) for x in (scalars, flat, small, outs, small_outs, inputs, outs)]

    def run(*refs):
        groups, at = [], 0
        for n in counts:
            groups.append(refs[at : at + n])
            at += n
        scalar_refs, far_in, near_in, far_out, near_out, held_in, held_out = groups
        arrived, left, *rest = refs[at:]
        pairs, ends = [], []
        for a, held in zip(inputs, held_in):
            if isinstance(a, list):
                rows = a[0].shape[0]
                for index in gathered_order(scalar_refs[0]):
                    pairs.append((None, held.at[pl.ds(pl.multiple_of(index * rows, rows), rows)]))
            else:
                pairs.append((pl.ds(a[1], a[2]), held))
            ends.append(len(pairs))
        moves = [
            pltpu.make_async_copy(x if part is None else x.at[part], held, arrived.at[k])
            for k, (x, (part, held)) in enumerate(zip(far_in, pairs))
        ]
        for move in moves:
            move.start()
        early = ends[len(inputs) - late - 1]
        for move in moves[:early]:
            move.wait()

        def arrive():
            for move in moves[early:]:
                move.wait()

        body(
            *([arrive] if late else []),
            *scalar_refs, *held_in, *near_in, *held_out, *near_out, *rest,
        )
        moves = [
            pltpu.make_async_copy(a, b, left.at[k]) for k, (a, b) in enumerate(zip(held_out, far_out))
        ]
        for move in moves:
            move.start()
        for move in moves:
            move.wait()

    vmem, hbm = pl.BlockSpec(memory_space=pltpu.VMEM), pl.BlockSpec(memory_space=pltpu.HBM)
    taken = [
        shape_of(8 * a[0].shape[0], a[0].shape[1], kind=a[0].dtype)
        if isinstance(a, list)
        else shape_of(a[2], *a[0].shape[1:], kind=a[0].dtype)
        for a in inputs
    ]
    held = [pltpu.VMEM(a.shape, a.dtype) for a in (*taken, *outs)]
    limit = sum(size_of(a) for a in (*taken, *outs, *small, *small_outs)) + mib * 1024 * 1024
    return pl.pallas_call(
        run,
        out_shape=(*[pltpu.HBM(a.shape, a.dtype) for a in outs], *small_outs),
        in_specs=[pl.BlockSpec(memory_space=pltpu.SMEM)] * len(scalars)
        + [pl.BlockSpec(memory_space=pl.ANY)] * moved
        + [hbm] * (len(flat) - moved)
        + [vmem] * len(small),
        out_specs=(*[hbm] * len(outs), *[vmem] * len(small_outs)),
        scratch_shapes=[
            *held,
            pltpu.SemaphoreType.DMA((len(flat),)),
            pltpu.SemaphoreType.DMA((max(1, len(outs)),)),
            *scratch,
        ],
        compiler_params=pltpu.CompilerParams(vmem_limit_bytes=limit),
        cost_estimate=pl.CostEstimate(
            flops=flops,
            bytes_accessed=0 if quick else sum(size_of(a) for a in (*taken, *outs)),
            transcendentals=exps,
        ),
    )(
        *scalars,
        *flat[:moved],
        *[pltpu.with_memory_space_constraint(a, pltpu.HBM) for a in flat[moved:]],
        *small,
    )


def lane_of(shape):
    return lax.broadcasted_iota(jnp.int32, shape, len(shape) - 1)


def exchange_halves(a, b):
    front = lane_of(a.shape) < HDIM
    return (
        jnp.where(front, a, pltpu.roll(b, HDIM, 1)),
        jnp.where(front, pltpu.roll(a, HDIM, 1), b),
    )


def nt(a, b):
    return lax.dot_general(a, b, (((1,), (1,)), ((), ())), preferred_element_type=WIDE)


def nn(a, b):
    return lax.dot_general(a, b, (((1,), (0,)), ((), ())), preferred_element_type=WIDE)


def turn(x, cosine, sine, sign):
    lane = lax.rem(lane_of(x.shape), HDIM)
    ahead = pltpu.roll(x, x.shape[1] - 8, 1)
    behind = pltpu.roll(x, 8, 1)
    swapped = jnp.where(lane < 8, -ahead, behind) * sign
    return x * cosine + swapped * sine


def rotation_table(angles_table):
    tokens = angles_table.shape[1]
    rest = jnp.zeros((112, tokens), WIDE)
    x = jnp.concatenate([angles_table, rest], axis=0).T
    lane = lane_of(x.shape)
    c = jnp.where(lane < 8, x, 0.0)
    c = c + pltpu.roll(c, 8, 1)
    c = c + pltpu.roll(c, HDIM, 1) + jnp.where(lax.rem(lane, HDIM) < 16, 0.0, 1.0)
    s = jnp.where((lane >= 8) & (lane < 16), x, 0.0)
    s = s + pltpu.roll(s, 120, 1)
    s = s + pltpu.roll(s, HDIM, 1)
    return c, s


def project_kernel(
    arrive, place, tok, table, w, gain, shift, bias,
    normed, stats, x0, x1, x2, x3, cosine_out, sine_out, kept,
):
    rows = 64

    def norm_rows(i, carry):
        at = pl.ds(pl.multiple_of(i * rows, rows), rows)
        x = tok[at, :].astype(WIDE)
        mean = jnp.mean(x, axis=-1, keepdims=True)
        center = x - mean
        scale = lax.rsqrt(jnp.mean(center * center, axis=-1, keepdims=True) + 1e-05)
        normed[at, :] = (center * scale * gain[...] + shift[...]).astype(LOW)
        stats[at, :] = jnp.where(lane_of((rows, 128)) < HDIM, mean, scale)
        return carry

    lax.fori_loop(0, BLOCK // rows, norm_rows, 0)
    cosine, sine = rotation_table(table[...])
    cosine_out[...] = cosine
    sine_out[...] = sine
    arrive()
    mixed = [nn(normed[...], w[c]) + bias[c : c + 1, :] for c in range(3)]
    for pair in range(2):
        lanes = slice(pair * 128, pair * 128 + 128)
        q = turn(mixed[0][:, lanes], cosine, sine, 1.0) * 0.125
        k = turn(mixed[1][:, lanes], cosine, sine, 1.0)
        kv = exchange_halves(k, mixed[2][:, lanes])
        qq = exchange_halves(q[:HALF], q[HALF:])
        for one in range(2):
            kept[2 * pair + one, :BLOCK, :] = kv[one].astype(LOW)
            kept[2 * pair + one, BLOCK:, :] = qq[one].astype(LOW)
    for k, out in enumerate((x0, x1, x2, x3)):
        out[...] = kept[place[1] ^ k]


def padded_queries(q2):
    x = q2.astype(WIDE)
    front = lane_of(x.shape) < HDIM
    return (
        jnp.where(front, x, 0.0).astype(LOW),
        jnp.where(front, pltpu.roll(x, HDIM, 1), 0.0).astype(LOW),
    )


def padded_behind(d2):
    x = d2.astype(WIDE)
    front = lane_of(x.shape) < HDIM
    return (
        jnp.where(front, 0.0, pltpu.roll(x, HDIM, 1)).astype(LOW),
        jnp.where(front, 0.0, x).astype(LOW),
    )


def allowed_keys(key_block, first_query, begin):
    shape = (BLOCK, begin.shape[1])
    key_at = key_block * BLOCK + lax.broadcasted_iota(jnp.int32, shape, 0)
    query_at = first_query + lax.broadcasted_iota(jnp.int32, shape, 1)
    return (key_at <= query_at) & (key_at >= begin)


def for_steps(count, work):
    def pair(i, carry):
        work([2 * i, 2 * i + 1])
        return carry

    lax.fori_loop(0, count // 2, pair, 0)

    @pl.when(lax.rem(count, 2) == 1)
    def _():
        work([count - 1])


def key_blocks(place, rels, t):
    return [4 * t + (place[0] ^ rel) for rel in rels], place[1] ^ t


def forward_kernel(rels, first, last, *refs):
    place, kv0, kv1, q0, q1, q2, q3, begin = refs[:8]
    if first:
        acc_out, peak_out, kvt, queries, kept_q = refs[8:]
    else:
        acc_in, peak_in, o0, o1, o2, o3, out_t, total, kvt, queries, kept_q, kept_o = refs[8:]
        acc_out, peak_out = out_t, total
    me = place[1]
    front = lane_of((BLOCK, 128)) < HDIM
    for k, q in enumerate((q0, q1, q2, q3)):
        kept_q[me ^ k] = q[...]
    for i, kv in enumerate((kv0, kv1)):
        for t in range(4):
            kvt[i, t] = jnp.where(front, 1.0, kv[t].astype(WIDE)).T.astype(LOW)

    def one_query_block(j, carry):
        first_query = (4 * j + place[0]) * BLOCK
        queries[:HALF, :], queries[HALF:, :] = padded_queries(kept_q[j])
        if first:
            peak_out[j] = jnp.full((8, BLOCK), -1e30, WIDE)
            acc_out[j] = jnp.zeros((128, BLOCK), WIDE)
        else:
            peak_out[j] = peak_in[j]
            acc_out[j] = acc_in[j]

        def some_blocks(steps):
            scores, sources = [], []
            for t in steps:
                blocks, at = key_blocks(place, rels, t)
                for i, kv in enumerate((kv0, kv1)):
                    ok = allowed_keys(blocks[i], first_query, begin[j, :1])
                    scores.append(jnp.where(ok, nt(kv[at], queries[...]), -1e30))
                    sources.append((i, at))
            old = peak_out[j, :1]
            new = old
            for one in scores:
                new = jnp.maximum(new, jnp.max(one, axis=0, keepdims=True))
            done = acc_out[j] * jnp.exp(old - new)
            for one, (i, at) in zip(scores, sources):
                done += nn(kvt[i, at], jnp.exp(one - new).astype(LOW))
            acc_out[j] = done
            peak_out[j, :1] = new

        for_steps(j + 1, some_blocks)
        if last:
            weight_sum = acc_out[j, :1]
            done = acc_out[j] / weight_sum
            out_t[j] = done
            total[j, :1] = peak_out[j, :1] + jnp.log(weight_sum)
            rows = done.T
            x, y = rows[:HALF], rows[HALF:]
            kept_o[j] = jnp.where(lane_of(x.shape) < HDIM, pltpu.roll(x, HDIM, 1), y).astype(LOW)
        return carry

    lax.fori_loop(0, 4, one_query_block, 0)
    if last:
        for k, out in enumerate((o0, o1, o2, o3)):
            out[...] = kept_o[me ^ k]


def backward_kernel(rels, first, *refs):
    place, kv0, kv1, q0, q1, q2, q3, d0, d1, d2, d3, out_t, total, begin = refs[:14]
    if first:
        acc, keep, send, kvt, queries, grads, dot_rows, dkv, kept_q, kept_d = refs[14:]
    else:
        (
            acc_in, g0, g1, g2, g3, keep, send,
            kvt, queries, grads, dot_rows, dkv, kept_q, kept_d, acc, kept_g,
        ) = refs[14:]
    me = place[1]
    for k in range(4):
        kept_q[me ^ k] = (q0, q1, q2, q3)[k][...]
        kept_d[me ^ k] = (d0, d1, d2, d3)[k][...]
    for i, kv in enumerate((kv0, kv1)):
        for t in range(4):
            kvt[i, t] = kv[t].astype(WIDE).T.astype(LOW)
    dkv[...] = jnp.zeros(dkv.shape, WIDE)

    def one_query_block(j, carry):
        first_query = (4 * j + place[0]) * BLOCK
        queries[:HALF, :], queries[HALF:, :] = padded_queries(kept_q[j])
        grads[:HALF, :], grads[HALF:, :] = padded_behind(kept_d[j])
        dot_rows[...] = jnp.sum(grads[...].astype(WIDE).T * out_t[j], axis=0, keepdims=True)
        acc[j] = jnp.zeros((128, BLOCK), WIDE) if first else acc_in[j]

        def some_blocks(steps):
            for t in steps:
                blocks, at = key_blocks(place, rels, t)
                for i, kv in enumerate((kv0, kv1)):
                    term = 0.0
                    for half in range(2):
                        some = slice(half * HALF, half * HALF + HALF)
                        ok = allowed_keys(blocks[i], first_query + half * HALF, begin[j, :1, some])
                        scores = nt(kv[at], queries[some, :])
                        probs = jnp.where(ok, jnp.exp(scores - total[j, :1, some]), 0.0)
                        grad_probs = nt(kv[at], grads[some, :])
                        grad_scores = (probs * (grad_probs - dot_rows[:, some])).astype(LOW)
                        term += nn(grad_scores, queries[some, :])
                        term += nn(probs.astype(LOW), grads[some, :])
                        acc[j, :, some] += nn(kvt[i, at], grad_scores)
                    dkv[i, at] += term

        for_steps(j + 1, some_blocks)
        if not first:
            rows = acc[j].T
            x, y = rows[:HALF], rows[HALF:]
            kept_g[j] = jnp.where(lane_of(x.shape) < HDIM, x, pltpu.roll(y, HDIM, 1)).astype(LOW)
        return carry

    lax.fori_loop(0, 4, one_query_block, 0)
    if not first:
        for k, out in enumerate((g0, g1, g2, g3)):
            out[...] = kept_g[me ^ k]
    for t in range(4):
        keep[t] = dkv[0, t].astype(LOW)
        send[t] = dkv[1, t].astype(LOW)


def branch_kernel(arrive, place, h0, h1, h2, h3, w, attended, *refs):
    outs, (partial, kept) = refs[:8], refs[8:]
    for k, h in enumerate((h0, h1, h2, h3)):
        kept[place[1] ^ k] = h[...]
    for pair in range(2):
        lanes = slice(pair * 128, pair * 128 + 128)
        x, y = exchange_halves(kept[2 * pair].astype(WIDE), kept[2 * pair + 1].astype(WIDE))
        attended[:HALF, lanes] = x.astype(LOW)
        attended[HALF:, lanes] = y.astype(LOW)
    arrive()
    for n in range(4):
        at = slice(n * 512, n * 512 + 512)
        partial[:, at] = nn(attended[...], w[:, at]).astype(LOW)
    deal_rows(place, partial, outs)


def grad_attended_kernel(place, grad, w, d0, d1, d2, d3, kept):
    g = nt(grad[...], w[...])
    for pair in range(2):
        lanes = slice(pair * 128, pair * 128 + 128)
        both = exchange_halves(g[:HALF, lanes], g[HALF:, lanes])
        for one in range(2):
            kept[2 * pair + one] = both[one].astype(LOW)
    for k, out in enumerate((d0, d1, d2, d3)):
        out[...] = kept[place[1] ^ k]


def join_kernel(keep, received, far, g0, g1, g2, g3, x0, x1, x2, x3):
    for k in range(4):
        total = keep[k].astype(WIDE) + received[k].astype(WIDE) + far[k].astype(WIDE)
        out = (x0, x1, x2, x3)[k]
        out[:BLOCK, :] = total.astype(LOW)
        out[BLOCK:, :] = (g0, g1, g2, g3)[k][...]


def grad_project_kernel(
    arrive, place, x0, x1, x2, x3, cosine, sine, tok, stats, w,
    grad_mixed, partial, gain_sum, shift_sum, bias_sum, parts, kept,
):
    for k, x in enumerate((x0, x1, x2, x3)):
        parts[place[1] ^ k] = x[:BLOCK, :]
        kept[place[1] ^ k] = x[BLOCK:, :]
    for pair in range(2):
        lanes = slice(pair * 128, pair * 128 + 128)
        k, v = exchange_halves(parts[2 * pair].astype(WIDE), parts[2 * pair + 1].astype(WIDE))
        q = exchange_halves(kept[2 * pair].astype(WIDE), kept[2 * pair + 1].astype(WIDE))
        q = jnp.concatenate(q, axis=0)
        q = turn(q, cosine[...], sine[...], -1.0) * 0.125
        k = turn(k, cosine[...], sine[...], -1.0)
        for c, part in enumerate((q, k, v)):
            start = c * 256 + pair * 128
            low = part.astype(LOW)
            grad_mixed[:, start : start + 128] = low
            bias_sum[c : c + 1, lanes] = jnp.sum(low.astype(WIDE), axis=0, keepdims=True)
    arrive()
    mean, scale = stats[:, 0:1], stats[:, 64:65]
    for n in range(4):
        at = slice(n * 512, n * 512 + 512)
        total = nt(grad_mixed[:, :256], w[0, at, :])
        total += nt(grad_mixed[:, 256:512], w[1, at, :])
        total += nt(grad_mixed[:, 512:], w[2, at, :])
        partial[:, at] = total.astype(LOW)
        normal = (tok[:, at].astype(WIDE) - mean) * scale
        gain_sum[:, at] = jnp.sum(total * normal, axis=0, keepdims=True)
        shift_sum[:, at] = jnp.sum(total, axis=0, keepdims=True)


def hidden_gradient_kernel(cot, w, grad_hidden):
    grad_hidden[...] = nt(cot[...], w[...])


def feed_kernel(arrive, place, second, w_gate, w_up, grad_hidden, hidden, grad_gate, grad_up, partial):
    gate = nt(second[...], w_gate[0])
    arrive()
    up = nt(second[...], w_up[0])
    sigmoid = 1.0 / (1.0 + jnp.exp(-gate))
    activated = gate * sigmoid
    hidden[...] = (activated * up).astype(LOW)
    grad = grad_hidden[...]
    grad_up[...] = (grad * activated).astype(LOW)
    grad_gate[...] = (grad * up * sigmoid * (1.0 + gate * (1.0 - sigmoid))).astype(LOW)
    for n in range(4):
        at = slice(n * 512, n * 512 + 512)
        partial[:, at] = (nn(grad_gate[...], w_gate[0, :, at]) + nn(grad_up[...], w_up[0, :, at])).astype(LOW)


def for_rows(work):
    rows = 16

    def one(i, carry):
        work(pl.ds(pl.multiple_of(i * rows, rows), rows))
        return carry

    lax.fori_loop(0, 64 // rows, one, 0)


def summed(parts, at):
    one = [parts[k][at, :] for k in range(8)] if isinstance(parts, tuple) else [parts[k, at, :] for k in range(8)]
    total = one[0].astype(WIDE)
    for x in one[1:]:
        total += x.astype(WIDE)
    return total


def second_norm_kernel(*refs):
    parts, (tok, gain, shift, low, middle, normal, stats) = refs[:8], refs[8:]

    def work(at):
        x = tok[at, :].astype(WIDE) + summed(parts, at)
        center = x - jnp.mean(x, axis=-1, keepdims=True)
        scale = lax.rsqrt(jnp.mean(center * center, axis=-1, keepdims=True) + 1e-05)
        rows = center * scale
        low[at, :] = (rows * gain[...] + shift[...]).astype(LOW)
        middle[at, :] = x
        normal[at, :] = rows
        stats[at, :] = jnp.broadcast_to(scale, (scale.shape[0], 128))

    for_rows(work)


def norm_gradient(grad, rows, scale, gain):
    scaled = grad * gain
    return scale * (
        scaled
        - jnp.mean(scaled, axis=-1, keepdims=True)
        - rows * jnp.mean(scaled * rows, axis=-1, keepdims=True)
    )


def second_gradient_kernel(parts, cot, normal, stats, gain, copies, grad_middle, sums):
    sums[...] = jnp.zeros(sums.shape, WIDE)

    def work(at):
        grad, rows = summed(parts, at), normal[at, :]
        done = cot[at, :].astype(WIDE) + norm_gradient(grad, rows, stats[at, 0:1], gain[...])
        low = done.astype(LOW)
        for k in range(8):
            copies[k, at, :] = low
        grad_middle[at, :] = done
        sums[0:1, :] += jnp.sum(grad * rows, axis=0, keepdims=True)
        sums[1:2, :] += jnp.sum(grad, axis=0, keepdims=True)

    for_rows(work)


def feed_sum_kernel(place, parts, middle, out):
    rows = 16
    mine = place[3]

    def one(i, carry):
        at = pl.ds(pl.multiple_of(i * rows, rows), rows)
        total = parts[0, at, :].astype(WIDE)
        for k in range(1, 4):
            total += parts[k, at, :].astype(WIDE)
        here = i * rows - mine * 64
        own = pl.ds(pl.multiple_of(jnp.clip(here, 0, 64 - rows), rows), rows)
        inside = (here >= 0) & (here < 64)
        out[at, :] = (total + jnp.where(inside, middle[own, :], 0.0)).astype(LOW)
        return carry

    lax.fori_loop(0, 128 // rows, one, 0)


def layer_out_kernel(a, b, copies):
    rows = 16

    def one(i, carry):
        at = pl.ds(pl.multiple_of(i * rows, rows), rows)
        low = (a[at, :].astype(WIDE) + b[at, :].astype(WIDE)).astype(LOW)
        for k in range(4):
            copies[k, at, :] = low
        return carry

    lax.fori_loop(0, 128 // rows, one, 0)


def first_gradient_kernel(parts, grad_middle, tok, stats, vectors, gain, low):
    def work(at):
        mean, scale = stats[at, 0:1], stats[at, 64:65]
        rows = (tok[at, :].astype(WIDE) - mean) * scale
        done = norm_gradient(summed(parts, at), rows, scale, gain[...])
        low[at, :2048] = (grad_middle[at, :] + done).astype(LOW)
        low[at, 2048:] = vectors[at, :].astype(LOW)

    for_rows(work)


def last_kernel(place, gathered, out, total):
    out[...] = gathered[:, :2048]
    done = gathered[:64, 2048:].astype(WIDE)
    for k in range(1, 8):
        done += gathered[k * 64 : k * 64 + 64, 2048:].astype(WIDE)
    total[...] = done


def weight_kernel(widths, sources, arrive, place, *refs):
    count = max(max(pair) for pair in sources) + 1
    inputs = refs[:count]
    mine, theirs, turned = refs[count:]
    first_core = place[2] == 0
    start = 0
    for n, ((left, right), width) in enumerate(zip(sources, widths)):
        if n == 1:
            arrive()
        left, right = inputs[left], inputs[right]
        turned[:width, :] = left[...].astype(WIDE).T.astype(LOW)

        def one(n, carry, start=start, right=right, width=width):
            columns = right[:, pl.ds(pl.multiple_of(n * 256, 256), 256)]
            both = nn(turned[:width, :], columns)
            first, second = both[:, :128], both[:, 128:]
            at = pl.ds(start, width)
            mine[n, at, :] = jnp.where(first_core, first, second).astype(LOW)
            theirs[n, at, :] = jnp.where(first_core, second, first).astype(LOW)
            return carry

        lax.fori_loop(0, 8, one, 0, unroll=4)
        start += width


def weight_grads(pairs, place):
    inputs, sources = [], []
    for pair in pairs:
        for a in pair:
            if not any(a is b for b in inputs):
                inputs.append(a)
        sources.append(tuple(next(k for k, b in enumerate(inputs) if b is a) for a in pair))
    widths = tuple(a.shape[1] for a, _ in pairs)
    out = jax.ShapeDtypeStruct((8, sum(widths), 128), LOW)
    return kernel_call(
        functools.partial(weight_kernel, widths, sources),
        (out, out),
        inputs,
        scalars=(place,),
        scratch=(pltpu.VMEM((max(widths), BLOCK), LOW),),
        late=len(inputs) - 2,
        quick=True,
    )


def swapped(x, axis):
    return lax.ppermute(x, axis, [(0, 1), (1, 0)])


def across(pieces):
    moved = [
        lax.ppermute(pieces[k], SPREAD, [(i, i ^ k) for i in range(4)]) for k in range(1, 4)
    ]
    return (pieces[0], *moved)


def z_parts_kernel(place, mine, received, *refs):
    outs, (held_a, held_b, done, came, went) = refs[:4], refs[4:]
    z = place[0]
    order = [(k, xh) for k in (1, 3, 2, 0) for xh in range(2)]
    moves = []
    for n, (k, xh) in enumerate(order):
        at = xh * 4 + lax.rem(z + k, 4)
        moves.append(
            (
                pltpu.make_async_copy(mine.at[at], held_a.at[n], came.at[2 * n]),
                pltpu.make_async_copy(received.at[at], held_b.at[n], came.at[2 * n + 1]),
                pltpu.make_async_copy(done.at[n], outs[k].at[xh], went.at[n]),
            )
        )
    for a, b, _ in moves:
        a.start()
        b.start()
    for n, (a, b, out) in enumerate(moves):
        a.wait()
        b.wait()
        done[n] = (held_a[n].astype(WIDE) + held_b[n].astype(WIDE)).astype(LOW)
        out.start()
    for _, _, out in moves:
        out.wait()


def z_parts(mine, received):
    rows = mine.shape[1]
    hbm = pl.BlockSpec(memory_space=pltpu.HBM)
    held = pltpu.VMEM((8, rows, 128), LOW)
    return pl.pallas_call(
        z_parts_kernel,
        in_specs=[pl.BlockSpec(memory_space=pltpu.SMEM), hbm, hbm],
        out_specs=[hbm] * 4,
        out_shape=[pltpu.HBM((2, rows, 128), LOW)] * 4,
        scratch_shapes=[
            held,
            held,
            held,
            pltpu.SemaphoreType.DMA((16,)),
            pltpu.SemaphoreType.DMA((8,)),
        ],
        compiler_params=pltpu.CompilerParams(vmem_limit_bytes=24 * 1024 * 1024),
        cost_estimate=pl.CostEstimate(flops=0, bytes_accessed=0, transcendentals=0),
    )(
        lax.axis_index(Z).reshape(1),
        *[pltpu.with_memory_space_constraint(a, pltpu.HBM) for a in (mine, received)],
    )


def settled_kernel(x, out, held, came, went):
    rows = x.shape[1]
    moves = []
    for k in range(x.shape[0]):
        at = pl.ds(k * rows, rows)
        moves.append(
            (
                pltpu.make_async_copy(x.at[k], held.at[k], came.at[k]),
                pltpu.make_async_copy(held.at[k, :, pl.ds(0, 2048)], out.at[at], went.at[k]),
            )
        )
    for come, _ in moves:
        come.start()
    for come, go in moves:
        come.wait()
        go.start()
    for _, go in moves:
        go.wait()


def settled(x):
    hbm = pl.BlockSpec(memory_space=pltpu.HBM)
    parts, rows = x.shape[:2]
    return pl.pallas_call(
        settled_kernel,
        out_shape=pltpu.HBM((parts * rows, 2048), x.dtype),
        in_specs=[pl.BlockSpec(memory_space=pl.ANY)],
        out_specs=hbm,
        scratch_shapes=[
            pltpu.VMEM(x.shape, x.dtype),
            pltpu.SemaphoreType.DMA((parts,)),
            pltpu.SemaphoreType.DMA((parts,)),
        ],
        compiler_params=pltpu.CompilerParams(vmem_limit_bytes=8 * 1024 * 1024),
        cost_estimate=pl.CostEstimate(flops=0, bytes_accessed=0, transcendentals=0),
    )(x)


def z_permute(part, distance):
    return lax.ppermute(part, Z, [(i, (i + distance) % 4) for i in range(4)])


def xh_halves(moved):
    xh = lax.axis_index("xh")

    def added(at):
        return sum(lax.dynamic_index_in_dim(x, at, 0, False).astype(WIDE) for x in moved)

    return added(xh), added(1 - xh).astype(LOW)


def dealt(x, axis):
    return lax.all_to_all(x, axis, split_axis=0, concat_axis=0, tiled=True)


def tp_parts(partial):
    return dealt(partial.reshape(8, -1, partial.shape[1]), TP)


def y_moved(x, distance):
    return lax.ppermute(x, "y", [(i, (i + distance) % 4) for i in range(4)])


def scattered(pieces):
    moved = {
        k: lax.ppermute(pieces[k], TP, [(i, i ^ k) for i in range(8)]) for k in (5, 4, 7, 3, 6, 2, 1)
    }
    return [pieces[0], *[moved[k] for k in range(1, 8)]]


def gathered(share, *beside):
    across_x, *beside = lax.optimization_barrier((swapped(share, "xl"), *beside))
    back, ahead, far = (y_moved(share, k) for k in (1, 3, 2))
    shares = [
        share, across_x, back, ahead, far,
        y_moved(across_x, 1), y_moved(across_x, 3), swapped(far, "xl"),
    ]
    return (shares, *beside) if beside else shares


def summed_by_pairs(x, pairs):
    for axis, size, distance in pairs:
        x = x + lax.ppermute(x, axis, [(i, i ^ distance) for i in range(size)])
    return x


def shape_of(*dims, kind=LOW):
    return jax.ShapeDtypeStruct(dims, kind)


def body(
    tokens, cotangent, segment_ids, first_gain, first_shift, second_gain, second_shift,
    w_qkv, qkv_bias, w_out, w_gate_up, w_down,
):
    ctx = lax.axis_index(CTX)
    tp = lax.axis_index(TP)
    group = lax.axis_index(("zl", "core"))
    place = jnp.stack(
        [group, lax.axis_index(SPREAD), lax.axis_index("core"), lax.axis_index("xl"), lax.axis_index("y")]
    )
    tied = lax.optimization_barrier

    def my_share(array):
        return lax.dynamic_slice_in_dim(array, tp * 64, 64)

    labels = jnp.arange(DOCS, dtype=jnp.int32)
    starts = jnp.sum((segment_ids[None, :] < labels[:, None]).astype(jnp.int32), axis=1)
    begins = jnp.sum(
        jnp.where(segment_ids[None, :] == labels[:, None], starts[:, None], 0), axis=0
    )
    begin = lax.dynamic_index_in_dim(begins.reshape(4, 4, 1, BLOCK), group, 1, False)
    begin = jnp.broadcast_to(begin, (4, 8, BLOCK))
    own = lax.dynamic_slice_in_dim(begins, ctx * BLOCK, BLOCK)
    places = ctx * BLOCK + jnp.arange(BLOCK, dtype=jnp.int32) - own
    frequency = 10000.0 ** (-jnp.arange(8, dtype=WIDE) / 8.0)
    angles = frequency[:, None] * places.astype(WIDE)[None, :]
    table = jnp.concatenate([jnp.cos(angles), jnp.sin(angles)], axis=0)

    w3 = jnp.transpose(w_qkv, (1, 0, 2))
    w2 = jnp.transpose(w_gate_up, (1, 2, 0))
    quarter, piece = shape_of(HALF, 128), shape_of(BLOCK + HALF, 128)
    wide_block = shape_of(BLOCK, 128, kind=WIDE)
    four = pltpu.VMEM((4, HALF, 128), LOW)
    normed_low, stats1, *packed, cosine, sine = kernel_call(
        project_kernel,
        (shape_of(BLOCK, 2048), wide_block, *[piece] * 4, wide_block, wide_block),
        (tokens, table, w3),
        small=(first_gain[None], first_shift[None], qkv_bias),
        scalars=(place,),
        scratch=(pltpu.VMEM((4, BLOCK + HALF, 128), LOW),),
        late=1,
        flops=2 * 512 * 2048 * 768,
    )
    (grad_hidden,) = kernel_call(
        hidden_gradient_kernel,
        (shape_of(BLOCK, 704, kind=WIDE),),
        (cotangent, w_down),
        flops=2 * 512 * 2048 * 704,
    )
    *packed, grad_hidden, tok_share, cot_share = tied(
        (*across(packed), grad_hidden, my_share(tokens), my_share(cotangent))
    )
    kv = jnp.stack([x[:BLOCK] for x in packed])
    queries = [(x, BLOCK, HALF) for x in packed]
    kv_c = swapped(kv, "core")
    state = (shape_of(4, 128, BLOCK, kind=WIDE), shape_of(4, 8, BLOCK, kind=WIDE))
    acc, peak = kernel_call(
        functools.partial(forward_kernel, (0, 1), True, False),
        state,
        (kv, kv_c, *queries, begin),
        scalars=(place,),
        scratch=(pltpu.VMEM((2, 4, 128, BLOCK), LOW), pltpu.VMEM((BLOCK, 128), LOW), four),
        flops=20 * 4 * BLOCK * BLOCK * 128,
        exps=20 * BLOCK * BLOCK,
        mib=24,
    )
    acc, peak, kv_z = tied((acc, peak, swapped(kv, "zl")))
    kv_zc = swapped(kv_z, "core")
    *heads, out_t, total = kernel_call(
        functools.partial(forward_kernel, (2, 3), False, True),
        (*[quarter] * 4, *state),
        (kv_z, kv_zc, *queries, begin, acc, peak),
        scalars=(place,),
        scratch=(pltpu.VMEM((2, 4, 128, BLOCK), LOW), pltpu.VMEM((BLOCK, 128), LOW), four, four),
        flops=20 * 4 * BLOCK * BLOCK * 128,
        exps=20 * BLOCK * BLOCK,
        mib=24,
    )
    heads = across(heads)
    share, low_share = shape_of(64, 2048, kind=WIDE), shape_of(64, 2048)
    attended_low, *partial_branch = kernel_call(
        branch_kernel,
        (shape_of(BLOCK, 256), *[low_share] * 8),
        (*heads, w_out),
        scalars=(place,),
        scratch=(pltpu.VMEM((BLOCK, 2048), LOW), four),
        late=1,
        flops=2 * 512 * 256 * 2048,
    )
    branch_parts = scattered(partial_branch)
    second_share, middle, second_rows, stats2 = kernel_call(
        second_norm_kernel,
        (low_share, share, share, shape_of(64, 128, kind=WIDE)),
        (*branch_parts, tok_share),
        small=(second_gain[None], second_shift[None]),
    )
    second_low = gathered(second_share)
    strip = shape_of(BLOCK, 704)
    hidden_low, grad_gate, grad_up, partial_second = kernel_call(
        feed_kernel,
        (strip, strip, strip, shape_of(BLOCK, 2048)),
        (second_low, (w2, 0, 1), (w2, 1, 1), grad_hidden),
        scalars=(place,),
        late=2,
        flops=8 * 512 * 2048 * 704,
        mib=24,
    )
    second_parts = tp_parts(partial_second)

    feed_mine, feed_theirs = weight_grads(
        ((grad_gate, second_low), (grad_up, second_low), (hidden_low, cotangent)), place
    )
    second_parts, feed_mine, feed_theirs = tied((second_parts, feed_mine, feed_theirs))
    copies, grad_middle, second_sums = kernel_call(
        second_gradient_kernel,
        (shape_of(8, 64, 2048), share),
        (second_parts, cot_share, second_rows, stats2),
        moved=1,
        small=(second_gain[None],),
        small_outs=(shape_of(2, 2048, kind=WIDE),),
    )
    grad_branch = dealt(copies, TP).reshape(BLOCK, 2048)
    partial_feed = jnp.dot(hidden_low, w_down, preferred_element_type=WIDE).astype(LOW)
    grad_branch, partial_feed = tied((grad_branch, partial_feed))
    feed_z = z_parts(feed_mine, swapped(feed_theirs, "core"))
    feed_1, feed_3 = z_permute(feed_z[1], 1), z_permute(feed_z[3], 3)
    grads = kernel_call(
        grad_attended_kernel,
        (*[quarter] * 4,),
        (grad_branch, w_out),
        moved=1,
        scalars=(place,),
        scratch=(four,),
        flops=2 * 512 * 256 * 2048,
    )
    feed_1, feed_3, partial_feed, *grads = tied((feed_1, feed_3, partial_feed, *grads))
    feed_parts = dealt(partial_feed.reshape(4, 128, 2048), "y")
    *grads, feed_2 = tied((*across(grads), feed_z[2]))
    feed_2 = z_permute(feed_2, 2)
    scratch = (
        pltpu.VMEM((2, 4, 128, BLOCK), LOW),
        pltpu.VMEM((BLOCK, 128), LOW),
        pltpu.VMEM((BLOCK, 128), LOW),
        pltpu.VMEM((1, BLOCK), WIDE),
        pltpu.VMEM((2, 4, BLOCK, 128), WIDE),
        four,
        four,
    )
    blocks = shape_of(4, BLOCK, 128)
    acc, keep1, send1 = kernel_call(
        functools.partial(backward_kernel, (2, 3), True),
        (state[0], blocks, blocks),
        (kv_z, kv_zc, *queries, *grads, out_t, total, begin),
        scalars=(place,),
        scratch=scratch,
        flops=20 * 10 * BLOCK * BLOCK * 128,
        exps=20 * BLOCK * BLOCK,
        mib=28,
    )
    acc, send1, feed_parts, feed_2 = tied((acc, send1, feed_parts, feed_2))
    (feed_half,) = kernel_call(
        feed_sum_kernel,
        (shape_of(128, 2048),),
        (feed_parts, middle),
        scalars=(place,),
        moved=1,
    )
    far = (keep1.astype(WIDE) + swapped(send1, "core").astype(WIDE)).astype(LOW)
    acc, far, feed_half = tied((acc, far, feed_half))
    near = kernel_call(
        functools.partial(backward_kernel, (0, 1), False),
        (*[quarter] * 4, blocks, blocks),
        (kv, kv_c, *queries, *grads, out_t, total, begin, acc),
        scalars=(place,),
        scratch=(*scratch, pltpu.VMEM((4, 128, BLOCK), WIDE), four),
        flops=20 * 10 * BLOCK * BLOCK * 128,
        exps=20 * BLOCK * BLOCK,
        mib=28,
    )
    *near, far, feed_other = tied((*near, swapped(far, "zl"), swapped(feed_half, "xl")))
    *grad_queries, keep0, send0 = near
    pieces = kernel_call(
        join_kernel,
        (*[piece] * 4,),
        (keep0, swapped(send0, "core"), far, *grad_queries),
    )
    (copies4,) = kernel_call(layer_out_kernel, (shape_of(4, 128, 2048),), (feed_half, feed_other))
    feed_keep, feed_send = xh_halves([feed_z[0], feed_1, feed_2, feed_3])
    *pieces, copies4, feed_send = tied((*pieces, copies4, feed_send))
    *pieces, feed_send = tied((*across(pieces), feed_send))
    feed_received = swapped(feed_send, "xh")
    layer_out = dealt(copies4, "y")
    grad_mixed, partial_normed, gain_sum, shift_sum, bias_sum = kernel_call(
        grad_project_kernel,
        (shape_of(BLOCK, 768), shape_of(BLOCK, 2048)),
        (*pieces, cosine, sine, tokens, stats1, w3),
        small_outs=(
            shape_of(1, 2048, kind=WIDE),
            shape_of(1, 2048, kind=WIDE),
            shape_of(3, 256, kind=WIDE),
        ),
        scalars=(place,),
        scratch=(pltpu.VMEM((4, BLOCK, 128), LOW), four),
        late=3,
        flops=2 * 512 * 2048 * 768,
    )
    partial_normed, layer_out = tied((partial_normed, layer_out))
    layer_out = settled(layer_out)
    normed_parts = tp_parts(partial_normed)

    rest_mine, rest_theirs = weight_grads(
        ((grad_mixed, normed_low), (attended_low, grad_branch)), place
    )
    rest_mine, rest_theirs, feed_received = tied((rest_mine, rest_theirs, feed_received))
    rest_z = z_parts(rest_mine, swapped(rest_theirs, "core"))
    vectors = jnp.concatenate([gain_sum, shift_sum, second_sums], axis=0).reshape(32, 256)
    vectors = jnp.concatenate([vectors, bias_sum], axis=0)
    vectors = summed_by_pairs(vectors, (("core", 2, 1), ("zl", 2, 1), ("zh", 2, 1)))
    vectors, *rest_z = tied((vectors, *rest_z))
    vectors = summed_by_pairs(vectors, (("xh", 2, 1),))
    rest_1, rest_3 = z_permute(rest_z[1], 1), z_permute(rest_z[3], 3)
    normed_parts, vectors = tied((normed_parts, vectors))
    bias_grad = vectors[32:]
    (last_share,) = kernel_call(
        first_gradient_kernel,
        (shape_of(64, 2048 + 128),),
        (normed_parts, grad_middle, tok_share, my_share(stats1), vectors[:32].reshape(64, 128)),
        moved=1,
        small=(first_gain[None],),
    )
    last_shares, rest_1, rest_3 = gathered(last_share, rest_1, rest_3)
    grad_tokens, vectors = kernel_call(
        last_kernel,
        (shape_of(BLOCK, 2048),),
        (last_shares,),
        scalars=(place,),
        small_outs=(shape_of(64, 128, kind=WIDE),),
        quick=True,
    )
    vectors = vectors.reshape(4, 2048)
    rest_z = (rest_z[0], rest_1, z_permute(rest_z[2], 2), rest_3)
    rest_keep, rest_send = xh_halves(rest_z)
    rest_w = rest_keep + swapped(rest_send, "xh").astype(WIDE)
    feed_w = feed_keep + feed_received.astype(WIDE)
    return (
        layer_out,
        grad_tokens,
        vectors[0],
        vectors[1],
        vectors[2],
        vectors[3],
        jnp.transpose(rest_w[:768].reshape(3, 256, 128), (2, 0, 1)),
        bias_grad,
        rest_w[768:],
        jnp.transpose(feed_w[:1408].reshape(2, 704, 128), (2, 0, 1)),
        feed_w[1408:],
    )


def solution(mesh):
    fine = Mesh(
        mesh.devices.reshape(2, 2, 2, 2, 4, 2), ("xh", "zh", "zl", "core", "y", "xl")
    )
    rows = P(CTX, None)
    return jax.shard_map(
        body,
        mesh=fine,
        in_specs=(
            rows, rows, P(), P(), P(), P(), P(),
            P(None, None, TP), P(None, TP), P(TP, None), P(None, None, TP), P(TP, None),
        ),
        out_specs=(
            rows, rows, P(), P(), P(), P(),
            P(CTX, None, TP), P(None, TP), P(TP, CTX), P(CTX, None, TP), P(TP, CTX),
        ),
        check_vma=False,
    )
```

profile of v0, /device:TPU:104, one launch (start us, length us, event | category | flops | bytes accessed | tf_op | source)
XLA Modules:
  0.0 403.7 jit_solution(10788563009316475213)
XLA Ops:
  5.6 8.7 %shard_map.203 = (bf16[512,2048]{1,0:T(8,128)(2,1)}, f32[512,128]{1,0:T(8,128)}, bf16[768,128]{1,0:T(8,128)(2,1)}, bf16[768,128]{1,0:T(8,128)(2,1)}, bf16[768,12...) custom-call(s32[5]{0:T(128)S(1)} %stack.38.refs_0_, ...), custom_call_target="tpu_custom_call" | custom-call | flops 1610612736 | bytes 8945664 | tf_op jit(solution)/shard_map/pallas_call | solution.py:102
  14.9 3.0 collective-permute-start.1
  18.0 2.9 collective-permute-start.2
  20.9 5.5 %shard_map.204.refs_11_ = f32[512,704]{1,0:T(8,128)} custom-call(bf16[512,2048]{1,0:T(8,128)(2,1)} %refs_12_.1, bf16[704,2048]{1,0:T(8,128)(2,1)} %refs_1_.3), custom_call_target="tpu_custom_call" | custom-call | flops 1476395008 | bytes 6422528 | tf_op jit(solution)/shard_map/pallas_call | solution.py:102
  32.6 12.6 %shard_map.205 = (f32[4,128,512]{2,1,0:T(8,128)}, f32[4,8,512]{2,1,0:T(8,128)}) custom-call(s32[5]{0:T(128)S(1)} %stack.38.refs_0_, bf16[4,512,128]{2,1,0:T(8,128)(2,1)} %copy-done.17, bf16[4,512,128]{2,1,0:T(8,128)(2,1)} %copy-done.43, bf16[768,128]{1,0:T(8,128)(2,1)} %get-tuple-element.155.refs_3_, bf16[768,128]{1,0:T(8,128)(2,1)} %copy-done.40, ...), custom_call_target="tpu_custom_call" | custom-call | flops 2684354560 | bytes 2490368 | tf_op jit(solution)/shard_map/pallas_call | solution.py:102
  48.3 14.1 %shard_map.206 = (bf16[256,128]{1,0:T(8,128)(2,1)}, bf16[256,128]{1,0:T(8,128)(2,1)}, bf16[256,128]{1,0:T(8,128)(2,1)}, bf16[256,128]{1,0:T(8,128)(2,1)}, f32[4,128,512]{2,1,0:T(8,128)}, /*index=5*/f32[4,8,512]{2,1,0:T(8,128)}) custom-call(s32[5]{0:T(128)S(1)} %stack.38.refs_0_, bf16[4,512,128]{2,1,0:T(8,128)(2,1)} %copy-done.44, ...), custom_call_target="tpu_custom_call" | custom-call | flops 2684354560 | bytes 3866624 | tf_op jit(solution)/shard_map/pallas_call | solution.py:102
  66.1 2.9 collective-permute-start.8
  70.0 4.5 %collective-permute-done.8.refs_4_ = bf16[256,128]{1,0:T(8,128)(2,1)S(1)} collective-permute-done((bf16[256,128]{1,0:T(8,128)(2,1)}, bf16[256,128]{1,0:T(8,128)(2,1)S(1)}, u32[]{:S(2)}, u32[]{:S(2)}) %collective-permute-start.8) | collective-permute-done | bytes 65568 | tf_op jit(solution)/shard_map/ppermute | solution.py:612
  75.1 4.1 %shard_map.207 = (bf16[512,256]{1,0:T(8,128)(2,1)}, bf16[64,2048]{1,0:T(8,128)(2,1)}, bf16[64,2048]{1,0:T(8,128)(2,1)}, bf16[64,2048]{1,0:T(8,128)(2,1)}, bf16[6...) custom-call(s32[5]{0:T(128)S(1)} %stack.38.refs_0_, ...), custom_call_target="tpu_custom_call" | custom-call | flops 536870912 | bytes 3670016 | tf_op jit(solution)/shard_map/pallas_call | solution.py:102
  90.3 10.6 %collective-permute-done.10.refs_2_ = bf16[64,2048]{1,0:T(8,128)(2,1)S(1)} collective-permute-done((bf16[64,2048]{1,0:T(8,128)(2,1)}, bf16[64,2048]{1,0:T(8,128)(2,1)S(1)}, u32[]{:S(2)}, u32[]{:S(2)}) %collective-permute-start.10) | collective-permute-done | bytes 262176 | tf_op jit(solution)/shard_map/ppermute | solution.py:732
  100.9 3.3 collective-permute-start.15
  105.9 3.8 collective-permute-done.14.refs_6_
  110.5 3.9 shard_map.208
  132.5 12.7 %shard_map.209 = (bf16[512,704]{1,0:T(8,128)(2,1)}, bf16[512,704]{1,0:T(8,128)(2,1)}, bf16[512,704]{1,0:T(8,128)(2,1)}, bf16[512,2048]{1,0:T(8,128)(2,1)}) custom-call(s32[5]{0:T(128)S(1)} %stack.38.refs_0_, bf16[64,2048]{1,0:T(8,128)(2,1)} %get-tuple-element.177.refs_1_.refs_2_, bf16[64,2048]{1,0:T(8,128)(2,1)} %copy-done.29, bf16[64,2048]{1,0:T(8,128)(2,1)} %copy-done.31, ...), custom_call_target="tpu_custom_call" | custom-call | flops 5905580032 | bytes 13565952 | tf_op jit(solution)/shard_map/pallas_call | solution.py:102
  145.3 6.3 %all-to-all-start = ((bf16[8,64,2048]{2,1,0:T(8,128)(2,1)}), bf16[8,64,2048]{2,1,0:T(8,128)(2,1)S(1)}, u32[]{:S(2)}, u32[]{:S(2)}) async-start(bf16[8,64,2048]{2,1,0:T(8,128)(2,1)} %bitcast.62), calls=%async_computation | async-start | bytes 4194304 | tf_op jit(solution)/shard_map/all_to_all | solution.py:719
  151.6 12.2 %shard_map.210 = (bf16[8,2112,128]{2,1,0:T(8,128)(2,1)}, bf16[8,2112,128]{2,1,0:T(8,128)(2,1)}) custom-call(s32[5]{0:T(128)S(1)} %stack.38.refs_0_, bf16[512,704]{1,0:T(8,128)(2,1)} %get-tuple-element.180.refs_1_, bf16[64,2048]{1,0:T(8,128)(2,1)} %get-tuple-element.177.refs_1_.refs_2_, bf16[64,2048]{1,0:T(8,128)(2,1)} %copy-done.29, ...), custom_call_target="tpu_custom_call" | custom-call | tf_op jit(solution)/shard_map/pallas_call | solution.py:102
  163.8 6.2 %all-to-all-done.refs_0_ = bf16[8,64,2048]{2,1,0:T(8,128)(2,1)S(1)} async-done(((bf16[8,64,2048]{2,1,0:T(8,128)(2,1)}), bf16[8,64,2048]{2,1,0:T(8,128)(2,1)S(1)}, u32[]{:S(2)}, u32[]{:S(2)}) %all-to-all-start) | async-done | bytes 2097184 | tf_op jit(solution)/shard_map/all_to_all | solution.py:719
  170.0 3.7 shard_map.212
  173.7 5.3 %all-to-all-start.1 = ((bf16[8,64,2048]{2,1,0:T(8,128)(2,1)}), bf16[8,64,2048]{2,1,0:T(8,128)(2,1)S(1)}, u32[]{:S(2)}, u32[]{:S(2)}) async-start(bf16[8,64,2048]{2,1,0:T(8,128)(2,1)} %get-tuple-element.193), calls=%async_computation.1 | async-start | bytes 4194304 | tf_op jit(solution)/shard_map/all_to_all | solution.py:719
  179.0 5.7 %shard_map.211 = (bf16[2,2112,128]{2,1,0:T(8,128)(2,1)}, bf16[2,2112,128]{2,1,0:T(8,128)(2,1)}, bf16[2,2112,128]{2,1,0:T(8,128)(2,1)}, bf16[2,2112,128]{2,1,0:T(8,128)(2,1)}) custom-call(s32[1]{0:T(128)} %bitcast.12.place, bf16[8,2112,128]{2,1,0:T(8,128)(2,1)} %get-tuple-element.185.mine, bf16[8,2112,128]{2,1,0:T(8,128)(2,1)} %collective-permute-done.23.received), custom_call_target="tpu_custom_call" | custom-call | tf_op jit(solution)/shard_map/pallas_call | solution.py:647
  187.5 3.1 convolution_convert_fusion
  190.7 14.5 %all-to-all-done.1 = bf16[8,64,2048]{2,1,0:T(8,128)(2,1)S(1)} async-done(((bf16[8,64,2048]{2,1,0:T(8,128)(2,1)}), bf16[8,64,2048]{2,1,0:T(8,128)(2,1)S(1)}, u32[]{:S(2)}, u32[]{:S(2)}) %all-to-all-start.1) | async-done | bytes 2097184 | tf_op jit(solution)/shard_map/all_to_all | solution.py:719
  205.1 3.5 shard_map.213
  211.2 3.6 collective-permute-done.25
  214.7 4.9 %all-to-all-start.2 = ((bf16[4,128,2048]{2,1,0:T(8,128)(2,1)}), bf16[4,128,2048]{2,1,0:T(8,128)(2,1)S(1)}, u32[]{:S(2)}, u32[]{:S(2)}) async-start(bf16[4,128,2048]{2,1,0:T(8,128)(2,1)} %bitcast.61), calls=%async_computation.2 | async-start | bytes 4194304 | tf_op jit(solution)/shard_map/all_to_all | solution.py:719
  221.3 4.8 %collective-permute-start.28 = (bf16[256,128]{1,0:T(8,128)(2,1)S(1)}, bf16[256,128]{1,0:T(8,128)(2,1)S(1)}, u32[]{:S(2)}, u32[]{:S(2)}) collective-permute-start(bf16[256,128]{1,0:T(8,128)(2,1)S(1)} %copy-done.50), channel_id=1, source_target_pairs={{0,96},{32,64},{64,32},{96,0},{1,97},{33,65},{65,33},{97,1},{2,98}... | collective-permute-start | bytes 196616 | tf_op jit(solution)/shard_map/ppermute | solution.py:612
  226.2 3.3 collective-permute-done.28.refs_10_
  232.3 20.1 %shard_map.214 = (f32[4,128,512]{2,1,0:T(8,128)}, bf16[4,512,128]{2,1,0:T(8,128)(2,1)}, bf16[4,512,128]{2,1,0:T(8,128)(2,1)}) custom-call(s32[5]{0:T(128)S(1)} %stack.38.refs_0_, bf16[4,512,128]{2,1,0:T(8,128)(2,1)} %copy-done.44, bf16[4,512,128]{2,1,0:T(8,128)(2,1)} %copy-done.45, bf16[768,128]{1,0:T(8,128)(2,1)} %get-tuple-element.155.refs_3_, ...), custom_call_target="tpu_custom_call" | custom-call | flops 6710886400 | bytes 4849664 | tf_op jit(solution)/shard_map/pallas_call | solution.py:102
  253.9 2.9 shard_map.215.refs_0_
  260.0 20.9 %shard_map.216 = (bf16[256,128]{1,0:T(8,128)(2,1)}, bf16[256,128]{1,0:T(8,128)(2,1)}, bf16[256,128]{1,0:T(8,128)(2,1)}, bf16[256,128]{1,0:T(8,128)(2,1)}, bf16[4...) custom-call(s32[5]{0:T(128)S(1)} %stack.38.refs_0_, bf16[4,512,128]{2,1,0:T(8,128)(2,1)} %copy-done.17, ...), custom_call_target="tpu_custom_call" | custom-call | flops 6710886400 | bytes 5111808 | tf_op jit(solution)/shard_map/pallas_call | solution.py:102
  290.9 4.9 %all-to-all-start.3 = ((bf16[4,128,2048]{2,1,0:T(8,128)(2,1)}), bf16[4,128,2048]{2,1,0:T(8,128)(2,1)S(1)}, u32[]{:S(2)}, u32[]{:S(2)}) async-start(bf16[4,128,2048]{2,1,0:T(8,128)(2,1)} %shard_map.218), calls=%async_computation.3 | async-start | bytes 4194304 | tf_op jit(solution)/shard_map/all_to_all | solution.py:719
  298.2 3.3 collective-permute-start.35
  304.3 3.0 collective-permute-done.35.refs_3_
  307.2 4.2 %collective-permute-done.36.refs_4_ = bf16[768,128]{1,0:T(8,128)(2,1)S(1)} collective-permute-done((bf16[768,128]{1,0:T(8,128)(2,1)S(1)}, bf16[768,128]{1,0:T(8,128)(2,1)S(1)}, u32[]{:S(2)}, u32[]{:S(2)}) %collective-permute-start.36) | collective-permute-done | bytes 196640 | tf_op jit(solution)/shard_map/ppermute | solution.py:612
  311.5 3.0 collective-permute-start.40
  314.5 7.0 %shard_map.219 = (bf16[512,768]{1,0:T(8,128)(2,1)}, bf16[512,2048]{1,0:T(8,128)(2,1)}, f32[1,2048]{1,0:T(1,128)S(1)}, f32[1,2048]{1,0:T(1,128)S(1)}, f32[3,256]{1,0:T(4,128)S(1)}) custom-call(s32[5]{0:T(128)S(1)} %stack.38.refs_0_, bf16[768,128]{1,0:T(8,128)(2,1)} %get-tuple-element.250.refs_1_, bf16[768,128]{1,0:T(8,128)(2,1)} %copy-done.36, ...), custom_call_target="tpu_custom_call" | custom-call | flops 1610612736 | bytes 9699328 | tf_op jit(solution)/shard_map/pallas_call | solution.py:102
  321.4 7.8 %shard_map.221 = (bf16[8,1024,128]{2,1,0:T(8,128)(2,1)}, bf16[8,1024,128]{2,1,0:T(8,128)(2,1)}) custom-call(s32[5]{0:T(128)S(1)} %stack.38.refs_0_, bf16[512,768]{1,0:T(8,128)(2,1)} %get-tuple-element.265.refs_1_, bf16[512,2048]{1,0:T(8,128)(2,1)} %get-tuple-element.266.refs_2_, bf16[512,256]{1,0:T(8,128)(2,1)} %get-tuple-element.267.refs_3_, ...), custom_call_target="tpu_custom_call" | custom-call | tf_op jit(solution)/shard_map/pallas_call | solution.py:102
  330.0 5.1 %all-to-all-start.4 = ((bf16[8,64,2048]{2,1,0:T(8,128)(2,1)}), bf16[8,64,2048]{2,1,0:T(8,128)(2,1)}, u32[]{:S(2)}, u32[]{:S(2)}) async-start(bf16[8,64,2048]{2,1,0:T(8,128)(2,1)} %bitcast.60), calls=%async_computation.4 | async-start | bytes 4194304 | tf_op jit(solution)/shard_map/all_to_all | solution.py:719
  337.6 3.0 collective-permute-done.38
  342.8 3.3 collective-permute-done.39
  346.1 3.4 shard_map.222
  356.3 4.5 %collective-permute-done.42 = f32[35,256]{1,0:T(8,128)S(1)} collective-permute-done((f32[35,256]{1,0:T(8,128)S(1)}, f32[35,256]{1,0:T(8,128)S(1)}, u32[]{:S(2)}, u32[]{:S(2)}) %collective-permute-start.42) | collective-permute-done | bytes 35872 | tf_op jit(solution)/shard_map/ppermute | solution.py:749
  362.2 3.3 shard_map.223.refs_1_
  367.7 5.0 %collective-permute-done.44 = bf16[2,1024,128]{2,1,0:T(8,128)(2,1)} collective-permute-done((bf16[2,1024,128]{2,1,0:T(8,128)(2,1)}, bf16[2,1024,128]{2,1,0:T(8,128)(2,1)}, u32[]{:S(2)}, u32[]{:S(2)}) %collective-permute-start.44) | collective-permute-done | bytes 524320 | tf_op jit(solution)/shard_map/ppermute | solution.py:706
  372.8 3.4 collective-permute-done.45
  383.2 4.1 %collective-permute-done.53 = bf16[1024,128]{1,0:T(8,128)(2,1)} collective-permute-done((bf16[1024,128]{1,0:T(8,128)(2,1)}, bf16[1024,128]{1,0:T(8,128)(2,1)}, u32[]{:S(2)}, u32[]{:S(2)}) %collective-permute-start.53) | collective-permute-done | bytes 262176 | tf_op jit(solution)/shard_map/ppermute | solution.py:607
  387.2 3.1 collective-permute-start.51
  399.0 3.6 shard_map.224
  (243 shorter events, 113.1 us)
Async XLA Ops:
  14.3 14.0 %collective-permute-start = (bf16[768,128]{1,0:T(8,128)(2,1)}, bf16[768,128]{1,0:T(8,128)(2,1)S(1)}, u32[]{:S(2)}, u32[]{:S(2)}) collective-permute-start(bf16[768,128]{1,0:T(8,128)(2,1)} %get-tuple-element.152), channel_id=1, source_target_pairs={{0,32},{32,0},{64,96},{96,64},{1,33},{33,1},{65,97},{97,65},{2,34}... | collective-permute-start | bytes 589832 | tf_op jit(solution)/shard_map/ppermute | solution.py:612
  14.9 13.4 %collective-permute-start.1 = (bf16[768,128]{1,0:T(8,128)(2,1)}, bf16[768,128]{1,0:T(8,128)(2,1)S(1)}, u32[]{:S(2)}, u32[]{:S(2)}) collective-permute-start(bf16[768,128]{1,0:T(8,128)(2,1)} %get-tuple-element.153), channel_id=1, source_target_pairs={{0,64},{32,96},{64,0},{96,32},{1,65},{33,97},{65,1},{97,33},{2,66}... | collective-permute-start | bytes 589832 | tf_op jit(solution)/shard_map/ppermute | solution.py:612
  18.0 11.7 %collective-permute-start.2 = (bf16[768,128]{1,0:T(8,128)(2,1)}, bf16[768,128]{1,0:T(8,128)(2,1)S(1)}, u32[]{:S(2)}, u32[]{:S(2)}) collective-permute-start(bf16[768,128]{1,0:T(8,128)(2,1)} %get-tuple-element.154), channel_id=1, source_target_pairs={{0,96},{32,64},{64,32},{96,0},{1,97},{33,65},{65,33},{97,1},{2,98}... | collective-permute-start | bytes 589832 | tf_op jit(solution)/shard_map/ppermute | solution.py:612
  29.9 15.4 %collective-permute-start.4 = (bf16[4,512,128]{2,1,0:T(8,128)(2,1)S(1)}, bf16[4,512,128]{2,1,0:T(8,128)(2,1)S(1)}, u32[]{:S(2)}, u32[]{:S(2)}) collective-permute-start(bf16[4,512,128]{2,1,0:T(8,128)(2,1)S(1)} %pad_maximum_fusion.refs_1_), channel_id=1, source_target_pairs={{0,16},{16,0},{1,17},{17,1},{2,18},{18,2},{3,19},{19,3},{4,20},{20... | collective-permute-start | bytes 1572872 | tf_op jit(solution)/shard_map/ppermute | solution.py:607
  62.4 6.6 %collective-permute-start.6 = (bf16[256,128]{1,0:T(8,128)(2,1)}, bf16[256,128]{1,0:T(8,128)(2,1)S(1)}, u32[]{:S(2)}, u32[]{:S(2)}) collective-permute-start(bf16[256,128]{1,0:T(8,128)(2,1)} %get-tuple-element.165), channel_id=1, source_target_pairs={{0,32},{32,0},{64,96},{96,64},{1,33},{33,1},{65,97},{97,65},{2,34}... | collective-permute-start | bytes 196616 | tf_op jit(solution)/shard_map/ppermute | solution.py:612
  66.1 8.4 %collective-permute-start.8 = (bf16[256,128]{1,0:T(8,128)(2,1)}, bf16[256,128]{1,0:T(8,128)(2,1)S(1)}, u32[]{:S(2)}, u32[]{:S(2)}) collective-permute-start(bf16[256,128]{1,0:T(8,128)(2,1)} %get-tuple-element.167), channel_id=1, source_target_pairs={{0,96},{32,64},{64,32},{96,0},{1,97},{33,65},{65,33},{97,1},{2,98}... | collective-permute-start | bytes 196616 | tf_op jit(solution)/shard_map/ppermute | solution.py:612
  79.1 9.5 %collective-permute-start.9 = (bf16[64,2048]{1,0:T(8,128)(2,1)}, bf16[64,2048]{1,0:T(8,128)(2,1)S(1)}, u32[]{:S(2)}, u32[]{:S(2)}) collective-permute-start(bf16[64,2048]{1,0:T(8,128)(2,1)} %get-tuple-element.169), channel_id=1, source_target_pairs={{0,1},{1,0},{2,3},{3,2},{4,5},{5,4},{6,7},{7,6},{8,9},{9,8},{10,11... | collective-permute-start | bytes 786440 | tf_op jit(solution)/shard_map/ppermute | solution.py:732
  79.8 21.1 %collective-permute-start.10 = (bf16[64,2048]{1,0:T(8,128)(2,1)}, bf16[64,2048]{1,0:T(8,128)(2,1)S(1)}, u32[]{:S(2)}, u32[]{:S(2)}) collective-permute-start(bf16[64,2048]{1,0:T(8,128)(2,1)} %get-tuple-element.170), channel_id=1, source_target_pairs={{0,2},{1,3},{2,0},{3,1},{4,6},{5,7},{6,4},{7,5},{8,10},{9,11},{10,... | collective-permute-start | bytes 786440 | tf_op jit(solution)/shard_map/ppermute | solution.py:732
  80.3 23.9 %collective-permute-start.11 = (bf16[64,2048]{1,0:T(8,128)(2,1)}, bf16[64,2048]{1,0:T(8,128)(2,1)S(1)}, u32[]{:S(2)}, u32[]{:S(2)}) collective-permute-start(bf16[64,2048]{1,0:T(8,128)(2,1)} %get-tuple-element.171), channel_id=1, source_target_pairs={{0,3},{1,2},{2,1},{3,0},{4,7},{5,6},{6,5},{7,4},{8,11},{9,10},{10,... | collective-permute-start | bytes 786440 | tf_op jit(solution)/shard_map/ppermute | solution.py:732
  82.7 23.1 %collective-permute-start.12 = (bf16[64,2048]{1,0:T(8,128)(2,1)}, bf16[64,2048]{1,0:T(8,128)(2,1)S(1)}, u32[]{:S(2)}, u32[]{:S(2)}) collective-permute-start(bf16[64,2048]{1,0:T(8,128)(2,1)} %get-tuple-element.172), channel_id=1, source_target_pairs={{0,4},{1,5},{2,6},{3,7},{4,0},{5,1},{6,2},{7,3},{8,12},{9,13},{10,... | collective-permute-start | bytes 786440 | tf_op jit(solution)/shard_map/ppermute | solution.py:732
  85.0 20.8 %collective-permute-start.13 = (bf16[64,2048]{1,0:T(8,128)(2,1)}, bf16[64,2048]{1,0:T(8,128)(2,1)S(1)}, u32[]{:S(2)}, u32[]{:S(2)}) collective-permute-start(bf16[64,2048]{1,0:T(8,128)(2,1)} %get-tuple-element.173), channel_id=1, source_target_pairs={{0,5},{1,4},{2,7},{3,6},{4,1},{5,0},{6,3},{7,2},{8,13},{9,12},{10,... | collective-permute-start | bytes 786440 | tf_op jit(solution)/shard_map/ppermute | solution.py:732
  88.7 21.0 %collective-permute-start.14 = (bf16[64,2048]{1,0:T(8,128)(2,1)}, bf16[64,2048]{1,0:T(8,128)(2,1)S(1)}, u32[]{:S(2)}, u32[]{:S(2)}) collective-permute-start(bf16[64,2048]{1,0:T(8,128)(2,1)} %get-tuple-element.174), channel_id=1, source_target_pairs={{0,6},{1,7},{2,4},{3,5},{4,2},{5,3},{6,0},{7,1},{8,14},{9,15},{10,... | collective-permute-start | bytes 786440 | tf_op jit(solution)/shard_map/ppermute | solution.py:732
  100.9 8.8 %collective-permute-start.15 = (bf16[64,2048]{1,0:T(8,128)(2,1)}, bf16[64,2048]{1,0:T(8,128)(2,1)S(1)}, u32[]{:S(2)}, u32[]{:S(2)}) collective-permute-start(bf16[64,2048]{1,0:T(8,128)(2,1)} %get-tuple-element.175), channel_id=1, source_target_pairs={{0,7},{1,6},{2,5},{3,4},{4,3},{5,2},{6,1},{7,0},{8,15},{9,14},{10,... | collective-permute-start | bytes 786440 | tf_op jit(solution)/shard_map/ppermute | solution.py:732
  114.4 8.6 %collective-permute-start.16 = (bf16[64,2048]{1,0:T(8,128)(2,1)}, bf16[64,2048]{1,0:T(8,128)(2,1)S(1)}, u32[]{:S(2)}, u32[]{:S(2)}) collective-permute-start(bf16[64,2048]{1,0:T(8,128)(2,1)} %get-tuple-element.177.refs_1_.refs_2_), channel_id=1, source_target_pairs={{0,1},{1,0},{2,3},{3,2},{4,5},{5,4},{6,7},{7,6},{8,9},{9,8},{10,11... | collective-permute-start | bytes 786440 | tf_op jit(solution)/shard_map/ppermute | solution.py:607
  115.5 9.6 %collective-permute-start.19 = (bf16[64,2048]{1,0:T(8,128)(2,1)}, bf16[64,2048]{1,0:T(8,128)(2,1)S(1)}, u32[]{:S(2)}, u32[]{:S(2)}) collective-permute-start(bf16[64,2048]{1,0:T(8,128)(2,1)} %get-tuple-element.177.refs_1_.refs_2_), channel_id=1, source_target_pairs={{0,4},{2,6},{4,0},{6,2},{1,5},{3,7},{5,1},{7,3},{8,12},{10,14},{12... | collective-permute-start | bytes 786440 | tf_op jit(solution)/shard_map/ppermute | solution.py:727
  118.4 8.7 %collective-permute-start.17 = (bf16[64,2048]{1,0:T(8,128)(2,1)}, bf16[64,2048]{1,0:T(8,128)(2,1)S(1)}, u32[]{:S(2)}, u32[]{:S(2)}) collective-permute-start(bf16[64,2048]{1,0:T(8,128)(2,1)} %get-tuple-element.177.refs_1_.refs_2_), channel_id=1, source_target_pairs={{0,2},{2,4},{4,6},{6,0},{1,3},{3,5},{5,7},{7,1},{8,10},{10,12},{12... | collective-permute-start | bytes 786440 | tf_op jit(solution)/shard_map/ppermute | solution.py:727
  118.9 8.5 %collective-permute-start.18 = (bf16[64,2048]{1,0:T(8,128)(2,1)}, bf16[64,2048]{1,0:T(8,128)(2,1)S(1)}, u32[]{:S(2)}, u32[]{:S(2)}) collective-permute-start(bf16[64,2048]{1,0:T(8,128)(2,1)} %get-tuple-element.177.refs_1_.refs_2_), channel_id=1, source_target_pairs={{0,6},{2,0},{4,2},{6,4},{1,7},{3,1},{5,3},{7,5},{8,14},{10,8},{12,... | collective-permute-start | bytes 786440 | tf_op jit(solution)/shard_map/ppermute | solution.py:727
  125.1 6.8 %collective-permute-start.22 = (bf16[64,2048]{1,0:T(8,128)(2,1)S(1)}, bf16[64,2048]{1,0:T(8,128)(2,1)S(1)}, u32[]{:S(2)}, u32[]{:S(2)}) collective-permute-start(bf16[64,2048]{1,0:T(8,128)(2,1)S(1)} %collective-permute-done.19.refs_5_.refs_6_), channel_id=1, source_target_pairs={{0,1},{1,0},{2,3},{3,2},{4,5},{5,4},{6,7},{7,6},{8,9},{9,8},{10,11... | collective-permute-start | bytes 786440 | tf_op jit(solution)/shard_map/ppermute | solution.py:607
  145.3 24.7 %all-to-all-start = ((bf16[8,64,2048]{2,1,0:T(8,128)(2,1)}), bf16[8,64,2048]{2,1,0:T(8,128)(2,1)S(1)}, u32[]{:S(2)}, u32[]{:S(2)}) async-start(bf16[8,64,2048]{2,1,0:T(8,128)(2,1)} %bitcast.62), calls=%async_computation | async-start | bytes 4194304 | tf_op jit(solution)/shard_map/all_to_all | solution.py:719
  170.0 9.0 %collective-permute-start.23 = (bf16[8,2112,128]{2,1,0:T(8,128)(2,1)}, bf16[8,2112,128]{2,1,0:T(8,128)(2,1)}, u32[]{:S(2)}, u32[]{:S(2)}) collective-permute-start(bf16[8,2112,128]{2,1,0:T(8,128)(2,1)} %get-tuple-element.186), channel_id=1, source_target_pairs={{0,8},{8,0},{1,9},{9,1},{2,10},{10,2},{3,11},{11,3},{4,12},{12,4},... | collective-permute-start | bytes 12976136 | tf_op jit(solution)/shard_map/ppermute | solution.py:607
  173.7 31.5 %all-to-all-start.1 = ((bf16[8,64,2048]{2,1,0:T(8,128)(2,1)}), bf16[8,64,2048]{2,1,0:T(8,128)(2,1)S(1)}, u32[]{:S(2)}, u32[]{:S(2)}) async-start(bf16[8,64,2048]{2,1,0:T(8,128)(2,1)} %get-tuple-element.193), calls=%async_computation.1 | async-start | bytes 4194304 | tf_op jit(solution)/shard_map/all_to_all | solution.py:719
  184.7 26.5 %collective-permute-start.24 = (bf16[2,2112,128]{2,1,0:T(8,128)(2,1)}, bf16[2,2112,128]{2,1,0:T(8,128)(2,1)S(1)}, u32[]{:S(2)}, u32[]{:S(2)}) collective-permute-start(bf16[2,2112,128]{2,1,0:T(8,128)(2,1)} %get-tuple-element.187), channel_id=1, source_target_pairs={{0,16},{16,32},{32,48},{48,0},{1,17},{17,33},{33,49},{49,1},{2,18}... | collective-permute-start | bytes 3244040 | tf_op jit(solution)/shard_map/ppermute | solution.py:706
  187.3 27.4 %collective-permute-start.25 = (bf16[2,2112,128]{2,1,0:T(8,128)(2,1)}, bf16[2,2112,128]{2,1,0:T(8,128)(2,1)}, u32[]{:S(2)}, u32[]{:S(2)}) collective-permute-start(bf16[2,2112,128]{2,1,0:T(8,128)(2,1)} %get-tuple-element.188), channel_id=1, source_target_pairs={{0,48},{16,0},{32,16},{48,32},{1,49},{17,1},{33,17},{49,33},{2,50}... | collective-permute-start | bytes 3244040 | tf_op jit(solution)/shard_map/ppermute | solution.py:706
  214.7 39.2 %all-to-all-start.2 = ((bf16[4,128,2048]{2,1,0:T(8,128)(2,1)}), bf16[4,128,2048]{2,1,0:T(8,128)(2,1)S(1)}, u32[]{:S(2)}, u32[]{:S(2)}) async-start(bf16[4,128,2048]{2,1,0:T(8,128)(2,1)} %bitcast.61), calls=%async_computation.2 | async-start | bytes 4194304 | tf_op jit(solution)/shard_map/all_to_all | solution.py:719
  219.7 6.5 %collective-permute-start.26 = (bf16[256,128]{1,0:T(8,128)(2,1)}, bf16[256,128]{1,0:T(8,128)(2,1)S(1)}, u32[]{:S(2)}, u32[]{:S(2)}) collective-permute-start(bf16[256,128]{1,0:T(8,128)(2,1)} %get-tuple-element.201), channel_id=1, source_target_pairs={{0,32},{32,0},{64,96},{96,64},{1,33},{33,1},{65,97},{97,65},{2,34}... | collective-permute-start | bytes 196616 | tf_op jit(solution)/shard_map/ppermute | solution.py:612
  221.3 8.2 %collective-permute-start.28 = (bf16[256,128]{1,0:T(8,128)(2,1)S(1)}, bf16[256,128]{1,0:T(8,128)(2,1)S(1)}, u32[]{:S(2)}, u32[]{:S(2)}) collective-permute-start(bf16[256,128]{1,0:T(8,128)(2,1)S(1)} %copy-done.50), channel_id=1, source_target_pairs={{0,96},{32,64},{64,32},{96,0},{1,97},{33,65},{65,33},{97,1},{2,98}... | collective-permute-start | bytes 196616 | tf_op jit(solution)/shard_map/ppermute | solution.py:612
  229.5 24.4 %collective-permute-start.29 = (bf16[2,2112,128]{2,1,0:T(8,128)(2,1)}, bf16[2,2112,128]{2,1,0:T(8,128)(2,1)}, u32[]{:S(2)}, u32[]{:S(2)}) collective-permute-start(bf16[2,2112,128]{2,1,0:T(8,128)(2,1)} %get-tuple-element.214), channel_id=1, source_target_pairs={{0,32},{16,48},{32,0},{48,16},{1,33},{17,49},{33,1},{49,17},{2,34}... | collective-permute-start | bytes 3244040 | tf_op jit(solution)/shard_map/ppermute | solution.py:706
  257.0 23.9 %collective-permute-start.31 = (bf16[4,512,128]{2,1,0:T(8,128)(2,1)S(1)}, bf16[4,512,128]{2,1,0:T(8,128)(2,1)S(1)}, u32[]{:S(2)}, u32[]{:S(2)}) collective-permute-start(bf16[4,512,128]{2,1,0:T(8,128)(2,1)S(1)} %add_convert_fusion.1), channel_id=1, source_target_pairs={{0,16},{16,0},{1,17},{17,1},{2,18},{18,2},{3,19},{19,3},{4,20},{20... | collective-permute-start | bytes 1572872 | tf_op jit(solution)/shard_map/ppermute | solution.py:607
  258.8 22.2 %collective-permute-start.32 = (bf16[128,2048]{1,0:T(8,128)(2,1)S(1)}, bf16[128,2048]{1,0:T(8,128)(2,1)S(1)}, u32[]{:S(2)}, u32[]{:S(2)}) collective-permute-start(bf16[128,2048]{1,0:T(8,128)(2,1)S(1)} %copy-done.8), channel_id=1, source_target_pairs={{0,1},{1,0},{2,3},{3,2},{4,5},{5,4},{6,7},{7,6},{8,9},{9,8},{10,11... | collective-permute-start | bytes 1572872 | tf_op jit(solution)/shard_map/ppermute | solution.py:607
  290.9 39.2 %all-to-all-start.3 = ((bf16[4,128,2048]{2,1,0:T(8,128)(2,1)}), bf16[4,128,2048]{2,1,0:T(8,128)(2,1)S(1)}, u32[]{:S(2)}, u32[]{:S(2)}) async-start(bf16[4,128,2048]{2,1,0:T(8,128)(2,1)} %shard_map.218), calls=%async_computation.3 | async-start | bytes 4194304 | tf_op jit(solution)/shard_map/all_to_all | solution.py:719
  295.8 8.5 %collective-permute-start.34 = (bf16[768,128]{1,0:T(8,128)(2,1)}, bf16[768,128]{1,0:T(8,128)(2,1)S(1)}, u32[]{:S(2)}, u32[]{:S(2)}) collective-permute-start(bf16[768,128]{1,0:T(8,128)(2,1)} %get-tuple-element.246), channel_id=1, source_target_pairs={{0,32},{32,0},{64,96},{96,64},{1,33},{33,1},{65,97},{97,65},{2,34}... | collective-permute-start | bytes 589832 | tf_op jit(solution)/shard_map/ppermute | solution.py:612
  298.2 9.0 %collective-permute-start.35 = (bf16[768,128]{1,0:T(8,128)(2,1)}, bf16[768,128]{1,0:T(8,128)(2,1)S(1)}, u32[]{:S(2)}, u32[]{:S(2)}) collective-permute-start(bf16[768,128]{1,0:T(8,128)(2,1)} %get-tuple-element.247), channel_id=1, source_target_pairs={{0,64},{32,96},{64,0},{96,32},{1,65},{33,97},{65,1},{97,33},{2,66}... | collective-permute-start | bytes 589832 | tf_op jit(solution)/shard_map/ppermute | solution.py:612
  301.6 9.9 %collective-permute-start.36 = (bf16[768,128]{1,0:T(8,128)(2,1)S(1)}, bf16[768,128]{1,0:T(8,128)(2,1)S(1)}, u32[]{:S(2)}, u32[]{:S(2)}) collective-permute-start(bf16[768,128]{1,0:T(8,128)(2,1)S(1)} %copy-done.46), channel_id=1, source_target_pairs={{0,96},{32,64},{64,32},{96,0},{1,97},{33,65},{65,33},{97,1},{2,98}... | collective-permute-start | bytes 589832 | tf_op jit(solution)/shard_map/ppermute | solution.py:612
  311.5 17.8 %collective-permute-start.40 = (bf16[2112,128]{1,0:T(8,128)(2,1)}, bf16[2112,128]{1,0:T(8,128)(2,1)S(1)}, u32[]{:S(2)}, u32[]{:S(2)}) collective-permute-start(bf16[2112,128]{1,0:T(8,128)(2,1)} %fusion), channel_id=1, source_target_pairs={{0,64},{64,0},{1,65},{65,1},{2,66},{66,2},{3,67},{67,3},{4,68},{68... | collective-permute-start | bytes 1622024 | tf_op jit(solution)/shard_map/ppermute | solution.py:607
  330.0 16.1 %collective-permute-start.41 = (bf16[8,1024,128]{2,1,0:T(8,128)(2,1)}, bf16[8,1024,128]{2,1,0:T(8,128)(2,1)}, u32[]{:S(2)}, u32[]{:S(2)}) collective-permute-start(bf16[8,1024,128]{2,1,0:T(8,128)(2,1)} %get-tuple-element.272), channel_id=1, source_target_pairs={{0,8},{8,0},{1,9},{9,1},{2,10},{10,2},{3,11},{11,3},{4,12},{12,4},... | collective-permute-start | bytes 6291464 | tf_op jit(solution)/shard_map/ppermute | solution.py:607
  330.0 31.5 %all-to-all-start.4 = ((bf16[8,64,2048]{2,1,0:T(8,128)(2,1)}), bf16[8,64,2048]{2,1,0:T(8,128)(2,1)}, u32[]{:S(2)}, u32[]{:S(2)}) async-start(bf16[8,64,2048]{2,1,0:T(8,128)(2,1)} %bitcast.60), calls=%async_computation.4 | async-start | bytes 4194304 | tf_op jit(solution)/shard_map/all_to_all | solution.py:719
  349.5 23.3 %collective-permute-start.44 = (bf16[2,1024,128]{2,1,0:T(8,128)(2,1)}, bf16[2,1024,128]{2,1,0:T(8,128)(2,1)}, u32[]{:S(2)}, u32[]{:S(2)}) collective-permute-start(bf16[2,1024,128]{2,1,0:T(8,128)(2,1)} %get-tuple-element.281), channel_id=1, source_target_pairs={{0,16},{16,32},{32,48},{48,0},{1,17},{17,33},{33,49},{49,1},{2,18}... | collective-permute-start | bytes 1572872 | tf_op jit(solution)/shard_map/ppermute | solution.py:706
  351.6 24.6 %collective-permute-start.45 = (bf16[2,1024,128]{2,1,0:T(8,128)(2,1)}, bf16[2,1024,128]{2,1,0:T(8,128)(2,1)}, u32[]{:S(2)}, u32[]{:S(2)}) collective-permute-start(bf16[2,1024,128]{2,1,0:T(8,128)(2,1)} %get-tuple-element.282), channel_id=1, source_target_pairs={{0,48},{16,0},{32,16},{48,32},{1,49},{17,1},{33,17},{49,33},{2,50}... | collective-permute-start | bytes 1572872 | tf_op jit(solution)/shard_map/ppermute | solution.py:706
  351.6 24.6 %collective-permute-start.52 = (bf16[2,1024,128]{2,1,0:T(8,128)(2,1)}, bf16[2,1024,128]{2,1,0:T(8,128)(2,1)}, u32[]{:S(2)}, u32[]{:S(2)}) collective-permute-start(bf16[2,1024,128]{2,1,0:T(8,128)(2,1)} %get-tuple-element.288), channel_id=1, source_target_pairs={{0,32},{16,48},{32,0},{48,16},{1,33},{17,49},{33,1},{49,17},{2,34}... | collective-permute-start | bytes 1572872 | tf_op jit(solution)/shard_map/ppermute | solution.py:706
  353.8 7.0 %collective-permute-start.42 = (f32[35,256]{1,0:T(8,128)S(1)}, f32[35,256]{1,0:T(8,128)S(1)}, u32[]{:S(2)}, u32[]{:S(2)}) collective-permute-start(f32[35,256]{1,0:T(8,128)S(1)} %add.157), channel_id=1, source_target_pairs={{0,64},{64,0},{1,65},{65,1},{2,66},{66,2},{3,67},{67,3},{4,68},{68... | collective-permute-start | bytes 107528 | tf_op jit(solution)/shard_map/ppermute | solution.py:749
  365.5 10.7 %collective-permute-start.43 = (bf16[64,2176]{1,0:T(8,128)(2,1)}, bf16[64,2176]{1,0:T(8,128)(2,1)S(1)}, u32[]{:S(2)}, u32[]{:S(2)}) collective-permute-start(bf16[64,2176]{1,0:T(8,128)(2,1)} %shard_map.223.refs_1_), channel_id=1, source_target_pairs={{0,1},{1,0},{2,3},{3,2},{4,5},{5,4},{6,7},{7,6},{8,9},{9,8},{10,11... | collective-permute-start | bytes 835592 | tf_op jit(solution)/shard_map/ppermute | solution.py:607
  366.3 16.6 %collective-permute-start.48 = (bf16[64,2176]{1,0:T(8,128)(2,1)}, bf16[64,2176]{1,0:T(8,128)(2,1)}, u32[]{:S(2)}, u32[]{:S(2)}) collective-permute-start(bf16[64,2176]{1,0:T(8,128)(2,1)} %shard_map.223.refs_1_), channel_id=1, source_target_pairs={{0,4},{2,6},{4,0},{6,2},{1,5},{3,7},{5,1},{7,3},{8,12},{10,14},{12... | collective-permute-start | bytes 835592 | tf_op jit(solution)/shard_map/ppermute | solution.py:727
  378.2 9.0 %collective-permute-start.53 = (bf16[1024,128]{1,0:T(8,128)(2,1)}, bf16[1024,128]{1,0:T(8,128)(2,1)}, u32[]{:S(2)}, u32[]{:S(2)}) collective-permute-start(bf16[1024,128]{1,0:T(8,128)(2,1)} %fusion.1), channel_id=1, source_target_pairs={{0,64},{64,0},{1,65},{65,1},{2,66},{66,2},{3,67},{67,3},{4,68},{68... | collective-permute-start | bytes 786440 | tf_op jit(solution)/shard_map/ppermute | solution.py:607
  379.1 19.8 %collective-permute-start.46 = (bf16[64,2176]{1,0:T(8,128)(2,1)}, bf16[64,2176]{1,0:T(8,128)(2,1)}, u32[]{:S(2)}, u32[]{:S(2)}) collective-permute-start(bf16[64,2176]{1,0:T(8,128)(2,1)} %shard_map.223.refs_1_), channel_id=1, source_target_pairs={{0,2},{2,4},{4,6},{6,0},{1,3},{3,5},{5,7},{7,1},{8,10},{10,12},{12... | collective-permute-start | bytes 835592 | tf_op jit(solution)/shard_map/ppermute | solution.py:727
  380.8 18.1 %collective-permute-start.47 = (bf16[64,2176]{1,0:T(8,128)(2,1)}, bf16[64,2176]{1,0:T(8,128)(2,1)}, u32[]{:S(2)}, u32[]{:S(2)}) collective-permute-start(bf16[64,2176]{1,0:T(8,128)(2,1)} %shard_map.223.refs_1_), channel_id=1, source_target_pairs={{0,6},{2,0},{4,2},{6,4},{1,7},{3,1},{5,3},{7,5},{8,14},{10,8},{12,... | collective-permute-start | bytes 835592 | tf_op jit(solution)/shard_map/ppermute | solution.py:727
  381.2 17.8 %collective-permute-start.49 = (bf16[64,2176]{1,0:T(8,128)(2,1)S(1)}, bf16[64,2176]{1,0:T(8,128)(2,1)}, u32[]{:S(2)}, u32[]{:S(2)}) collective-permute-start(bf16[64,2176]{1,0:T(8,128)(2,1)S(1)} %collective-permute-done.43.refs_2_), channel_id=1, source_target_pairs={{0,2},{2,4},{4,6},{6,0},{1,3},{3,5},{5,7},{7,1},{8,10},{10,12},{12... | collective-permute-start | bytes 835592 | tf_op jit(solution)/shard_map/ppermute | solution.py:727
  382.9 16.1 %collective-permute-start.50 = (bf16[64,2176]{1,0:T(8,128)(2,1)S(1)}, bf16[64,2176]{1,0:T(8,128)(2,1)}, u32[]{:S(2)}, u32[]{:S(2)}) collective-permute-start(bf16[64,2176]{1,0:T(8,128)(2,1)S(1)} %collective-permute-done.43.refs_2_), channel_id=1, source_target_pairs={{0,6},{2,0},{4,2},{6,4},{1,7},{3,1},{5,3},{7,5},{8,14},{10,8},{12,... | collective-permute-start | bytes 835592 | tf_op jit(solution)/shard_map/ppermute | solution.py:727
  387.2 11.7 %collective-permute-start.51 = (bf16[64,2176]{1,0:T(8,128)(2,1)}, bf16[64,2176]{1,0:T(8,128)(2,1)}, u32[]{:S(2)}, u32[]{:S(2)}) collective-permute-start(bf16[64,2176]{1,0:T(8,128)(2,1)} %collective-permute-done.48.refs_5_), channel_id=1, source_target_pairs={{0,1},{1,0},{2,3},{3,2},{4,5},{5,4},{6,7},{7,6},{8,9},{9,8},{10,11... | collective-permute-start | bytes 835592 | tf_op jit(solution)/shard_map/ppermute | solution.py:607
  (66 other events, 441.0 us)
where the time goes:
time: 412 us; the launch traced here: 404 us
  Pallas kernels  162 us (39%)
  starting transfers between devices  106 us (26%)
  waiting for transfers between devices  102 us (25%)
  local copies, waits for them, and re-layouts  17.7 us (4%)
  other arithmetic  10.5 us (3%)
    pallas_call x19, Pallas kernels, kernel_call(): pl.pallas_call(run, out_shape=(*[pltpu.HBM(a.shape, a.dtype) for a in out...  152 us
    all_to_all x5, starting transfers between devices, dealt(): return lax.all_to_all(x, axis, split_axis=0, concat_axis=0, tiled=True)  26.6 us
    ppermute x12, starting transfers between devices, across(): lax.ppermute(pieces[k], SPREAD, [(i, i ^ k) for i in range(4)])  26.1 us
    all_to_all x5, waiting for transfers between devices, dealt(): return lax.all_to_all(x, axis, split_axis=0, concat_axis=0, tiled=True)  21.4 us
    ppermute x12, waiting for transfers between devices, across(): lax.ppermute(pieces[k], SPREAD, [(i, i ^ k) for i in range(4)])  19.2 us
    ppermute x7, waiting for transfers between devices, scattered(): lax.ppermute(pieces[k], TP, [(i, i ^ k) for i in range(8)])  18.5 us
    ppermute x6, waiting for transfers between devices, z_permute(): return lax.ppermute(part, Z, [(i, (i + distance) % 4) for i in range(4)])  16 us
    ppermute x15, starting transfers between devices, swapped(): return lax.ppermute(x, axis, [(0, 1), (1, 0)])  14.9 us
  transfers between devices with their start and end apart: 59, of which 31 were waited for; matrix products, arithmetic and copies ran while one was open for 5% of the time, Pallas kernels for 28%

commit v1 on v0

--- a/solution.py
+++ b/solution.py
@@ -36,9 +36,26 @@
 
 
 def deal_rows(place, rows, outs):
-    tp = place[4] * 2 + place[3]
-    for k, out in enumerate(outs):
-        out[...] = rows[pl.ds(pl.multiple_of((tp ^ k) * 64, 64), 64), :]
+    x, y = place[3], place[4]
+    far = lax.rem(y + 2, 4)
+    firsts = [
+        lax.rem(y + 1, 4) * 2, lax.rem(y + 3, 4) * 2,
+        far * 2 + 1 - x, y * 2 + x, y * 2 + 1 - x, far * 2 + x,
+    ]
+    for first, out in zip(firsts, outs):
+        out[...] = rows[pl.ds(pl.multiple_of(first * 64, 64), out.shape[0]), :]
+
+
+def meet_kernel(place, below, above, crossed, other, far, out_other, out_far):
+    column = pl.multiple_of((1 - place[3]) * 64, 64)
+
+    def work(at):
+        there = pl.ds(pl.multiple_of(column + at.start, 16), at.size)
+        total = other[at, :].astype(WIDE) + below[there, :].astype(WIDE) + above[there, :].astype(WIDE)
+        out_other[at, :] = total.astype(LOW)
+        out_far[at, :] = (far[at, :].astype(WIDE) + crossed[at, :].astype(WIDE)).astype(LOW)
+
+    for_rows(work)
 
 
 def kernel_call(
@@ -364,7 +381,7 @@
 
 
 def branch_kernel(arrive, place, h0, h1, h2, h3, w, attended, *refs):
-    outs, (partial, kept) = refs[:8], refs[8:]
+    outs, (partial, kept) = refs[:6], refs[6:]
     for k, h in enumerate((h0, h1, h2, h3)):
         kept[place[1] ^ k] = h[...]
     for pair in range(2):
@@ -460,18 +477,22 @@
 
 
 def summed(parts, at):
-    one = [parts[k][at, :] for k in range(8)] if isinstance(parts, tuple) else [parts[k, at, :] for k in range(8)]
-    total = one[0].astype(WIDE)
-    for x in one[1:]:
-        total += x.astype(WIDE)
+    total = parts[0, at, :].astype(WIDE)
+    for k in range(1, 8):
+        total += parts[k, at, :].astype(WIDE)
     return total
 
 
-def second_norm_kernel(*refs):
-    parts, (tok, gain, shift, low, middle, normal, stats) = refs[:8], refs[8:]
+def second_norm_kernel(
+    place, below, above, own, other, far, tok, gain, shift, low, middle, normal, stats
+):
+    column = pl.multiple_of(place[3] * 64, 64)
 
     def work(at):
-        x = tok[at, :].astype(WIDE) + summed(parts, at)
+        there = pl.ds(pl.multiple_of(column + at.start, 16), at.size)
+        x = tok[at, :].astype(WIDE) + own[at, :].astype(WIDE)
+        x += below[there, :].astype(WIDE) + above[there, :].astype(WIDE)
+        x += other[at, :].astype(WIDE) + far[at, :].astype(WIDE)
         center = x - jnp.mean(x, axis=-1, keepdims=True)
         scale = lax.rsqrt(jnp.mean(center * center, axis=-1, keepdims=True) + 1e-05)
         rows = center * scale
@@ -550,12 +571,45 @@
     for_rows(work)
 
 
-def last_kernel(place, gathered, out, total):
-    out[...] = gathered[:, :2048]
-    done = gathered[:64, 2048:].astype(WIDE)
+def last_kernel(place, *refs):
+    shares, (out, total, held, came, went) = refs[:8], refs[8:]
+    moves = []
+    for k, (x, index) in enumerate(zip(shares, gathered_order(place))):
+        at = pl.ds(pl.multiple_of(index * 64, 64), 64)
+        moves.append(
+            (
+                pltpu.make_async_copy(x, held.at[k], came.at[k]),
+                pltpu.make_async_copy(held.at[k, :, pl.ds(0, 2048)], out.at[at], went.at[k]),
+            )
+        )
+    for come, _ in moves:
+        come.start()
+    for come, go in moves:
+        come.wait()
+        go.start()
+    done = held[0, :, 2048:].astype(WIDE)
     for k in range(1, 8):
-        done += gathered[k * 64 : k * 64 + 64, 2048:].astype(WIDE)
+        done += held[k, :, 2048:].astype(WIDE)
     total[...] = done
+    for _, go in moves:
+        go.wait()
+
+
+def last_call(shares, place):
+    hbm = pl.BlockSpec(memory_space=pltpu.HBM)
+    return pl.pallas_call(
+        last_kernel,
+        out_shape=(pltpu.HBM((BLOCK, 2048), LOW), shape_of(64, 128, kind=WIDE)),
+        in_specs=[pl.BlockSpec(memory_space=pltpu.SMEM), *[hbm] * 8],
+        out_specs=(hbm, pl.BlockSpec(memory_space=pltpu.VMEM)),
+        scratch_shapes=[
+            pltpu.VMEM((8, 64, 2048 + 128), LOW),
+            pltpu.SemaphoreType.DMA((8,)),
+            pltpu.SemaphoreType.DMA((8,)),
+        ],
+        compiler_params=pltpu.CompilerParams(vmem_limit_bytes=8 * 1024 * 1024),
+        cost_estimate=pl.CostEstimate(flops=0, bytes_accessed=0, transcendentals=0),
+    )(place, *[pltpu.with_memory_space_constraint(a, pltpu.HBM) for a in shares])
 
 
 def weight_kernel(widths, sources, arrive, place, *refs):
@@ -727,13 +781,6 @@
     return lax.ppermute(x, "y", [(i, (i + distance) % 4) for i in range(4)])
 
 
-def scattered(pieces):
-    moved = {
-        k: lax.ppermute(pieces[k], TP, [(i, i ^ k) for i in range(8)]) for k in (5, 4, 7, 3, 6, 2, 1)
-    }
-    return [pieces[0], *[moved[k] for k in range(1, 8)]]
-
-
 def gathered(share, *beside):
     across_x, *beside = lax.optimization_barrier((swapped(share, "xl"), *beside))
     back, ahead, far = (y_moved(share, k) for k in (1, 3, 2))
@@ -836,18 +883,28 @@
     share, low_share = shape_of(64, 2048, kind=WIDE), shape_of(64, 2048)
     attended_low, *partial_branch = kernel_call(
         branch_kernel,
-        (shape_of(BLOCK, 256), *[low_share] * 8),
+        (shape_of(BLOCK, 256), *[shape_of(128, 2048)] * 2, *[low_share] * 4),
         (*heads, w_out),
         scalars=(place,),
         scratch=(pltpu.VMEM((BLOCK, 2048), LOW), four),
         late=1,
         flops=2 * 512 * 256 * 2048,
     )
-    branch_parts = scattered(partial_branch)
+    to_above, to_below, to_other, own_part, other_part, far_part = partial_branch
+    from_below, from_above = y_moved(to_above, 1), y_moved(to_below, 3)
+    other_part, far_part = kernel_call(
+        meet_kernel,
+        (low_share, low_share),
+        (from_below, from_above, swapped(to_other, "xl"), other_part, far_part),
+        scalars=(place,),
+        quick=True,
+    )
+    other_part, far_part = swapped(other_part, "xl"), y_moved(far_part, 2)
     second_share, middle, second_rows, stats2 = kernel_call(
         second_norm_kernel,
         (low_share, share, share, shape_of(64, 128, kind=WIDE)),
-        (*branch_parts, tok_share),
+        (from_below, from_above, own_part, other_part, far_part, tok_share),
+        scalars=(place,),
         small=(second_gain[None], second_shift[None]),
     )
     second_low = gathered(second_share)
@@ -941,8 +998,10 @@
         (keep0, swapped(send0, "core"), far, *grad_queries),
     )
     (copies4,) = kernel_call(layer_out_kernel, (shape_of(4, 128, 2048),), (feed_half, feed_other))
-    feed_keep, feed_send = xh_halves([feed_z[0], feed_1, feed_2, feed_3])
-    *pieces, copies4, feed_send = tied((*pieces, copies4, feed_send))
+    *pieces, copies4, feed_0, feed_1, feed_2, feed_3 = tied(
+        (*pieces, copies4, feed_z[0], feed_1, feed_2, feed_3)
+    )
+    feed_keep, feed_send = xh_halves([feed_0, feed_1, feed_2, feed_3])
     *pieces, feed_send = tied((*across(pieces), feed_send))
     feed_received = swapped(feed_send, "xh")
     layer_out = dealt(copies4, "y")
@@ -985,14 +1044,7 @@
         small=(first_gain[None],),
     )
     last_shares, rest_1, rest_3 = gathered(last_share, rest_1, rest_3)
-    grad_tokens, vectors = kernel_call(
-        last_kernel,
-        (shape_of(BLOCK, 2048),),
-        (last_shares,),
-        scalars=(place,),
-        small_outs=(shape_of(64, 128, kind=WIDE),),
-        quick=True,
-    )
+    grad_tokens, vectors = last_call(last_shares, place)
     vectors = vectors.reshape(4, 2048)
     rest_z = (rest_z[0], rest_1, z_permute(rest_z[2], 2), rest_3)
     rest_keep, rest_send = xh_halves(rest_z)

time: 412 us -> 407 us (0.988)
  the two profiles are of different devices: /device:TPU:104 before, /device:TPU:0 now
where the time goes in v1:
time: 407 us; the launch traced here: 399 us
  Pallas kernels  166 us (41%)
  starting transfers between devices  101 us (25%)
  waiting for transfers between devices  99.2 us (24%)
  local copies, waits for them, and re-layouts  18.4 us (5%)
  other arithmetic  9.89 us (2%)
    pallas_call x19, Pallas kernels, kernel_call(): pl.pallas_call(run, out_shape=(*[pltpu.HBM(a.shape, a.dtype) for a in out...  153 us
    all_to_all x5, waiting for transfers between devices, dealt(): return lax.all_to_all(x, axis, split_axis=0, concat_axis=0, tiled=True)  27.8 us
    ppermute x12, starting transfers between devices, across(): lax.ppermute(pieces[k], SPREAD, [(i, i ^ k) for i in range(4)])  26.7 us
    ppermute x13, starting transfers between devices, y_moved(): return lax.ppermute(x, 'y', [(i, (i + distance) % 4) for i in range(4)])  24.4 us
    ppermute x12, waiting for transfers between devices, across(): lax.ppermute(pieces[k], SPREAD, [(i, i ^ k) for i in range(4)])  22.6 us
    all_to_all x5, starting transfers between devices, dealt(): return lax.all_to_all(x, axis, split_axis=0, concat_axis=0, tiled=True)  21.6 us
    ppermute x17, starting transfers between devices, swapped(): return lax.ppermute(x, axis, [(0, 1), (1, 0)])  13.9 us
    ppermute x17, waiting for transfers between devices, swapped(): return lax.ppermute(x, axis, [(0, 1), (1, 0)])  13.9 us
  transfers between devices with their start and end apart: 57, of which 31 were waited for; matrix products, arithmetic and copies ran while one was open for 5% of the time, Pallas kernels for 28%

profile of v1, /device:TPU:0, one launch (start us, length us, event | category | flops | bytes accessed | tf_op | source)
XLA Modules:
  0.0 399.4 jit_solution(17764524511461499860)
XLA Ops:
  5.6 8.7 %shard_map.203 = (bf16[512,2048]{1,0:T(8,128)(2,1)}, f32[512,128]{1,0:T(8,128)}, bf16[768,128]{1,0:T(8,128)(2,1)}, bf16[768,128]{1,0:T(8,128)(2,1)}, bf16[768,12...) custom-call(s32[5]{0:T(128)S(1)} %stack.38.refs_0_.place, ...), custom_call_target="tpu_custom_call" | custom-call | flops 1610612736 | bytes 8945664 | tf_op jit(solution)/shard_map/pallas_call | solution.py:119
  14.3 4.0 %collective-permute-start = (bf16[768,128]{1,0:T(8,128)(2,1)}, bf16[768,128]{1,0:T(8,128)(2,1)S(1)}, u32[]{:S(2)}, u32[]{:S(2)}) collective-permute-start(bf16[768,128]{1,0:T(8,128)(2,1)} %get-tuple-element.155), channel_id=1, source_target_pairs={{0,32},{32,0},{64,96},{96,64},{1,33},{33,1},{65,97},{97,65},{2,34}... | collective-permute-start | bytes 589832 | tf_op jit(solution)/shard_map/ppermute | solution.py:666
  18.3 3.0 collective-permute-start.1
  21.4 5.4 %shard_map.204.refs_11_ = f32[512,704]{1,0:T(8,128)} custom-call(bf16[512,2048]{1,0:T(8,128)(2,1)} %refs_12_.1, bf16[704,2048]{1,0:T(8,128)(2,1)} %refs_1_.3), custom_call_target="tpu_custom_call" | custom-call | flops 1476395008 | bytes 6422528 | tf_op jit(solution)/shard_map/pallas_call | solution.py:119
  34.5 13.0 %shard_map.205 = (f32[4,128,512]{2,1,0:T(8,128)}, f32[4,8,512]{2,1,0:T(8,128)}) custom-call(s32[5]{0:T(128)S(1)} %stack.38.refs_0_.place, bf16[4,512,128]{2,1,0:T(8,128)(2,1)} %copy-done.18, bf16[4,512,128]{2,1,0:T(8,128)(2,1)} %copy-done.40, bf16[768,128]{1,0:T(8,128)(2,1)} %get-tuple-element.158.refs_3_, bf16[768,128]{1,0:T(8,128)(2,1)} %copy-done.37, ...), custom_call_target="tpu_custom_call" | custom-call | flops 2684354560 | bytes 2490368 | tf_op jit(solution)/shard_map/pallas_call | solution.py:119
  50.6 14.4 %shard_map.206 = (bf16[256,128]{1,0:T(8,128)(2,1)}, bf16[256,128]{1,0:T(8,128)(2,1)}, bf16[256,128]{1,0:T(8,128)(2,1)}, bf16[256,128]{1,0:T(8,128)(2,1)}, f32[4,128,512]{2,1,0:T(8,128)}, /*index=5*/f32[4,8,512]{2,1,0:T(8,128)}) custom-call(s32[5]{0:T(128)S(1)} %stack.38.refs_0_.place, bf16[4,512,128]{2,1,0:T(8,128)(2,1)} %copy-done.41, ...), custom_call_target="tpu_custom_call" | custom-call | flops 2684354560 | bytes 3866624 | tf_op jit(solution)/shard_map/pallas_call | solution.py:119
  67.1 3.0 collective-permute-start.7
  73.0 5.4 %collective-permute-done.8.refs_4_ = bf16[256,128]{1,0:T(8,128)(2,1)S(1)} collective-permute-done((bf16[256,128]{1,0:T(8,128)(2,1)}, bf16[256,128]{1,0:T(8,128)(2,1)S(1)}, u32[]{:S(2)}, u32[]{:S(2)}) %collective-permute-start.8) | collective-permute-done | bytes 65568 | tf_op jit(solution)/shard_map/ppermute | solution.py:666
  79.1 4.2 %shard_map.207 = (bf16[512,256]{1,0:T(8,128)(2,1)}, bf16[128,2048]{1,0:T(8,128)(2,1)}, bf16[128,2048]{1,0:T(8,128)(2,1)}, bf16[64,2048]{1,0:T(8,128)(2,1)}, bf16...) custom-call(s32[5]{0:T(128)S(1)} %stack.38.refs_0_.place, ...), custom_call_target="tpu_custom_call" | custom-call | flops 536870912 | bytes 3670016 | tf_op jit(solution)/shard_map/pallas_call | solution.py:119
  87.2 6.0 %collective-permute-done.11.refs_3_ = bf16[64,2048]{1,0:T(8,128)(2,1)S(1)} collective-permute-done((bf16[64,2048]{1,0:T(8,128)(2,1)}, bf16[64,2048]{1,0:T(8,128)(2,1)S(1)}, u32[]{:S(2)}, u32[]{:S(2)}) %collective-permute-start.11) | collective-permute-done | bytes 262176 | tf_op jit(solution)/shard_map/ppermute | solution.py:661
  93.2 3.9 collective-permute-done.9.refs_1_
  98.1 3.0 shard_map.208
  101.8 2.8 collective-permute-start.13
  104.5 3.2 collective-permute-done.12.refs_4_
  110.6 4.2 %shard_map.209 = (bf16[64,2048]{1,0:T(8,128)(2,1)}, f32[64,2048]{1,0:T(8,128)}, f32[64,2048]{1,0:T(8,128)}, f32[64,128]{1,0:T(8,128)}) custom-call(s32[5]{0:T(128)S(1)} %stack.38.refs_0_.place, bf16[128,2048]{1,0:T(8,128)(2,1)} %copy-done.8, bf16[128,2048]{1,0:T(8,128)(2,1)} %copy-done.9, bf16[64,2048]{1,0:T(8,128)(2,1)} %get-tuple-element.173.refs_3_, ...), custom_call_target="tpu_custom_call" | custom-call | bytes 3440640 | tf_op jit(solution)/shard_map/pallas_call | solution.py:119
  116.3 2.8 collective-permute-start.17
  130.5 2.8 collective-permute-done.18.refs_6_.refs_7_
  134.7 12.7 %shard_map.210 = (bf16[512,704]{1,0:T(8,128)(2,1)}, bf16[512,704]{1,0:T(8,128)(2,1)}, bf16[512,704]{1,0:T(8,128)(2,1)}, bf16[512,2048]{1,0:T(8,128)(2,1)}) custom-call(s32[5]{0:T(128)S(1)} %stack.38.refs_0_.place, bf16[64,2048]{1,0:T(8,128)(2,1)} %get-tuple-element.180.refs_1_.refs_2_, bf16[64,2048]{1,0:T(8,128)(2,1)} %copy-done.26, ...), custom_call_target="tpu_custom_call" | custom-call | flops 5905580032 | bytes 13565952 | tf_op jit(solution)/shard_map/pallas_call | solution.py:119
  147.5 4.2 %all-to-all-start = ((bf16[8,64,2048]{2,1,0:T(8,128)(2,1)}), bf16[8,64,2048]{2,1,0:T(8,128)(2,1)S(1)}, u32[]{:S(2)}, u32[]{:S(2)}) async-start(bf16[8,64,2048]{2,1,0:T(8,128)(2,1)} %bitcast.62), calls=%async_computation | async-start | bytes 4194304 | tf_op jit(solution)/shard_map/all_to_all | solution.py:773
  151.7 12.2 %shard_map.211 = (bf16[8,2112,128]{2,1,0:T(8,128)(2,1)}, bf16[8,2112,128]{2,1,0:T(8,128)(2,1)}) custom-call(s32[5]{0:T(128)S(1)} %stack.38.refs_0_.place, bf16[512,704]{1,0:T(8,128)(2,1)} %get-tuple-element.183.refs_1_, bf16[64,2048]{1,0:T(8,128)(2,1)} %get-tuple-element.180.refs_1_.refs_2_, bf16[64,2048]{1,0:T(8,128)(2,1)} %copy-done.26, ...), custom_call_target="tpu_custom_call" | custom-call | tf_op jit(solution)/shard_map/pallas_call | solution.py:119
  163.9 11.2 %all-to-all-done.refs_0_ = bf16[8,64,2048]{2,1,0:T(8,128)(2,1)S(1)} async-done(((bf16[8,64,2048]{2,1,0:T(8,128)(2,1)}), bf16[8,64,2048]{2,1,0:T(8,128)(2,1)S(1)}, u32[]{:S(2)}, u32[]{:S(2)}) %all-to-all-start) | async-done | bytes 2097184 | tf_op jit(solution)/shard_map/all_to_all | solution.py:773
  175.1 3.7 shard_map.213
  178.8 3.6 all-to-all-start.1
  182.8 5.7 %shard_map.212 = (bf16[2,2112,128]{2,1,0:T(8,128)(2,1)}, bf16[2,2112,128]{2,1,0:T(8,128)(2,1)}, bf16[2,2112,128]{2,1,0:T(8,128)(2,1)}, bf16[2,2112,128]{2,1,0:T(8,128)(2,1)}) custom-call(s32[1]{0:T(128)} %bitcast.12.place, bf16[8,2112,128]{2,1,0:T(8,128)(2,1)} %get-tuple-element.188.mine, bf16[8,2112,128]{2,1,0:T(8,128)(2,1)} %collective-permute-done.21.received), custom_call_target="tpu_custom_call" | custom-call | tf_op jit(solution)/shard_map/pallas_call | solution.py:701
  192.0 3.1 convolution_convert_fusion
  195.1 15.2 %all-to-all-done.1 = bf16[8,64,2048]{2,1,0:T(8,128)(2,1)S(1)} async-done(((bf16[8,64,2048]{2,1,0:T(8,128)(2,1)}), bf16[8,64,2048]{2,1,0:T(8,128)(2,1)S(1)}, u32[]{:S(2)}, u32[]{:S(2)}) %all-to-all-start.1) | async-done | bytes 2097184 | tf_op jit(solution)/shard_map/all_to_all | solution.py:773
  210.3 3.5 shard_map.214
  216.9 4.4 %all-to-all-start.2 = ((bf16[4,128,2048]{2,1,0:T(8,128)(2,1)}), bf16[4,128,2048]{2,1,0:T(8,128)(2,1)S(1)}, u32[]{:S(2)}, u32[]{:S(2)}) async-start(bf16[4,128,2048]{2,1,0:T(8,128)(2,1)} %bitcast.61), calls=%async_computation.2 | async-start | bytes 4194304 | tf_op jit(solution)/shard_map/all_to_all | solution.py:773
  222.2 3.2 collective-permute-start.25
  228.0 5.6 %collective-permute-done.26.refs_10_ = bf16[256,128]{1,0:T(8,128)(2,1)S(1)} collective-permute-done((bf16[256,128]{1,0:T(8,128)(2,1)S(1)}, bf16[256,128]{1,0:T(8,128)(2,1)S(1)}, u32[]{:S(2)}, u32[]{:S(2)}) %collective-permute-start.26) | collective-permute-done | bytes 65568 | tf_op jit(solution)/shard_map/ppermute | solution.py:666
  235.1 20.4 %shard_map.215 = (f32[4,128,512]{2,1,0:T(8,128)}, bf16[4,512,128]{2,1,0:T(8,128)(2,1)}, bf16[4,512,128]{2,1,0:T(8,128)(2,1)}) custom-call(s32[5]{0:T(128)S(1)} %stack.38.refs_0_.place, bf16[4,512,128]{2,1,0:T(8,128)(2,1)} %copy-done.41, bf16[4,512,128]{2,1,0:T(8,128)(2,1)} %copy-done.42, bf16[768,128]{1,0:T(8,128)(2,1)} %get-tuple-element.158.refs_3_, ...), custom_call_target="tpu_custom_call" | custom-call | flops 6710886400 | bytes 4849664 | tf_op jit(solution)/shard_map/pallas_call | solution.py:119
  255.5 2.8 collective-permute-done.27
  258.3 2.9 shard_map.216.refs_0_
  263.8 21.2 %shard_map.217 = (bf16[256,128]{1,0:T(8,128)(2,1)}, bf16[256,128]{1,0:T(8,128)(2,1)}, bf16[256,128]{1,0:T(8,128)(2,1)}, bf16[256,128]{1,0:T(8,128)(2,1)}, bf16[4...) custom-call(s32[5]{0:T(128)S(1)} %stack.38.refs_0_.place, bf16[4,512,128]{2,1,0:T(8,128)(2,1)} %copy-done.18, ...), custom_call_target="tpu_custom_call" | custom-call | flops 6710886400 | bytes 5111808 | tf_op jit(solution)/shard_map/pallas_call | solution.py:119
  291.9 4.8 %all-to-all-start.3 = ((bf16[4,128,2048]{2,1,0:T(8,128)(2,1)}), bf16[4,128,2048]{2,1,0:T(8,128)(2,1)S(1)}, u32[]{:S(2)}, u32[]{:S(2)}) async-start(bf16[4,128,2048]{2,1,0:T(8,128)(2,1)} %shard_map.219), calls=%async_computation.3 | async-start | bytes 4194304 | tf_op jit(solution)/shard_map/all_to_all | solution.py:773
  297.8 3.1 collective-permute-start.33
  306.6 5.5 %collective-permute-done.34.refs_4_ = bf16[768,128]{1,0:T(8,128)(2,1)S(1)} collective-permute-done((bf16[768,128]{1,0:T(8,128)(2,1)S(1)}, bf16[768,128]{1,0:T(8,128)(2,1)S(1)}, u32[]{:S(2)}, u32[]{:S(2)}) %collective-permute-start.34) | collective-permute-done | bytes 196640 | tf_op jit(solution)/shard_map/ppermute | solution.py:666
  314.2 7.0 %shard_map.220 = (bf16[512,768]{1,0:T(8,128)(2,1)}, bf16[512,2048]{1,0:T(8,128)(2,1)}, f32[1,2048]{1,0:T(1,128)S(1)}, f32[1,2048]{1,0:T(1,128)S(1)}, f32[3,256]{1,0:T(4,128)S(1)}) custom-call(s32[5]{0:T(128)S(1)} %stack.38.refs_0_.place, bf16[768,128]{1,0:T(8,128)(2,1)} %get-tuple-element.256.refs_1_, bf16[768,128]{1,0:T(8,128)(2,1)} %copy-done.33, ...), custom_call_target="tpu_custom_call" | custom-call | flops 1610612736 | bytes 9699328 | tf_op jit(solution)/shard_map/pallas_call | solution.py:119
  321.2 7.8 %shard_map.222 = (bf16[8,1024,128]{2,1,0:T(8,128)(2,1)}, bf16[8,1024,128]{2,1,0:T(8,128)(2,1)}) custom-call(s32[5]{0:T(128)S(1)} %stack.38.refs_0_.place, bf16[512,768]{1,0:T(8,128)(2,1)} %get-tuple-element.271.refs_1_, bf16[512,2048]{1,0:T(8,128)(2,1)} %get-tuple-element.272.refs_2_, bf16[512,256]{1,0:T(8,128)(2,1)} %get-tuple-element.273.refs_3_, ...), custom_call_target="tpu_custom_call" | custom-call | tf_op jit(solution)/shard_map/pallas_call | solution.py:119
  329.8 4.6 %all-to-all-start.4 = ((bf16[8,64,2048]{2,1,0:T(8,128)(2,1)}), bf16[8,64,2048]{2,1,0:T(8,128)(2,1)}, u32[]{:S(2)}, u32[]{:S(2)}) async-start(bf16[8,64,2048]{2,1,0:T(8,128)(2,1)} %bitcast.60), calls=%async_computation.4 | async-start | bytes 4194304 | tf_op jit(solution)/shard_map/all_to_all | solution.py:773
  337.0 2.9 collective-permute-done.36
  342.0 3.5 collective-permute-done.37
  345.5 3.4 shard_map.223
  355.7 5.6 %collective-permute-done.40 = f32[35,256]{1,0:T(8,128)S(1)} collective-permute-done((f32[35,256]{1,0:T(8,128)S(1)}, f32[35,256]{1,0:T(8,128)S(1)}, u32[]{:S(2)}, u32[]{:S(2)}) %collective-permute-start.40) | collective-permute-done | bytes 35872 | tf_op jit(solution)/shard_map/ppermute | solution.py:796
  363.4 3.3 shard_map.224.refs_0_
  369.8 4.1 %collective-permute-done.42 = bf16[2,1024,128]{2,1,0:T(8,128)(2,1)} collective-permute-done((bf16[2,1024,128]{2,1,0:T(8,128)(2,1)}, bf16[2,1024,128]{2,1,0:T(8,128)(2,1)}, u32[]{:S(2)}, u32[]{:S(2)}) %collective-permute-start.42) | collective-permute-done | bytes 524320 | tf_op jit(solution)/shard_map/ppermute | solution.py:760
  382.1 3.2 collective-permute-start.48
  395.4 2.9 shard_map.225
  (236 shorter events, 110.2 us)
Async XLA Ops:
  14.3 14.5 %collective-permute-start = (bf16[768,128]{1,0:T(8,128)(2,1)}, bf16[768,128]{1,0:T(8,128)(2,1)S(1)}, u32[]{:S(2)}, u32[]{:S(2)}) collective-permute-start(bf16[768,128]{1,0:T(8,128)(2,1)} %get-tuple-element.155), channel_id=1, source_target_pairs={{0,32},{32,0},{64,96},{96,64},{1,33},{33,1},{65,97},{97,65},{2,34}... | collective-permute-start | bytes 589832 | tf_op jit(solution)/shard_map/ppermute | solution.py:666
  18.3 10.5 %collective-permute-start.1 = (bf16[768,128]{1,0:T(8,128)(2,1)}, bf16[768,128]{1,0:T(8,128)(2,1)S(1)}, u32[]{:S(2)}, u32[]{:S(2)}) collective-permute-start(bf16[768,128]{1,0:T(8,128)(2,1)} %get-tuple-element.156), channel_id=1, source_target_pairs={{0,64},{32,96},{64,0},{96,32},{1,65},{33,97},{65,1},{97,33},{2,66}... | collective-permute-start | bytes 589832 | tf_op jit(solution)/shard_map/ppermute | solution.py:666
  21.4 10.2 %collective-permute-start.2 = (bf16[768,128]{1,0:T(8,128)(2,1)}, bf16[768,128]{1,0:T(8,128)(2,1)S(1)}, u32[]{:S(2)}, u32[]{:S(2)}) collective-permute-start(bf16[768,128]{1,0:T(8,128)(2,1)} %get-tuple-element.157), channel_id=1, source_target_pairs={{0,96},{32,64},{64,32},{96,0},{1,97},{33,65},{65,33},{97,1},{2,98}... | collective-permute-start | bytes 589832 | tf_op jit(solution)/shard_map/ppermute | solution.py:666
  31.8 15.7 %collective-permute-start.4 = (bf16[4,512,128]{2,1,0:T(8,128)(2,1)S(1)}, bf16[4,512,128]{2,1,0:T(8,128)(2,1)S(1)}, u32[]{:S(2)}, u32[]{:S(2)}) collective-permute-start(bf16[4,512,128]{2,1,0:T(8,128)(2,1)S(1)} %pad_maximum_fusion.refs_1_), channel_id=1, source_target_pairs={{0,16},{16,0},{1,17},{17,1},{2,18},{18,2},{3,19},{19,3},{4,20},{20... | collective-permute-start | bytes 1572872 | tf_op jit(solution)/shard_map/ppermute | solution.py:661
  65.0 6.6 %collective-permute-start.6 = (bf16[256,128]{1,0:T(8,128)(2,1)}, bf16[256,128]{1,0:T(8,128)(2,1)S(1)}, u32[]{:S(2)}, u32[]{:S(2)}) collective-permute-start(bf16[256,128]{1,0:T(8,128)(2,1)} %get-tuple-element.168), channel_id=1, source_target_pairs={{0,32},{32,0},{64,96},{96,64},{1,33},{33,1},{65,97},{97,65},{2,34}... | collective-permute-start | bytes 196616 | tf_op jit(solution)/shard_map/ppermute | solution.py:666
  70.1 8.4 %collective-permute-start.8 = (bf16[256,128]{1,0:T(8,128)(2,1)}, bf16[256,128]{1,0:T(8,128)(2,1)S(1)}, u32[]{:S(2)}, u32[]{:S(2)}) collective-permute-start(bf16[256,128]{1,0:T(8,128)(2,1)} %get-tuple-element.170), channel_id=1, source_target_pairs={{0,96},{32,64},{64,32},{96,0},{1,97},{33,65},{65,33},{97,1},{2,98}... | collective-permute-start | bytes 196616 | tf_op jit(solution)/shard_map/ppermute | solution.py:666
  83.3 13.8 %collective-permute-start.9 = (bf16[128,2048]{1,0:T(8,128)(2,1)}, bf16[128,2048]{1,0:T(8,128)(2,1)S(1)}, u32[]{:S(2)}, u32[]{:S(2)}) collective-permute-start(bf16[128,2048]{1,0:T(8,128)(2,1)} %get-tuple-element.171), channel_id=1, source_target_pairs={{0,2},{2,4},{4,6},{6,0},{1,3},{3,5},{5,7},{7,1},{8,10},{10,12},{12... | collective-permute-start | bytes 1572872 | tf_op jit(solution)/shard_map/ppermute | solution.py:781
  85.0 12.2 %collective-permute-start.10 = (bf16[128,2048]{1,0:T(8,128)(2,1)}, bf16[128,2048]{1,0:T(8,128)(2,1)S(1)}, u32[]{:S(2)}, u32[]{:S(2)}) collective-permute-start(bf16[128,2048]{1,0:T(8,128)(2,1)} %get-tuple-element.172), channel_id=1, source_target_pairs={{0,6},{2,0},{4,2},{6,4},{1,7},{3,1},{5,3},{7,5},{8,14},{10,8},{12,... | collective-permute-start | bytes 1572872 | tf_op jit(solution)/shard_map/ppermute | solution.py:781
  86.6 6.6 %collective-permute-start.11 = (bf16[64,2048]{1,0:T(8,128)(2,1)}, bf16[64,2048]{1,0:T(8,128)(2,1)S(1)}, u32[]{:S(2)}, u32[]{:S(2)}) collective-permute-start(bf16[64,2048]{1,0:T(8,128)(2,1)} %get-tuple-element.174), channel_id=1, source_target_pairs={{0,1},{1,0},{2,3},{3,2},{4,5},{5,4},{6,7},{7,6},{8,9},{9,8},{10,11... | collective-permute-start | bytes 786440 | tf_op jit(solution)/shard_map/ppermute | solution.py:661
  101.1 6.7 %collective-permute-start.12 = (bf16[64,2048]{1,0:T(8,128)(2,1)}, bf16[64,2048]{1,0:T(8,128)(2,1)S(1)}, u32[]{:S(2)}, u32[]{:S(2)}) collective-permute-start(bf16[64,2048]{1,0:T(8,128)(2,1)} %get-tuple-element.177), channel_id=1, source_target_pairs={{0,1},{1,0},{2,3},{3,2},{4,5},{5,4},{6,7},{7,6},{8,9},{9,8},{10,11... | collective-permute-start | bytes 786440 | tf_op jit(solution)/shard_map/ppermute | solution.py:661
  101.8 8.1 %collective-permute-start.13 = (bf16[64,2048]{1,0:T(8,128)(2,1)}, bf16[64,2048]{1,0:T(8,128)(2,1)S(1)}, u32[]{:S(2)}, u32[]{:S(2)}) collective-permute-start(bf16[64,2048]{1,0:T(8,128)(2,1)} %get-tuple-element.178), channel_id=1, source_target_pairs={{0,4},{2,6},{4,0},{6,2},{1,5},{3,7},{5,1},{7,3},{8,12},{10,14},{12... | collective-permute-start | bytes 786440 | tf_op jit(solution)/shard_map/ppermute | solution.py:781
  114.8 7.5 %collective-permute-start.14 = (bf16[64,2048]{1,0:T(8,128)(2,1)}, bf16[64,2048]{1,0:T(8,128)(2,1)S(1)}, u32[]{:S(2)}, u32[]{:S(2)}) collective-permute-start(bf16[64,2048]{1,0:T(8,128)(2,1)} %get-tuple-element.180.refs_1_.refs_2_), channel_id=1, source_target_pairs={{0,1},{1,0},{2,3},{3,2},{4,5},{5,4},{6,7},{7,6},{8,9},{9,8},{10,11... | collective-permute-start | bytes 786440 | tf_op jit(solution)/shard_map/ppermute | solution.py:661
  116.3 11.0 %collective-permute-start.17 = (bf16[64,2048]{1,0:T(8,128)(2,1)}, bf16[64,2048]{1,0:T(8,128)(2,1)S(1)}, u32[]{:S(2)}, u32[]{:S(2)}) collective-permute-start(bf16[64,2048]{1,0:T(8,128)(2,1)} %get-tuple-element.180.refs_1_.refs_2_), channel_id=1, source_target_pairs={{0,4},{2,6},{4,0},{6,2},{1,5},{3,7},{5,1},{7,3},{8,12},{10,14},{12... | collective-permute-start | bytes 786440 | tf_op jit(solution)/shard_map/ppermute | solution.py:781
  119.1 11.4 %collective-permute-start.15 = (bf16[64,2048]{1,0:T(8,128)(2,1)}, bf16[64,2048]{1,0:T(8,128)(2,1)S(1)}, u32[]{:S(2)}, u32[]{:S(2)}) collective-permute-start(bf16[64,2048]{1,0:T(8,128)(2,1)} %get-tuple-element.180.refs_1_.refs_2_), channel_id=1, source_target_pairs={{0,2},{2,4},{4,6},{6,0},{1,3},{3,5},{5,7},{7,1},{8,10},{10,12},{12... | collective-permute-start | bytes 786440 | tf_op jit(solution)/shard_map/ppermute | solution.py:781
  120.0 10.5 %collective-permute-start.16 = (bf16[64,2048]{1,0:T(8,128)(2,1)}, bf16[64,2048]{1,0:T(8,128)(2,1)S(1)}, u32[]{:S(2)}, u32[]{:S(2)}) collective-permute-start(bf16[64,2048]{1,0:T(8,128)(2,1)} %get-tuple-element.180.refs_1_.refs_2_), channel_id=1, source_target_pairs={{0,6},{2,0},{4,2},{6,4},{1,7},{3,1},{5,3},{7,5},{8,14},{10,8},{12,... | collective-permute-start | bytes 786440 | tf_op jit(solution)/shard_map/ppermute | solution.py:781
  122.3 11.0 %collective-permute-start.18 = (bf16[64,2048]{1,0:T(8,128)(2,1)S(1)}, bf16[64,2048]{1,0:T(8,128)(2,1)S(1)}, u32[]{:S(2)}, u32[]{:S(2)}) collective-permute-start(bf16[64,2048]{1,0:T(8,128)(2,1)S(1)} %collective-permute-done.14.refs_2_.refs_3_), channel_id=1, source_target_pairs={{0,2},{2,4},{4,6},{6,0},{1,3},{3,5},{5,7},{7,1},{8,10},{10,12},{12... | collective-permute-start | bytes 786440 | tf_op jit(solution)/shard_map/ppermute | solution.py:781
  122.9 10.4 %collective-permute-start.19 = (bf16[64,2048]{1,0:T(8,128)(2,1)S(1)}, bf16[64,2048]{1,0:T(8,128)(2,1)S(1)}, u32[]{:S(2)}, u32[]{:S(2)}) collective-permute-start(bf16[64,2048]{1,0:T(8,128)(2,1)S(1)} %collective-permute-done.14.refs_2_.refs_3_), channel_id=1, source_target_pairs={{0,6},{2,0},{4,2},{6,4},{1,7},{3,1},{5,3},{7,5},{8,14},{10,8},{12,... | collective-permute-start | bytes 786440 | tf_op jit(solution)/shard_map/ppermute | solution.py:781
  127.3 6.8 %collective-permute-start.20 = (bf16[64,2048]{1,0:T(8,128)(2,1)S(1)}, bf16[64,2048]{1,0:T(8,128)(2,1)S(1)}, u32[]{:S(2)}, u32[]{:S(2)}) collective-permute-start(bf16[64,2048]{1,0:T(8,128)(2,1)S(1)} %collective-permute-done.17.refs_5_.refs_6_), channel_id=1, source_target_pairs={{0,1},{1,0},{2,3},{3,2},{4,5},{5,4},{6,7},{7,6},{8,9},{9,8},{10,11... | collective-permute-start | bytes 786440 | tf_op jit(solution)/shard_map/ppermute | solution.py:661
  147.5 27.6 %all-to-all-start = ((bf16[8,64,2048]{2,1,0:T(8,128)(2,1)}), bf16[8,64,2048]{2,1,0:T(8,128)(2,1)S(1)}, u32[]{:S(2)}, u32[]{:S(2)}) async-start(bf16[8,64,2048]{2,1,0:T(8,128)(2,1)} %bitcast.62), calls=%async_computation | async-start | bytes 4194304 | tf_op jit(solution)/shard_map/all_to_all | solution.py:773
  175.1 7.7 %collective-permute-start.21 = (bf16[8,2112,128]{2,1,0:T(8,128)(2,1)}, bf16[8,2112,128]{2,1,0:T(8,128)(2,1)}, u32[]{:S(2)}, u32[]{:S(2)}) collective-permute-start(bf16[8,2112,128]{2,1,0:T(8,128)(2,1)} %get-tuple-element.189), channel_id=1, source_target_pairs={{0,8},{8,0},{1,9},{9,1},{2,10},{10,2},{3,11},{11,3},{4,12},{12,4},... | collective-permute-start | bytes 12976136 | tf_op jit(solution)/shard_map/ppermute | solution.py:661
  178.8 31.5 %all-to-all-start.1 = ((bf16[8,64,2048]{2,1,0:T(8,128)(2,1)}), bf16[8,64,2048]{2,1,0:T(8,128)(2,1)S(1)}, u32[]{:S(2)}, u32[]{:S(2)}) async-start(bf16[8,64,2048]{2,1,0:T(8,128)(2,1)} %get-tuple-element.196), calls=%async_computation.1 | async-start | bytes 4194304 | tf_op jit(solution)/shard_map/all_to_all | solution.py:773
  188.5 27.4 %collective-permute-start.22 = (bf16[2,2112,128]{2,1,0:T(8,128)(2,1)}, bf16[2,2112,128]{2,1,0:T(8,128)(2,1)S(1)}, u32[]{:S(2)}, u32[]{:S(2)}) collective-permute-start(bf16[2,2112,128]{2,1,0:T(8,128)(2,1)} %get-tuple-element.190), channel_id=1, source_target_pairs={{0,16},{16,32},{32,48},{48,0},{1,17},{17,33},{33,49},{49,1},{2,18}... | collective-permute-start | bytes 3244040 | tf_op jit(solution)/shard_map/ppermute | solution.py:760
  189.6 26.4 %collective-permute-start.23 = (bf16[2,2112,128]{2,1,0:T(8,128)(2,1)}, bf16[2,2112,128]{2,1,0:T(8,128)(2,1)}, u32[]{:S(2)}, u32[]{:S(2)}) collective-permute-start(bf16[2,2112,128]{2,1,0:T(8,128)(2,1)} %get-tuple-element.191), channel_id=1, source_target_pairs={{0,48},{16,0},{32,16},{48,32},{1,49},{17,1},{33,17},{49,33},{2,50}... | collective-permute-start | bytes 3244040 | tf_op jit(solution)/shard_map/ppermute | solution.py:760
  216.9 41.4 %all-to-all-start.2 = ((bf16[4,128,2048]{2,1,0:T(8,128)(2,1)}), bf16[4,128,2048]{2,1,0:T(8,128)(2,1)S(1)}, u32[]{:S(2)}, u32[]{:S(2)}) async-start(bf16[4,128,2048]{2,1,0:T(8,128)(2,1)} %bitcast.61), calls=%async_computation.2 | async-start | bytes 4194304 | tf_op jit(solution)/shard_map/all_to_all | solution.py:773
  221.3 6.5 %collective-permute-start.24 = (bf16[256,128]{1,0:T(8,128)(2,1)S(1)}, bf16[256,128]{1,0:T(8,128)(2,1)S(1)}, u32[]{:S(2)}, u32[]{:S(2)}) collective-permute-start(bf16[256,128]{1,0:T(8,128)(2,1)S(1)} %copy-done.50), channel_id=1, source_target_pairs={{0,32},{32,0},{64,96},{96,64},{1,33},{33,1},{65,97},{97,65},{2,34}... | collective-permute-start | bytes 196616 | tf_op jit(solution)/shard_map/ppermute | solution.py:666
  225.4 8.2 %collective-permute-start.26 = (bf16[256,128]{1,0:T(8,128)(2,1)S(1)}, bf16[256,128]{1,0:T(8,128)(2,1)S(1)}, u32[]{:S(2)}, u32[]{:S(2)}) collective-permute-start(bf16[256,128]{1,0:T(8,128)(2,1)S(1)} %copy-done.47), channel_id=1, source_target_pairs={{0,96},{32,64},{64,32},{96,0},{1,97},{33,65},{65,33},{97,1},{2,98}... | collective-permute-start | bytes 196616 | tf_op jit(solution)/shard_map/ppermute | solution.py:666
  233.6 24.7 %collective-permute-start.27 = (bf16[2,2112,128]{2,1,0:T(8,128)(2,1)}, bf16[2,2112,128]{2,1,0:T(8,128)(2,1)}, u32[]{:S(2)}, u32[]{:S(2)}) collective-permute-start(bf16[2,2112,128]{2,1,0:T(8,128)(2,1)} %get-tuple-element.217), channel_id=1, source_target_pairs={{0,32},{16,48},{32,0},{48,16},{1,33},{17,49},{33,1},{49,17},{2,34}... | collective-permute-start | bytes 3244040 | tf_op jit(solution)/shard_map/ppermute | solution.py:760
  261.4 23.6 %collective-permute-start.29 = (bf16[4,512,128]{2,1,0:T(8,128)(2,1)S(1)}, bf16[4,512,128]{2,1,0:T(8,128)(2,1)S(1)}, u32[]{:S(2)}, u32[]{:S(2)}) collective-permute-start(bf16[4,512,128]{2,1,0:T(8,128)(2,1)S(1)} %add_convert_fusion.1), channel_id=1, source_target_pairs={{0,16},{16,0},{1,17},{17,1},{2,18},{18,2},{3,19},{19,3},{4,20},{20... | collective-permute-start | bytes 1572872 | tf_op jit(solution)/shard_map/ppermute | solution.py:661
  262.6 22.4 %collective-permute-start.30 = (bf16[128,2048]{1,0:T(8,128)(2,1)S(1)}, bf16[128,2048]{1,0:T(8,128)(2,1)S(1)}, u32[]{:S(2)}, u32[]{:S(2)}) collective-permute-start(bf16[128,2048]{1,0:T(8,128)(2,1)S(1)} %copy-done.10), channel_id=1, source_target_pairs={{0,1},{1,0},{2,3},{3,2},{4,5},{5,4},{6,7},{7,6},{8,9},{9,8},{10,11... | collective-permute-start | bytes 1572872 | tf_op jit(solution)/shard_map/ppermute | solution.py:661
  291.9 37.9 %all-to-all-start.3 = ((bf16[4,128,2048]{2,1,0:T(8,128)(2,1)}), bf16[4,128,2048]{2,1,0:T(8,128)(2,1)S(1)}, u32[]{:S(2)}, u32[]{:S(2)}) async-start(bf16[4,128,2048]{2,1,0:T(8,128)(2,1)} %shard_map.219), calls=%async_computation.3 | async-start | bytes 4194304 | tf_op jit(solution)/shard_map/all_to_all | solution.py:773
  296.7 8.5 %collective-permute-start.32 = (bf16[768,128]{1,0:T(8,128)(2,1)}, bf16[768,128]{1,0:T(8,128)(2,1)S(1)}, u32[]{:S(2)}, u32[]{:S(2)}) collective-permute-start(bf16[768,128]{1,0:T(8,128)(2,1)} %get-tuple-element.249), channel_id=1, source_target_pairs={{0,32},{32,0},{64,96},{96,64},{1,33},{33,1},{65,97},{97,65},{2,34}... | collective-permute-start | bytes 589832 | tf_op jit(solution)/shard_map/ppermute | solution.py:666
  297.8 8.8 %collective-permute-start.33 = (bf16[768,128]{1,0:T(8,128)(2,1)}, bf16[768,128]{1,0:T(8,128)(2,1)S(1)}, u32[]{:S(2)}, u32[]{:S(2)}) collective-permute-start(bf16[768,128]{1,0:T(8,128)(2,1)} %get-tuple-element.250), channel_id=1, source_target_pairs={{0,64},{32,96},{64,0},{96,32},{1,65},{33,97},{65,1},{97,33},{2,66}... | collective-permute-start | bytes 589832 | tf_op jit(solution)/shard_map/ppermute | solution.py:666
  300.9 11.1 %collective-permute-start.34 = (bf16[768,128]{1,0:T(8,128)(2,1)S(1)}, bf16[768,128]{1,0:T(8,128)(2,1)S(1)}, u32[]{:S(2)}, u32[]{:S(2)}) collective-permute-start(bf16[768,128]{1,0:T(8,128)(2,1)S(1)} %copy-done.43), channel_id=1, source_target_pairs={{0,96},{32,64},{64,32},{96,0},{1,97},{33,65},{65,33},{97,1},{2,98}... | collective-permute-start | bytes 589832 | tf_op jit(solution)/shard_map/ppermute | solution.py:666
  312.0 17.0 %collective-permute-start.38 = (bf16[2112,128]{1,0:T(8,128)(2,1)S(1)}, bf16[2112,128]{1,0:T(8,128)(2,1)S(1)}, u32[]{:S(2)}, u32[]{:S(2)}) collective-permute-start(bf16[2112,128]{1,0:T(8,128)(2,1)S(1)} %fusion), channel_id=1, source_target_pairs={{0,64},{64,0},{1,65},{65,1},{2,66},{66,2},{3,67},{67,3},{4,68},{68... | collective-permute-start | bytes 1622024 | tf_op jit(solution)/shard_map/ppermute | solution.py:661
  329.8 15.7 %collective-permute-start.39 = (bf16[8,1024,128]{2,1,0:T(8,128)(2,1)}, bf16[8,1024,128]{2,1,0:T(8,128)(2,1)}, u32[]{:S(2)}, u32[]{:S(2)}) collective-permute-start(bf16[8,1024,128]{2,1,0:T(8,128)(2,1)} %get-tuple-element.278), channel_id=1, source_target_pairs={{0,8},{8,0},{1,9},{9,1},{2,10},{10,2},{3,11},{11,3},{4,12},{12,4},... | collective-permute-start | bytes 6291464 | tf_op jit(solution)/shard_map/ppermute | solution.py:661
  329.8 33.0 %all-to-all-start.4 = ((bf16[8,64,2048]{2,1,0:T(8,128)(2,1)}), bf16[8,64,2048]{2,1,0:T(8,128)(2,1)}, u32[]{:S(2)}, u32[]{:S(2)}) async-start(bf16[8,64,2048]{2,1,0:T(8,128)(2,1)} %bitcast.60), calls=%async_computation.4 | async-start | bytes 4194304 | tf_op jit(solution)/shard_map/all_to_all | solution.py:773
  348.9 25.1 %collective-permute-start.42 = (bf16[2,1024,128]{2,1,0:T(8,128)(2,1)}, bf16[2,1024,128]{2,1,0:T(8,128)(2,1)}, u32[]{:S(2)}, u32[]{:S(2)}) collective-permute-start(bf16[2,1024,128]{2,1,0:T(8,128)(2,1)} %get-tuple-element.287), channel_id=1, source_target_pairs={{0,16},{16,32},{32,48},{48,0},{1,17},{17,33},{33,49},{49,1},{2,18}... | collective-permute-start | bytes 1572872 | tf_op jit(solution)/shard_map/ppermute | solution.py:760
  350.0 24.0 %collective-permute-start.43 = (bf16[2,1024,128]{2,1,0:T(8,128)(2,1)}, bf16[2,1024,128]{2,1,0:T(8,128)(2,1)}, u32[]{:S(2)}, u32[]{:S(2)}) collective-permute-start(bf16[2,1024,128]{2,1,0:T(8,128)(2,1)} %get-tuple-element.288), channel_id=1, source_target_pairs={{0,48},{16,0},{32,16},{48,32},{1,49},{17,1},{33,17},{49,33},{2,50}... | collective-permute-start | bytes 1572872 | tf_op jit(solution)/shard_map/ppermute | solution.py:760
  352.2 22.7 %collective-permute-start.50 = (bf16[2,1024,128]{2,1,0:T(8,128)(2,1)}, bf16[2,1024,128]{2,1,0:T(8,128)(2,1)}, u32[]{:S(2)}, u32[]{:S(2)}) collective-permute-start(bf16[2,1024,128]{2,1,0:T(8,128)(2,1)} %get-tuple-element.294), channel_id=1, source_target_pairs={{0,32},{16,48},{32,0},{48,16},{1,33},{17,49},{33,1},{49,17},{2,34}... | collective-permute-start | bytes 1572872 | tf_op jit(solution)/shard_map/ppermute | solution.py:760
  353.0 8.3 %collective-permute-start.40 = (f32[35,256]{1,0:T(8,128)S(1)}, f32[35,256]{1,0:T(8,128)S(1)}, u32[]{:S(2)}, u32[]{:S(2)}) collective-permute-start(f32[35,256]{1,0:T(8,128)S(1)} %add.157), channel_id=1, source_target_pairs={{0,64},{64,0},{1,65},{65,1},{2,66},{66,2},{3,67},{67,3},{4,68},{68... | collective-permute-start | bytes 107528 | tf_op jit(solution)/shard_map/ppermute | solution.py:796
  366.7 8.2 %collective-permute-start.41 = (bf16[64,2176]{1,0:T(8,128)(2,1)}, bf16[64,2176]{1,0:T(8,128)(2,1)S(1)}, u32[]{:S(2)}, u32[]{:S(2)}) collective-permute-start(bf16[64,2176]{1,0:T(8,128)(2,1)} %shard_map.224.refs_0_), channel_id=1, source_target_pairs={{0,1},{1,0},{2,3},{3,2},{4,5},{5,4},{6,7},{7,6},{8,9},{9,8},{10,11... | collective-permute-start | bytes 835592 | tf_op jit(solution)/shard_map/ppermute | solution.py:661
  367.2 14.9 %collective-permute-start.46 = (bf16[64,2176]{1,0:T(8,128)(2,1)}, bf16[64,2176]{1,0:T(8,128)(2,1)}, u32[]{:S(2)}, u32[]{:S(2)}) collective-permute-start(bf16[64,2176]{1,0:T(8,128)(2,1)} %shard_map.224.refs_0_), channel_id=1, source_target_pairs={{0,4},{2,6},{4,0},{6,2},{1,5},{3,7},{5,1},{7,3},{8,12},{10,14},{12... | collective-permute-start | bytes 835592 | tf_op jit(solution)/shard_map/ppermute | solution.py:781
  377.0 8.6 %collective-permute-start.51 = (bf16[1024,128]{1,0:T(8,128)(2,1)}, bf16[1024,128]{1,0:T(8,128)(2,1)}, u32[]{:S(2)}, u32[]{:S(2)}) collective-permute-start(bf16[1024,128]{1,0:T(8,128)(2,1)} %fusion.1), channel_id=1, source_target_pairs={{0,64},{64,0},{1,65},{65,1},{2,66},{66,2},{3,67},{67,3},{4,68},{68... | collective-permute-start | bytes 786440 | tf_op jit(solution)/shard_map/ppermute | solution.py:661
  378.9 16.5 %collective-permute-start.44 = (bf16[64,2176]{1,0:T(8,128)(2,1)}, bf16[64,2176]{1,0:T(8,128)(2,1)}, u32[]{:S(2)}, u32[]{:S(2)}) collective-permute-start(bf16[64,2176]{1,0:T(8,128)(2,1)} %shard_map.224.refs_0_), channel_id=1, source_target_pairs={{0,2},{2,4},{4,6},{6,0},{1,3},{3,5},{5,7},{7,1},{8,10},{10,12},{12... | collective-permute-start | bytes 835592 | tf_op jit(solution)/shard_map/ppermute | solution.py:781
  379.7 15.7 %collective-permute-start.45 = (bf16[64,2176]{1,0:T(8,128)(2,1)}, bf16[64,2176]{1,0:T(8,128)(2,1)}, u32[]{:S(2)}, u32[]{:S(2)}) collective-permute-start(bf16[64,2176]{1,0:T(8,128)(2,1)} %shard_map.224.refs_0_), channel_id=1, source_target_pairs={{0,6},{2,0},{4,2},{6,4},{1,7},{3,1},{5,3},{7,5},{8,14},{10,8},{12,... | collective-permute-start | bytes 835592 | tf_op jit(solution)/shard_map/ppermute | solution.py:781
  382.1 13.2 %collective-permute-start.47 = (bf16[64,2176]{1,0:T(8,128)(2,1)S(1)}, bf16[64,2176]{1,0:T(8,128)(2,1)}, u32[]{:S(2)}, u32[]{:S(2)}) collective-permute-start(bf16[64,2176]{1,0:T(8,128)(2,1)S(1)} %collective-permute-done.41.refs_1_), channel_id=1, source_target_pairs={{0,2},{2,4},{4,6},{6,0},{1,3},{3,5},{5,7},{7,1},{8,10},{10,12},{12... | collective-permute-start | bytes 835592 | tf_op jit(solution)/shard_map/ppermute | solution.py:781
  382.1 13.2 %collective-permute-start.48 = (bf16[64,2176]{1,0:T(8,128)(2,1)S(1)}, bf16[64,2176]{1,0:T(8,128)(2,1)}, u32[]{:S(2)}, u32[]{:S(2)}) collective-permute-start(bf16[64,2176]{1,0:T(8,128)(2,1)S(1)} %collective-permute-done.41.refs_1_), channel_id=1, source_target_pairs={{0,6},{2,0},{4,2},{6,4},{1,7},{3,1},{5,3},{7,5},{8,14},{10,8},{12,... | collective-permute-start | bytes 835592 | tf_op jit(solution)/shard_map/ppermute | solution.py:781
  385.5 9.9 %collective-permute-start.49 = (bf16[64,2176]{1,0:T(8,128)(2,1)}, bf16[64,2176]{1,0:T(8,128)(2,1)}, u32[]{:S(2)}, u32[]{:S(2)}) collective-permute-start(bf16[64,2176]{1,0:T(8,128)(2,1)} %collective-permute-done.46.refs_4_), channel_id=1, source_target_pairs={{0,1},{1,0},{2,3},{3,2},{4,5},{5,4},{6,7},{7,6},{8,9},{9,8},{10,11... | collective-permute-start | bytes 835592 | tf_op jit(solution)/shard_map/ppermute | solution.py:661
  (62 other events, 327.7 us)

commit v2 on v1

--- a/solution.py
+++ b/solution.py
@@ -59,7 +59,8 @@
 
 
 def kernel_call(
-    body, outs, inputs, *, small=(), small_outs=(), scalars=(), scratch=(), late=0, flops=0, exps=0, mib=12, quick=False, moved=0
+    body, outs, inputs, *, small=(), small_outs=(), scalars=(), scratch=(), late=0, flops=0, exps=0, mib=12, quick=False, moved=0,
+    leaving=False,
 ):
     inputs = [a if isinstance(a, (tuple, list)) else (a, 0, a.shape[0]) for a in inputs]
     flat = [x for a in inputs for x in (a if isinstance(a, list) else a[:1])]
@@ -95,16 +96,23 @@
             for move in moves[early:]:
                 move.wait()
 
+        outward = [
+            pltpu.make_async_copy(a, b, left.at[k]) for k, (a, b) in enumerate(zip(held_out, far_out))
+        ]
+        gone = []
+
+        def leave(*which):
+            for k in which:
+                outward[k].start()
+                gone.append(k)
+
         body(
             *([arrive] if late else []),
+            *([leave] if leaving else []),
             *scalar_refs, *held_in, *near_in, *held_out, *near_out, *rest,
         )
-        moves = [
-            pltpu.make_async_copy(a, b, left.at[k]) for k, (a, b) in enumerate(zip(held_out, far_out))
-        ]
-        for move in moves:
-            move.start()
-        for move in moves:
+        leave(*[k for k in range(len(outward)) if k not in gone])
+        for move in outward:
             move.wait()
 
     vmem, hbm = pl.BlockSpec(memory_space=pltpu.VMEM), pl.BlockSpec(memory_space=pltpu.HBM)
@@ -187,7 +195,7 @@
 
 
 def project_kernel(
-    arrive, place, tok, table, w, gain, shift, bias,
+    arrive, leave, place, tok, table, w, gain, shift, bias,
     normed, stats, x0, x1, x2, x3, cosine_out, sine_out, kept,
 ):
     rows = 64
@@ -206,6 +214,7 @@
     cosine, sine = rotation_table(table[...])
     cosine_out[...] = cosine
     sine_out[...] = sine
+    leave(0, 1, 6, 7)
     arrive()
     mixed = [nn(normed[...], w[c]) + bias[c : c + 1, :] for c in range(3)]
     for pair in range(2):
@@ -451,7 +460,7 @@
     grad_hidden[...] = nt(cot[...], w[...])
 
 
-def feed_kernel(arrive, place, second, w_gate, w_up, grad_hidden, hidden, grad_gate, grad_up, partial):
+def feed_kernel(arrive, leave, place, second, w_gate, w_up, grad_hidden, hidden, grad_gate, grad_up, partial):
     gate = nt(second[...], w_gate[0])
     arrive()
     up = nt(second[...], w_up[0])
@@ -461,6 +470,7 @@
     grad = grad_hidden[...]
     grad_up[...] = (grad * activated).astype(LOW)
     grad_gate[...] = (grad * up * sigmoid * (1.0 + gate * (1.0 - sigmoid))).astype(LOW)
+    leave(0, 1, 2)
     for n in range(4):
         at = slice(n * 512, n * 512 + 512)
         partial[:, at] = (nn(grad_gate[...], w_gate[0, :, at]) + nn(grad_up[...], w_up[0, :, at])).astype(LOW)
@@ -842,6 +852,7 @@
         scalars=(place,),
         scratch=(pltpu.VMEM((4, BLOCK + HALF, 128), LOW),),
         late=1,
+        leaving=True,
         flops=2 * 512 * 2048 * 768,
     )
     (grad_hidden,) = kernel_call(
@@ -915,6 +926,7 @@
         (second_low, (w2, 0, 1), (w2, 1, 1), grad_hidden),
         scalars=(place,),
         late=2,
+        leaving=True,
         flops=8 * 512 * 2048 * 704,
         mib=24,
     )
@@ -1034,7 +1046,8 @@
     vectors, *rest_z = tied((vectors, *rest_z))
     vectors = summed_by_pairs(vectors, (("xh", 2, 1),))
     rest_1, rest_3 = z_permute(rest_z[1], 1), z_permute(rest_z[3], 3)
-    normed_parts, vectors = tied((normed_parts, vectors))
+    feed_w = feed_keep + feed_received.astype(WIDE)
+    normed_parts, vectors, layer_out, feed_w = tied((normed_parts, vectors, layer_out, feed_w))
     bias_grad = vectors[32:]
     (last_share,) = kernel_call(
         first_gradient_kernel,
@@ -1049,7 +1062,6 @@
     rest_z = (rest_z[0], rest_1, z_permute(rest_z[2], 2), rest_3)
     rest_keep, rest_send = xh_halves(rest_z)
     rest_w = rest_keep + swapped(rest_send, "xh").astype(WIDE)
-    feed_w = feed_keep + feed_received.astype(WIDE)
     return (
         layer_out,
         grad_tokens,

time: 407 us -> 406 us (level)
  the two profiles are of different devices: /device:TPU:0 before, /device:TPU:8 now
where the time goes in v2:
time: 406 us; the launch traced here: 398 us
  Pallas kernels  166 us (41%)
  waiting for transfers between devices  101 us (25%)
  starting transfers between devices  97.5 us (24%)
  local copies, waits for them, and re-layouts  20 us (5%)
  other arithmetic  8.82 us (2%)
    pallas_call x19, Pallas kernels, kernel_call(): pl.pallas_call(run, out_shape=(*[pltpu.HBM(a.shape, a.dtype) for a in out...  152 us
    ppermute x12, starting transfers between devices, across(): lax.ppermute(pieces[k], SPREAD, [(i, i ^ k) for i in range(4)])  26.7 us
    all_to_all x5, starting transfers between devices, dealt(): return lax.all_to_all(x, axis, split_axis=0, concat_axis=0, tiled=True)  25.8 us
    all_to_all x5, waiting for transfers between devices, dealt(): return lax.all_to_all(x, axis, split_axis=0, concat_axis=0, tiled=True)  25.3 us
    ppermute x12, waiting for transfers between devices, across(): lax.ppermute(pieces[k], SPREAD, [(i, i ^ k) for i in range(4)])  18.2 us
    ppermute x17, waiting for transfers between devices, swapped(): return lax.ppermute(x, axis, [(0, 1), (1, 0)])  17.8 us
    ppermute x13, starting transfers between devices, y_moved(): return lax.ppermute(x, 'y', [(i, (i + distance) % 4) for i in range(4)])  16.8 us
    ppermute x6, waiting for transfers between devices, z_permute(): return lax.ppermute(part, Z, [(i, (i + distance) % 4) for i in range(4)])  16.5 us
  transfers between devices with their start and end apart: 57, of which 31 were waited for; matrix products, arithmetic and copies ran while one was open for 4% of the time, Pallas kernels for 29%

profile of v2, /device:TPU:8, one launch (start us, length us, event | category | flops | bytes accessed | tf_op | source)
XLA Modules:
  0.0 398.0 jit_solution(6631812550596156782)
XLA Ops:
  5.6 7.9 %shard_map.203 = (bf16[512,2048]{1,0:T(8,128)(2,1)}, f32[512,128]{1,0:T(8,128)}, bf16[768,128]{1,0:T(8,128)(2,1)}, bf16[768,128]{1,0:T(8,128)(2,1)}, bf16[768,12...) custom-call(s32[5]{0:T(128)S(1)} %stack.38.refs_0_.place, ...), custom_call_target="tpu_custom_call" | custom-call | flops 1610612736 | bytes 8945664 | tf_op jit(solution)/shard_map/pallas_call | solution.py:127
  13.5 4.0 collective-permute-start
  17.4 3.0 collective-permute-start.1
  20.5 5.4 %shard_map.204.refs_11_ = f32[512,704]{1,0:T(8,128)} custom-call(bf16[512,2048]{1,0:T(8,128)(2,1)} %refs_12_.1, bf16[704,2048]{1,0:T(8,128)(2,1)} %refs_1_.3), custom_call_target="tpu_custom_call" | custom-call | flops 1476395008 | bytes 6422528 | tf_op jit(solution)/shard_map/pallas_call | solution.py:127
  27.9 2.7 collective-permute-done.2.refs_6_
  33.7 13.0 %shard_map.205 = (f32[4,128,512]{2,1,0:T(8,128)}, f32[4,8,512]{2,1,0:T(8,128)}) custom-call(s32[5]{0:T(128)S(1)} %stack.38.refs_0_.place, bf16[4,512,128]{2,1,0:T(8,128)(2,1)} %copy-done.21, bf16[4,512,128]{2,1,0:T(8,128)(2,1)} %copy-done.46, bf16[768,128]{1,0:T(8,128)(2,1)} %get-tuple-element.160.refs_3_, bf16[768,128]{1,0:T(8,128)(2,1)} %copy-done.43, ...), custom_call_target="tpu_custom_call" | custom-call | flops 2684354560 | bytes 2490368 | tf_op jit(solution)/shard_map/pallas_call | solution.py:127
  49.7 14.3 %shard_map.206 = (bf16[256,128]{1,0:T(8,128)(2,1)}, bf16[256,128]{1,0:T(8,128)(2,1)}, bf16[256,128]{1,0:T(8,128)(2,1)}, bf16[256,128]{1,0:T(8,128)(2,1)}, f32[4,128,512]{2,1,0:T(8,128)}, /*index=5*/f32[4,8,512]{2,1,0:T(8,128)}) custom-call(s32[5]{0:T(128)S(1)} %stack.38.refs_0_.place, bf16[4,512,128]{2,1,0:T(8,128)(2,1)} %copy-done.47, ...), custom_call_target="tpu_custom_call" | custom-call | flops 2684354560 | bytes 3866624 | tf_op jit(solution)/shard_map/pallas_call | solution.py:127
  66.1 3.0 collective-permute-start.7
  72.1 5.4 %collective-permute-done.8.refs_4_ = bf16[256,128]{1,0:T(8,128)(2,1)S(1)} collective-permute-done((bf16[256,128]{1,0:T(8,128)(2,1)}, bf16[256,128]{1,0:T(8,128)(2,1)S(1)}, u32[]{:S(2)}, u32[]{:S(2)}) %collective-permute-start.8) | collective-permute-done | bytes 65568 | tf_op jit(solution)/shard_map/ppermute | solution.py:676
  78.1 4.2 %shard_map.207 = (bf16[512,256]{1,0:T(8,128)(2,1)}, bf16[128,2048]{1,0:T(8,128)(2,1)}, bf16[128,2048]{1,0:T(8,128)(2,1)}, bf16[64,2048]{1,0:T(8,128)(2,1)}, bf16...) custom-call(s32[5]{0:T(128)S(1)} %stack.38.refs_0_.place, ...), custom_call_target="tpu_custom_call" | custom-call | flops 536870912 | bytes 3670016 | tf_op jit(solution)/shard_map/pallas_call | solution.py:127
  85.0 6.0 %collective-permute-done.11.refs_3_ = bf16[64,2048]{1,0:T(8,128)(2,1)S(1)} collective-permute-done((bf16[64,2048]{1,0:T(8,128)(2,1)}, bf16[64,2048]{1,0:T(8,128)(2,1)S(1)}, u32[]{:S(2)}, u32[]{:S(2)}) %collective-permute-start.11) | collective-permute-done | bytes 262176 | tf_op jit(solution)/shard_map/ppermute | solution.py:671
  91.0 3.9 collective-permute-done.9.refs_1_
  97.0 3.0 shard_map.208
  102.9 3.7 collective-permute-done.12.refs_4_
  109.5 4.2 %shard_map.209 = (bf16[64,2048]{1,0:T(8,128)(2,1)}, f32[64,2048]{1,0:T(8,128)}, f32[64,2048]{1,0:T(8,128)}, f32[64,128]{1,0:T(8,128)}) custom-call(s32[5]{0:T(128)S(1)} %stack.38.refs_0_.place, bf16[128,2048]{1,0:T(8,128)(2,1)} %copy-done.8, bf16[128,2048]{1,0:T(8,128)(2,1)} %copy-done.9, bf16[64,2048]{1,0:T(8,128)(2,1)} %get-tuple-element.175.refs_3_, ...), custom_call_target="tpu_custom_call" | custom-call | bytes 3440640 | tf_op jit(solution)/shard_map/pallas_call | solution.py:127
  122.4 3.8 collective-permute-done.17.refs_5_.refs_6_
  133.7 12.7 %shard_map.210 = (bf16[512,704]{1,0:T(8,128)(2,1)}, bf16[512,704]{1,0:T(8,128)(2,1)}, bf16[512,704]{1,0:T(8,128)(2,1)}, bf16[512,2048]{1,0:T(8,128)(2,1)}) custom-call(s32[5]{0:T(128)S(1)} %stack.38.refs_0_.place, bf16[64,2048]{1,0:T(8,128)(2,1)} %get-tuple-element.182.refs_1_.refs_2_, bf16[64,2048]{1,0:T(8,128)(2,1)} %copy-done.34, ...), custom_call_target="tpu_custom_call" | custom-call | flops 5905580032 | bytes 13565952 | tf_op jit(solution)/shard_map/pallas_call | solution.py:127
  146.4 4.8 %all-to-all-start = ((bf16[8,64,2048]{2,1,0:T(8,128)(2,1)}), bf16[8,64,2048]{2,1,0:T(8,128)(2,1)S(1)}, u32[]{:S(2)}, u32[]{:S(2)}) async-start(bf16[8,64,2048]{2,1,0:T(8,128)(2,1)} %bitcast.62), calls=%async_computation | async-start | bytes 4194304 | tf_op jit(solution)/shard_map/all_to_all | solution.py:783
  151.2 12.2 %shard_map.211 = (bf16[8,2112,128]{2,1,0:T(8,128)(2,1)}, bf16[8,2112,128]{2,1,0:T(8,128)(2,1)}) custom-call(s32[5]{0:T(128)S(1)} %stack.38.refs_0_.place, bf16[512,704]{1,0:T(8,128)(2,1)} %get-tuple-element.185.refs_1_, bf16[64,2048]{1,0:T(8,128)(2,1)} %get-tuple-element.182.refs_1_.refs_2_, bf16[64,2048]{1,0:T(8,128)(2,1)} %copy-done.34, ...), custom_call_target="tpu_custom_call" | custom-call | tf_op jit(solution)/shard_map/pallas_call | solution.py:127
  163.4 9.2 %all-to-all-done.refs_0_ = bf16[8,64,2048]{2,1,0:T(8,128)(2,1)S(1)} async-done(((bf16[8,64,2048]{2,1,0:T(8,128)(2,1)}), bf16[8,64,2048]{2,1,0:T(8,128)(2,1)S(1)}, u32[]{:S(2)}, u32[]{:S(2)}) %all-to-all-start) | async-done | bytes 2097184 | tf_op jit(solution)/shard_map/all_to_all | solution.py:783
  172.7 3.7 shard_map.213
  176.3 5.5 %all-to-all-start.1 = ((bf16[8,64,2048]{2,1,0:T(8,128)(2,1)}), bf16[8,64,2048]{2,1,0:T(8,128)(2,1)S(1)}, u32[]{:S(2)}, u32[]{:S(2)}) async-start(bf16[8,64,2048]{2,1,0:T(8,128)(2,1)} %get-tuple-element.198), calls=%async_computation.1 | async-start | bytes 4194304 | tf_op jit(solution)/shard_map/all_to_all | solution.py:783
  181.8 5.7 %shard_map.212 = (bf16[2,2112,128]{2,1,0:T(8,128)(2,1)}, bf16[2,2112,128]{2,1,0:T(8,128)(2,1)}, bf16[2,2112,128]{2,1,0:T(8,128)(2,1)}, bf16[2,2112,128]{2,1,0:T(8,128)(2,1)}) custom-call(s32[1]{0:T(128)} %bitcast.12.place, bf16[8,2112,128]{2,1,0:T(8,128)(2,1)} %get-tuple-element.190.mine, bf16[8,2112,128]{2,1,0:T(8,128)(2,1)} %collective-permute-done.21.received), custom_call_target="tpu_custom_call" | custom-call | tf_op jit(solution)/shard_map/pallas_call | solution.py:711
  191.0 3.1 convolution_convert_fusion
  194.2 13.8 %all-to-all-done.1 = bf16[8,64,2048]{2,1,0:T(8,128)(2,1)S(1)} async-done(((bf16[8,64,2048]{2,1,0:T(8,128)(2,1)}), bf16[8,64,2048]{2,1,0:T(8,128)(2,1)S(1)}, u32[]{:S(2)}, u32[]{:S(2)}) %all-to-all-start.1) | async-done | bytes 2097184 | tf_op jit(solution)/shard_map/all_to_all | solution.py:783
  208.0 3.5 shard_map.214
  211.5 3.5 collective-permute-done.22
  216.0 4.8 %all-to-all-start.2 = ((bf16[4,128,2048]{2,1,0:T(8,128)(2,1)}), bf16[4,128,2048]{2,1,0:T(8,128)(2,1)S(1)}, u32[]{:S(2)}, u32[]{:S(2)}) async-start(bf16[4,128,2048]{2,1,0:T(8,128)(2,1)} %bitcast.61), calls=%async_computation.2 | async-start | bytes 4194304 | tf_op jit(solution)/shard_map/all_to_all | solution.py:783
  221.8 3.2 collective-permute-start.25
  227.5 5.6 %collective-permute-done.26.refs_10_ = bf16[256,128]{1,0:T(8,128)(2,1)S(1)} collective-permute-done((bf16[256,128]{1,0:T(8,128)(2,1)S(1)}, bf16[256,128]{1,0:T(8,128)(2,1)S(1)}, u32[]{:S(2)}, u32[]{:S(2)}) %collective-permute-start.26) | collective-permute-done | bytes 65568 | tf_op jit(solution)/shard_map/ppermute | solution.py:676
  234.6 20.4 %shard_map.215 = (f32[4,128,512]{2,1,0:T(8,128)}, bf16[4,512,128]{2,1,0:T(8,128)(2,1)}, bf16[4,512,128]{2,1,0:T(8,128)(2,1)}) custom-call(s32[5]{0:T(128)S(1)} %stack.38.refs_0_.place, bf16[4,512,128]{2,1,0:T(8,128)(2,1)} %copy-done.47, bf16[4,512,128]{2,1,0:T(8,128)(2,1)} %copy-done.48, bf16[768,128]{1,0:T(8,128)(2,1)} %get-tuple-element.160.refs_3_, ...), custom_call_target="tpu_custom_call" | custom-call | flops 6710886400 | bytes 4849664 | tf_op jit(solution)/shard_map/pallas_call | solution.py:127
  255.0 2.7 collective-permute-done.27
  257.7 2.9 shard_map.216.refs_0_
  263.2 21.2 %shard_map.217 = (bf16[256,128]{1,0:T(8,128)(2,1)}, bf16[256,128]{1,0:T(8,128)(2,1)}, bf16[256,128]{1,0:T(8,128)(2,1)}, bf16[256,128]{1,0:T(8,128)(2,1)}, bf16[4...) custom-call(s32[5]{0:T(128)S(1)} %stack.38.refs_0_.place, bf16[4,512,128]{2,1,0:T(8,128)(2,1)} %copy-done.21, ...), custom_call_target="tpu_custom_call" | custom-call | flops 6710886400 | bytes 5111808 | tf_op jit(solution)/shard_map/pallas_call | solution.py:127
  285.3 2.7 shard_map.219
  292.5 3.1 collective-permute-start.33
  297.9 4.8 %all-to-all-start.3 = ((bf16[4,128,2048]{2,1,0:T(8,128)(2,1)}), bf16[4,128,2048]{2,1,0:T(8,128)(2,1)S(1)}, u32[]{:S(2)}, u32[]{:S(2)}) async-start(bf16[4,128,2048]{2,1,0:T(8,128)(2,1)} %shard_map.219), calls=%async_computation.3 | async-start | bytes 4194304 | tf_op jit(solution)/shard_map/all_to_all | solution.py:783
  304.4 2.7 collective-permute-done.34.refs_4_
  309.3 7.0 %shard_map.220 = (bf16[512,768]{1,0:T(8,128)(2,1)}, bf16[512,2048]{1,0:T(8,128)(2,1)}, f32[1,2048]{1,0:T(1,128)S(1)}, f32[1,2048]{1,0:T(1,128)S(1)}, f32[3,256]{1,0:T(4,128)S(1)}) custom-call(s32[5]{0:T(128)S(1)} %stack.38.refs_0_.place, bf16[768,128]{1,0:T(8,128)(2,1)} %get-tuple-element.258.refs_1_, bf16[768,128]{1,0:T(8,128)(2,1)} %copy-done.41, ...), custom_call_target="tpu_custom_call" | custom-call | flops 1610612736 | bytes 9699328 | tf_op jit(solution)/shard_map/pallas_call | solution.py:127
  316.3 7.8 %shard_map.221 = (bf16[8,1024,128]{2,1,0:T(8,128)(2,1)}, bf16[8,1024,128]{2,1,0:T(8,128)(2,1)}) custom-call(s32[5]{0:T(128)S(1)} %stack.38.refs_0_.place, bf16[512,768]{1,0:T(8,128)(2,1)} %get-tuple-element.272.refs_1_, bf16[512,2048]{1,0:T(8,128)(2,1)} %get-tuple-element.273.refs_2_, bf16[512,256]{1,0:T(8,128)(2,1)} %get-tuple-element.274.refs_3_, ...), custom_call_target="tpu_custom_call" | custom-call | tf_op jit(solution)/shard_map/pallas_call | solution.py:127
  327.1 6.0 %all-to-all-start.4 = ((bf16[8,64,2048]{2,1,0:T(8,128)(2,1)}), bf16[8,64,2048]{2,1,0:T(8,128)(2,1)}, u32[]{:S(2)}, u32[]{:S(2)}) async-start(bf16[8,64,2048]{2,1,0:T(8,128)(2,1)} %bitcast.60), calls=%async_computation.4 | async-start | bytes 4194304 | tf_op jit(solution)/shard_map/all_to_all | solution.py:783
  335.5 3.0 collective-permute-done.36
  341.0 3.0 collective-permute-done.37
  344.0 3.5 shard_map.222
  357.9 3.3 shard_map.224.refs_0_
  364.2 10.2 %collective-permute-done.42 = bf16[2,1024,128]{2,1,0:T(8,128)(2,1)} collective-permute-done((bf16[2,1024,128]{2,1,0:T(8,128)(2,1)}, bf16[2,1024,128]{2,1,0:T(8,128)(2,1)}, u32[]{:S(2)}, u32[]{:S(2)}) %collective-permute-start.42) | collective-permute-done | bytes 524320 | tf_op jit(solution)/shard_map/ppermute | solution.py:770
  381.3 3.7 collective-permute-done.51
  394.0 2.9 shard_map.225
  (246 shorter events, 106.0 us)
Async XLA Ops:
  13.5 14.4 %collective-permute-start = (bf16[768,128]{1,0:T(8,128)(2,1)}, bf16[768,128]{1,0:T(8,128)(2,1)S(1)}, u32[]{:S(2)}, u32[]{:S(2)}) collective-permute-start(bf16[768,128]{1,0:T(8,128)(2,1)} %get-tuple-element.157), channel_id=1, source_target_pairs={{0,32},{32,0},{64,96},{96,64},{1,33},{33,1},{65,97},{97,65},{2,34}... | collective-permute-start | bytes 589832 | tf_op jit(solution)/shard_map/ppermute | solution.py:676
  17.4 10.5 %collective-permute-start.1 = (bf16[768,128]{1,0:T(8,128)(2,1)}, bf16[768,128]{1,0:T(8,128)(2,1)S(1)}, u32[]{:S(2)}, u32[]{:S(2)}) collective-permute-start(bf16[768,128]{1,0:T(8,128)(2,1)} %get-tuple-element.158), channel_id=1, source_target_pairs={{0,64},{32,96},{64,0},{96,32},{1,65},{33,97},{65,1},{97,33},{2,66}... | collective-permute-start | bytes 589832 | tf_op jit(solution)/shard_map/ppermute | solution.py:676
  20.5 10.2 %collective-permute-start.2 = (bf16[768,128]{1,0:T(8,128)(2,1)}, bf16[768,128]{1,0:T(8,128)(2,1)S(1)}, u32[]{:S(2)}, u32[]{:S(2)}) collective-permute-start(bf16[768,128]{1,0:T(8,128)(2,1)} %get-tuple-element.159), channel_id=1, source_target_pairs={{0,96},{32,64},{64,32},{96,0},{1,97},{33,65},{65,33},{97,1},{2,98}... | collective-permute-start | bytes 589832 | tf_op jit(solution)/shard_map/ppermute | solution.py:676
  30.9 15.7 %collective-permute-start.4 = (bf16[4,512,128]{2,1,0:T(8,128)(2,1)S(1)}, bf16[4,512,128]{2,1,0:T(8,128)(2,1)S(1)}, u32[]{:S(2)}, u32[]{:S(2)}) collective-permute-start(bf16[4,512,128]{2,1,0:T(8,128)(2,1)S(1)} %pad_maximum_fusion.refs_1_), channel_id=1, source_target_pairs={{0,16},{16,0},{1,17},{17,1},{2,18},{18,2},{3,19},{19,3},{4,20},{20... | collective-permute-start | bytes 1572872 | tf_op jit(solution)/shard_map/ppermute | solution.py:671
  64.0 6.6 %collective-permute-start.6 = (bf16[256,128]{1,0:T(8,128)(2,1)}, bf16[256,128]{1,0:T(8,128)(2,1)S(1)}, u32[]{:S(2)}, u32[]{:S(2)}) collective-permute-start(bf16[256,128]{1,0:T(8,128)(2,1)} %get-tuple-element.170), channel_id=1, source_target_pairs={{0,32},{32,0},{64,96},{96,64},{1,33},{33,1},{65,97},{97,65},{2,34}... | collective-permute-start | bytes 196616 | tf_op jit(solution)/shard_map/ppermute | solution.py:676
  69.1 8.4 %collective-permute-start.8 = (bf16[256,128]{1,0:T(8,128)(2,1)}, bf16[256,128]{1,0:T(8,128)(2,1)S(1)}, u32[]{:S(2)}, u32[]{:S(2)}) collective-permute-start(bf16[256,128]{1,0:T(8,128)(2,1)} %get-tuple-element.172), channel_id=1, source_target_pairs={{0,96},{32,64},{64,32},{96,0},{1,97},{33,65},{65,33},{97,1},{2,98}... | collective-permute-start | bytes 196616 | tf_op jit(solution)/shard_map/ppermute | solution.py:676
  82.3 12.5 %collective-permute-start.9 = (bf16[128,2048]{1,0:T(8,128)(2,1)}, bf16[128,2048]{1,0:T(8,128)(2,1)S(1)}, u32[]{:S(2)}, u32[]{:S(2)}) collective-permute-start(bf16[128,2048]{1,0:T(8,128)(2,1)} %get-tuple-element.173), channel_id=1, source_target_pairs={{0,2},{2,4},{4,6},{6,0},{1,3},{3,5},{5,7},{7,1},{8,10},{10,12},{12... | collective-permute-start | bytes 1572872 | tf_op jit(solution)/shard_map/ppermute | solution.py:791
  84.0 12.2 %collective-permute-start.10 = (bf16[128,2048]{1,0:T(8,128)(2,1)}, bf16[128,2048]{1,0:T(8,128)(2,1)S(1)}, u32[]{:S(2)}, u32[]{:S(2)}) collective-permute-start(bf16[128,2048]{1,0:T(8,128)(2,1)} %get-tuple-element.174), channel_id=1, source_target_pairs={{0,6},{2,0},{4,2},{6,4},{1,7},{3,1},{5,3},{7,5},{8,14},{10,8},{12,... | collective-permute-start | bytes 1572872 | tf_op jit(solution)/shard_map/ppermute | solution.py:791
  84.4 6.6 %collective-permute-start.11 = (bf16[64,2048]{1,0:T(8,128)(2,1)}, bf16[64,2048]{1,0:T(8,128)(2,1)S(1)}, u32[]{:S(2)}, u32[]{:S(2)}) collective-permute-start(bf16[64,2048]{1,0:T(8,128)(2,1)} %get-tuple-element.176), channel_id=1, source_target_pairs={{0,1},{1,0},{2,3},{3,2},{4,5},{5,4},{6,7},{7,6},{8,9},{9,8},{10,11... | collective-permute-start | bytes 786440 | tf_op jit(solution)/shard_map/ppermute | solution.py:671
  100.0 6.7 %collective-permute-start.12 = (bf16[64,2048]{1,0:T(8,128)(2,1)}, bf16[64,2048]{1,0:T(8,128)(2,1)S(1)}, u32[]{:S(2)}, u32[]{:S(2)}) collective-permute-start(bf16[64,2048]{1,0:T(8,128)(2,1)} %get-tuple-element.179), channel_id=1, source_target_pairs={{0,1},{1,0},{2,3},{3,2},{4,5},{5,4},{6,7},{7,6},{8,9},{9,8},{10,11... | collective-permute-start | bytes 786440 | tf_op jit(solution)/shard_map/ppermute | solution.py:671
  100.7 8.1 %collective-permute-start.13 = (bf16[64,2048]{1,0:T(8,128)(2,1)}, bf16[64,2048]{1,0:T(8,128)(2,1)S(1)}, u32[]{:S(2)}, u32[]{:S(2)}) collective-permute-start(bf16[64,2048]{1,0:T(8,128)(2,1)} %get-tuple-element.180), channel_id=1, source_target_pairs={{0,4},{2,6},{4,0},{6,2},{1,5},{3,7},{5,1},{7,3},{8,12},{10,14},{12... | collective-permute-start | bytes 786440 | tf_op jit(solution)/shard_map/ppermute | solution.py:791
  113.7 6.7 %collective-permute-start.14 = (bf16[64,2048]{1,0:T(8,128)(2,1)}, bf16[64,2048]{1,0:T(8,128)(2,1)S(1)}, u32[]{:S(2)}, u32[]{:S(2)}) collective-permute-start(bf16[64,2048]{1,0:T(8,128)(2,1)} %get-tuple-element.182.refs_1_.refs_2_), channel_id=1, source_target_pairs={{0,1},{1,0},{2,3},{3,2},{4,5},{5,4},{6,7},{7,6},{8,9},{9,8},{10,11... | collective-permute-start | bytes 786440 | tf_op jit(solution)/shard_map/ppermute | solution.py:671
  115.2 11.0 %collective-permute-start.17 = (bf16[64,2048]{1,0:T(8,128)(2,1)}, bf16[64,2048]{1,0:T(8,128)(2,1)S(1)}, u32[]{:S(2)}, u32[]{:S(2)}) collective-permute-start(bf16[64,2048]{1,0:T(8,128)(2,1)} %get-tuple-element.182.refs_1_.refs_2_), channel_id=1, source_target_pairs={{0,4},{2,6},{4,0},{6,2},{1,5},{3,7},{5,1},{7,3},{8,12},{10,14},{12... | collective-permute-start | bytes 786440 | tf_op jit(solution)/shard_map/ppermute | solution.py:791
  117.5 11.4 %collective-permute-start.15 = (bf16[64,2048]{1,0:T(8,128)(2,1)}, bf16[64,2048]{1,0:T(8,128)(2,1)S(1)}, u32[]{:S(2)}, u32[]{:S(2)}) collective-permute-start(bf16[64,2048]{1,0:T(8,128)(2,1)} %get-tuple-element.182.refs_1_.refs_2_), channel_id=1, source_target_pairs={{0,2},{2,4},{4,6},{6,0},{1,3},{3,5},{5,7},{7,1},{8,10},{10,12},{12... | collective-permute-start | bytes 786440 | tf_op jit(solution)/shard_map/ppermute | solution.py:791
  117.5 11.6 %collective-permute-start.16 = (bf16[64,2048]{1,0:T(8,128)(2,1)}, bf16[64,2048]{1,0:T(8,128)(2,1)S(1)}, u32[]{:S(2)}, u32[]{:S(2)}) collective-permute-start(bf16[64,2048]{1,0:T(8,128)(2,1)} %get-tuple-element.182.refs_1_.refs_2_), channel_id=1, source_target_pairs={{0,6},{2,0},{4,2},{6,4},{1,7},{3,1},{5,3},{7,5},{8,14},{10,8},{12,... | collective-permute-start | bytes 786440 | tf_op jit(solution)/shard_map/ppermute | solution.py:791
  120.4 11.4 %collective-permute-start.18 = (bf16[64,2048]{1,0:T(8,128)(2,1)S(1)}, bf16[64,2048]{1,0:T(8,128)(2,1)S(1)}, u32[]{:S(2)}, u32[]{:S(2)}) collective-permute-start(bf16[64,2048]{1,0:T(8,128)(2,1)S(1)} %collective-permute-done.14.refs_2_.refs_3_), channel_id=1, source_target_pairs={{0,2},{2,4},{4,6},{6,0},{1,3},{3,5},{5,7},{7,1},{8,10},{10,12},{12... | collective-permute-start | bytes 786440 | tf_op jit(solution)/shard_map/ppermute | solution.py:791
  121.7 10.2 %collective-permute-start.19 = (bf16[64,2048]{1,0:T(8,128)(2,1)S(1)}, bf16[64,2048]{1,0:T(8,128)(2,1)S(1)}, u32[]{:S(2)}, u32[]{:S(2)}) collective-permute-start(bf16[64,2048]{1,0:T(8,128)(2,1)S(1)} %collective-permute-done.14.refs_2_.refs_3_), channel_id=1, source_target_pairs={{0,6},{2,0},{4,2},{6,4},{1,7},{3,1},{5,3},{7,5},{8,14},{10,8},{12,... | collective-permute-start | bytes 786440 | tf_op jit(solution)/shard_map/ppermute | solution.py:791
  126.2 6.8 %collective-permute-start.20 = (bf16[64,2048]{1,0:T(8,128)(2,1)S(1)}, bf16[64,2048]{1,0:T(8,128)(2,1)S(1)}, u32[]{:S(2)}, u32[]{:S(2)}) collective-permute-start(bf16[64,2048]{1,0:T(8,128)(2,1)S(1)} %collective-permute-done.17.refs_5_.refs_6_), channel_id=1, source_target_pairs={{0,1},{1,0},{2,3},{3,2},{4,5},{5,4},{6,7},{7,6},{8,9},{9,8},{10,11... | collective-permute-start | bytes 786440 | tf_op jit(solution)/shard_map/ppermute | solution.py:671
  146.4 26.2 %all-to-all-start = ((bf16[8,64,2048]{2,1,0:T(8,128)(2,1)}), bf16[8,64,2048]{2,1,0:T(8,128)(2,1)S(1)}, u32[]{:S(2)}, u32[]{:S(2)}) async-start(bf16[8,64,2048]{2,1,0:T(8,128)(2,1)} %bitcast.62), calls=%async_computation | async-start | bytes 4194304 | tf_op jit(solution)/shard_map/all_to_all | solution.py:783
  172.6 9.2 %collective-permute-start.21 = (bf16[8,2112,128]{2,1,0:T(8,128)(2,1)}, bf16[8,2112,128]{2,1,0:T(8,128)(2,1)}, u32[]{:S(2)}, u32[]{:S(2)}) collective-permute-start(bf16[8,2112,128]{2,1,0:T(8,128)(2,1)} %get-tuple-element.191), channel_id=1, source_target_pairs={{0,8},{8,0},{1,9},{9,1},{2,10},{10,2},{3,11},{11,3},{4,12},{12,4},... | collective-permute-start | bytes 12976136 | tf_op jit(solution)/shard_map/ppermute | solution.py:671
  176.3 31.7 %all-to-all-start.1 = ((bf16[8,64,2048]{2,1,0:T(8,128)(2,1)}), bf16[8,64,2048]{2,1,0:T(8,128)(2,1)S(1)}, u32[]{:S(2)}, u32[]{:S(2)}) async-start(bf16[8,64,2048]{2,1,0:T(8,128)(2,1)} %get-tuple-element.198), calls=%async_computation.1 | async-start | bytes 4194304 | tf_op jit(solution)/shard_map/all_to_all | solution.py:783
  187.6 27.5 %collective-permute-start.22 = (bf16[2,2112,128]{2,1,0:T(8,128)(2,1)}, bf16[2,2112,128]{2,1,0:T(8,128)(2,1)S(1)}, u32[]{:S(2)}, u32[]{:S(2)}) collective-permute-start(bf16[2,2112,128]{2,1,0:T(8,128)(2,1)} %get-tuple-element.192), channel_id=1, source_target_pairs={{0,16},{16,32},{32,48},{48,0},{1,17},{17,33},{33,49},{49,1},{2,18}... | collective-permute-start | bytes 3244040 | tf_op jit(solution)/shard_map/ppermute | solution.py:770
  188.7 26.4 %collective-permute-start.23 = (bf16[2,2112,128]{2,1,0:T(8,128)(2,1)}, bf16[2,2112,128]{2,1,0:T(8,128)(2,1)}, u32[]{:S(2)}, u32[]{:S(2)}) collective-permute-start(bf16[2,2112,128]{2,1,0:T(8,128)(2,1)} %get-tuple-element.193), channel_id=1, source_target_pairs={{0,48},{16,0},{32,16},{48,32},{1,49},{17,1},{33,17},{49,33},{2,50}... | collective-permute-start | bytes 3244040 | tf_op jit(solution)/shard_map/ppermute | solution.py:770
  216.0 41.7 %all-to-all-start.2 = ((bf16[4,128,2048]{2,1,0:T(8,128)(2,1)}), bf16[4,128,2048]{2,1,0:T(8,128)(2,1)S(1)}, u32[]{:S(2)}, u32[]{:S(2)}) async-start(bf16[4,128,2048]{2,1,0:T(8,128)(2,1)} %bitcast.61), calls=%async_computation.2 | async-start | bytes 4194304 | tf_op jit(solution)/shard_map/all_to_all | solution.py:783
  220.9 6.5 %collective-permute-start.24 = (bf16[256,128]{1,0:T(8,128)(2,1)S(1)}, bf16[256,128]{1,0:T(8,128)(2,1)S(1)}, u32[]{:S(2)}, u32[]{:S(2)}) collective-permute-start(bf16[256,128]{1,0:T(8,128)(2,1)S(1)} %copy-done.55), channel_id=1, source_target_pairs={{0,32},{32,0},{64,96},{96,64},{1,33},{33,1},{65,97},{97,65},{2,34}... | collective-permute-start | bytes 196616 | tf_op jit(solution)/shard_map/ppermute | solution.py:676
  225.0 8.2 %collective-permute-start.26 = (bf16[256,128]{1,0:T(8,128)(2,1)S(1)}, bf16[256,128]{1,0:T(8,128)(2,1)S(1)}, u32[]{:S(2)}, u32[]{:S(2)}) collective-permute-start(bf16[256,128]{1,0:T(8,128)(2,1)S(1)} %copy-done.52), channel_id=1, source_target_pairs={{0,96},{32,64},{64,32},{96,0},{1,97},{33,65},{65,33},{97,1},{2,98}... | collective-permute-start | bytes 196616 | tf_op jit(solution)/shard_map/ppermute | solution.py:676
  233.2 24.5 %collective-permute-start.27 = (bf16[2,2112,128]{2,1,0:T(8,128)(2,1)}, bf16[2,2112,128]{2,1,0:T(8,128)(2,1)}, u32[]{:S(2)}, u32[]{:S(2)}) collective-permute-start(bf16[2,2112,128]{2,1,0:T(8,128)(2,1)} %get-tuple-element.219), channel_id=1, source_target_pairs={{0,32},{16,48},{32,0},{48,16},{1,33},{17,49},{33,1},{49,17},{2,34}... | collective-permute-start | bytes 3244040 | tf_op jit(solution)/shard_map/ppermute | solution.py:770
  260.8 23.7 %collective-permute-start.29 = (bf16[4,512,128]{2,1,0:T(8,128)(2,1)S(1)}, bf16[4,512,128]{2,1,0:T(8,128)(2,1)S(1)}, u32[]{:S(2)}, u32[]{:S(2)}) collective-permute-start(bf16[4,512,128]{2,1,0:T(8,128)(2,1)S(1)} %add_convert_fusion.1), channel_id=1, source_target_pairs={{0,16},{16,0},{1,17},{17,1},{2,18},{18,2},{3,19},{19,3},{4,20},{20... | collective-permute-start | bytes 1572872 | tf_op jit(solution)/shard_map/ppermute | solution.py:671
  261.9 22.6 %collective-permute-start.30 = (bf16[128,2048]{1,0:T(8,128)(2,1)S(1)}, bf16[128,2048]{1,0:T(8,128)(2,1)S(1)}, u32[]{:S(2)}, u32[]{:S(2)}) collective-permute-start(bf16[128,2048]{1,0:T(8,128)(2,1)S(1)} %copy-done.10), channel_id=1, source_target_pairs={{0,1},{1,0},{2,3},{3,2},{4,5},{5,4},{6,7},{7,6},{8,9},{9,8},{10,11... | collective-permute-start | bytes 1572872 | tf_op jit(solution)/shard_map/ppermute | solution.py:671
  291.3 13.1 %collective-permute-start.32 = (bf16[768,128]{1,0:T(8,128)(2,1)}, bf16[768,128]{1,0:T(8,128)(2,1)S(1)}, u32[]{:S(2)}, u32[]{:S(2)}) collective-permute-start(bf16[768,128]{1,0:T(8,128)(2,1)} %get-tuple-element.251), channel_id=1, source_target_pairs={{0,32},{32,0},{64,96},{96,64},{1,33},{33,1},{65,97},{97,65},{2,34}... | collective-permute-start | bytes 589832 | tf_op jit(solution)/shard_map/ppermute | solution.py:676
  292.5 11.9 %collective-permute-start.33 = (bf16[768,128]{1,0:T(8,128)(2,1)}, bf16[768,128]{1,0:T(8,128)(2,1)}, u32[]{:S(2)}, u32[]{:S(2)}) collective-permute-start(bf16[768,128]{1,0:T(8,128)(2,1)} %get-tuple-element.252), channel_id=1, source_target_pairs={{0,64},{32,96},{64,0},{96,32},{1,65},{33,97},{65,1},{97,33},{2,66}... | collective-permute-start | bytes 589832 | tf_op jit(solution)/shard_map/ppermute | solution.py:676
  295.6 11.5 %collective-permute-start.34 = (bf16[768,128]{1,0:T(8,128)(2,1)}, bf16[768,128]{1,0:T(8,128)(2,1)}, u32[]{:S(2)}, u32[]{:S(2)}) collective-permute-start(bf16[768,128]{1,0:T(8,128)(2,1)} %get-tuple-element.253), channel_id=1, source_target_pairs={{0,96},{32,64},{64,32},{96,0},{1,97},{33,65},{65,33},{97,1},{2,98}... | collective-permute-start | bytes 589832 | tf_op jit(solution)/shard_map/ppermute | solution.py:676
  297.9 29.2 %all-to-all-start.3 = ((bf16[4,128,2048]{2,1,0:T(8,128)(2,1)}), bf16[4,128,2048]{2,1,0:T(8,128)(2,1)S(1)}, u32[]{:S(2)}, u32[]{:S(2)}) async-start(bf16[4,128,2048]{2,1,0:T(8,128)(2,1)} %shard_map.219), calls=%async_computation.3 | async-start | bytes 4194304 | tf_op jit(solution)/shard_map/all_to_all | solution.py:783
  307.1 16.9 %collective-permute-start.38 = (bf16[2112,128]{1,0:T(8,128)(2,1)S(1)}, bf16[2112,128]{1,0:T(8,128)(2,1)S(1)}, u32[]{:S(2)}, u32[]{:S(2)}) collective-permute-start(bf16[2112,128]{1,0:T(8,128)(2,1)S(1)} %fusion), channel_id=1, source_target_pairs={{0,64},{64,0},{1,65},{65,1},{2,66},{66,2},{3,67},{67,3},{4,68},{68... | collective-permute-start | bytes 1622024 | tf_op jit(solution)/shard_map/ppermute | solution.py:671
  324.8 19.2 %collective-permute-start.39 = (bf16[8,1024,128]{2,1,0:T(8,128)(2,1)}, bf16[8,1024,128]{2,1,0:T(8,128)(2,1)}, u32[]{:S(2)}, u32[]{:S(2)}) collective-permute-start(bf16[8,1024,128]{2,1,0:T(8,128)(2,1)} %get-tuple-element.279), channel_id=1, source_target_pairs={{0,8},{8,0},{1,9},{9,1},{2,10},{10,2},{3,11},{11,3},{4,12},{12,4},... | collective-permute-start | bytes 6291464 | tf_op jit(solution)/shard_map/ppermute | solution.py:671
  327.1 30.1 %all-to-all-start.4 = ((bf16[8,64,2048]{2,1,0:T(8,128)(2,1)}), bf16[8,64,2048]{2,1,0:T(8,128)(2,1)}, u32[]{:S(2)}, u32[]{:S(2)}) async-start(bf16[8,64,2048]{2,1,0:T(8,128)(2,1)} %bitcast.60), calls=%async_computation.4 | async-start | bytes 4194304 | tf_op jit(solution)/shard_map/all_to_all | solution.py:783
  347.6 9.7 %collective-permute-start.40 = (f32[35,256]{1,0:T(8,128)S(1)}, f32[35,256]{1,0:T(8,128)S(1)}, u32[]{:S(2)}, u32[]{:S(2)}) collective-permute-start(f32[35,256]{1,0:T(8,128)S(1)} %add.157), channel_id=1, source_target_pairs={{0,64},{64,0},{1,65},{65,1},{2,66},{66,2},{3,67},{67,3},{4,68},{68... | collective-permute-start | bytes 107528 | tf_op jit(solution)/shard_map/ppermute | solution.py:806
  349.8 24.6 %collective-permute-start.42 = (bf16[2,1024,128]{2,1,0:T(8,128)(2,1)}, bf16[2,1024,128]{2,1,0:T(8,128)(2,1)}, u32[]{:S(2)}, u32[]{:S(2)}) collective-permute-start(bf16[2,1024,128]{2,1,0:T(8,128)(2,1)} %get-tuple-element.291), channel_id=1, source_target_pairs={{0,16},{16,32},{32,48},{48,0},{1,17},{17,33},{33,49},{49,1},{2,18}... | collective-permute-start | bytes 1572872 | tf_op jit(solution)/shard_map/ppermute | solution.py:770
  350.9 23.5 %collective-permute-start.43 = (bf16[2,1024,128]{2,1,0:T(8,128)(2,1)}, bf16[2,1024,128]{2,1,0:T(8,128)(2,1)}, u32[]{:S(2)}, u32[]{:S(2)}) collective-permute-start(bf16[2,1024,128]{2,1,0:T(8,128)(2,1)} %get-tuple-element.292), channel_id=1, source_target_pairs={{0,48},{16,0},{32,16},{48,32},{1,49},{17,1},{33,17},{49,33},{2,50}... | collective-permute-start | bytes 1572872 | tf_op jit(solution)/shard_map/ppermute | solution.py:770
  353.0 21.4 %collective-permute-start.50 = (bf16[2,1024,128]{2,1,0:T(8,128)(2,1)}, bf16[2,1024,128]{2,1,0:T(8,128)(2,1)}, u32[]{:S(2)}, u32[]{:S(2)}) collective-permute-start(bf16[2,1024,128]{2,1,0:T(8,128)(2,1)} %get-tuple-element.298), channel_id=1, source_target_pairs={{0,32},{16,48},{32,0},{48,16},{1,33},{17,49},{33,1},{49,17},{2,34}... | collective-permute-start | bytes 1572872 | tf_op jit(solution)/shard_map/ppermute | solution.py:770
  361.2 13.2 %collective-permute-start.41 = (bf16[64,2176]{1,0:T(8,128)(2,1)}, bf16[64,2176]{1,0:T(8,128)(2,1)S(1)}, u32[]{:S(2)}, u32[]{:S(2)}) collective-permute-start(bf16[64,2176]{1,0:T(8,128)(2,1)} %shard_map.224.refs_0_), channel_id=1, source_target_pairs={{0,1},{1,0},{2,3},{3,2},{4,5},{5,4},{6,7},{7,6},{8,9},{9,8},{10,11... | collective-permute-start | bytes 835592 | tf_op jit(solution)/shard_map/ppermute | solution.py:671
  362.2 18.8 %collective-permute-start.46 = (bf16[64,2176]{1,0:T(8,128)(2,1)}, bf16[64,2176]{1,0:T(8,128)(2,1)S(1)}, u32[]{:S(2)}, u32[]{:S(2)}) collective-permute-start(bf16[64,2176]{1,0:T(8,128)(2,1)} %shard_map.224.refs_0_), channel_id=1, source_target_pairs={{0,4},{2,6},{4,0},{6,2},{1,5},{3,7},{5,1},{7,3},{8,12},{10,14},{12... | collective-permute-start | bytes 835592 | tf_op jit(solution)/shard_map/ppermute | solution.py:791
  375.8 9.2 %collective-permute-start.51 = (bf16[1024,128]{1,0:T(8,128)(2,1)S(1)}, bf16[1024,128]{1,0:T(8,128)(2,1)S(1)}, u32[]{:S(2)}, u32[]{:S(2)}) collective-permute-start(bf16[1024,128]{1,0:T(8,128)(2,1)S(1)} %fusion.1), channel_id=1, source_target_pairs={{0,64},{64,0},{1,65},{65,1},{2,66},{66,2},{3,67},{67,3},{4,68},{68... | collective-permute-start | bytes 786440 | tf_op jit(solution)/shard_map/ppermute | solution.py:671
  377.2 15.0 %collective-permute-start.44 = (bf16[64,2176]{1,0:T(8,128)(2,1)}, bf16[64,2176]{1,0:T(8,128)(2,1)S(1)}, u32[]{:S(2)}, u32[]{:S(2)}) collective-permute-start(bf16[64,2176]{1,0:T(8,128)(2,1)} %shard_map.224.refs_0_), channel_id=1, source_target_pairs={{0,2},{2,4},{4,6},{6,0},{1,3},{3,5},{5,7},{7,1},{8,10},{10,12},{12... | collective-permute-start | bytes 835592 | tf_op jit(solution)/shard_map/ppermute | solution.py:791
  378.9 13.3 %collective-permute-start.45 = (bf16[64,2176]{1,0:T(8,128)(2,1)}, bf16[64,2176]{1,0:T(8,128)(2,1)S(1)}, u32[]{:S(2)}, u32[]{:S(2)}) collective-permute-start(bf16[64,2176]{1,0:T(8,128)(2,1)} %shard_map.224.refs_0_), channel_id=1, source_target_pairs={{0,6},{2,0},{4,2},{6,4},{1,7},{3,1},{5,3},{7,5},{8,14},{10,8},{12,... | collective-permute-start | bytes 835592 | tf_op jit(solution)/shard_map/ppermute | solution.py:791
  379.2 13.0 %collective-permute-start.47 = (bf16[64,2176]{1,0:T(8,128)(2,1)S(1)}, bf16[64,2176]{1,0:T(8,128)(2,1)S(1)}, u32[]{:S(2)}, u32[]{:S(2)}) collective-permute-start(bf16[64,2176]{1,0:T(8,128)(2,1)S(1)} %collective-permute-done.41.refs_1_), channel_id=1, source_target_pairs={{0,2},{2,4},{4,6},{6,0},{1,3},{3,5},{5,7},{7,1},{8,10},{10,12},{12... | collective-permute-start | bytes 835592 | tf_op jit(solution)/shard_map/ppermute | solution.py:791
  381.0 11.3 %collective-permute-start.48 = (bf16[64,2176]{1,0:T(8,128)(2,1)S(1)}, bf16[64,2176]{1,0:T(8,128)(2,1)S(1)}, u32[]{:S(2)}, u32[]{:S(2)}) collective-permute-start(bf16[64,2176]{1,0:T(8,128)(2,1)S(1)} %collective-permute-done.41.refs_1_), channel_id=1, source_target_pairs={{0,6},{2,0},{4,2},{6,4},{1,7},{3,1},{5,3},{7,5},{8,14},{10,8},{12,... | collective-permute-start | bytes 835592 | tf_op jit(solution)/shard_map/ppermute | solution.py:791
  385.0 7.3 %collective-permute-start.49 = (bf16[64,2176]{1,0:T(8,128)(2,1)S(1)}, bf16[64,2176]{1,0:T(8,128)(2,1)S(1)}, u32[]{:S(2)}, u32[]{:S(2)}) collective-permute-start(bf16[64,2176]{1,0:T(8,128)(2,1)S(1)} %collective-permute-done.46.refs_4_), channel_id=1, source_target_pairs={{0,1},{1,0},{2,3},{3,2},{4,5},{5,4},{6,7},{7,6},{8,9},{9,8},{10,11... | collective-permute-start | bytes 835592 | tf_op jit(solution)/shard_map/ppermute | solution.py:671
  (67 other events, 341.6 us)

commit v3 on v2

--- a/solution.py
+++ b/solution.py
@@ -1056,10 +1056,11 @@
         moved=1,
         small=(first_gain[None],),
     )
+    last_share, rest_2 = tied((last_share, rest_z[2]))
     last_shares, rest_1, rest_3 = gathered(last_share, rest_1, rest_3)
     grad_tokens, vectors = last_call(last_shares, place)
     vectors = vectors.reshape(4, 2048)
-    rest_z = (rest_z[0], rest_1, z_permute(rest_z[2], 2), rest_3)
+    rest_z = (rest_z[0], rest_1, z_permute(rest_2, 2), rest_3)
     rest_keep, rest_send = xh_halves(rest_z)
     rest_w = rest_keep + swapped(rest_send, "xh").astype(WIDE)
     return (

time: 406 us -> 406 us (level)
  the two profiles are of different devices: /device:TPU:8 before, /device:TPU:0 now
where the time goes in v3:
time: 406 us; the launch traced here: 398 us
  Pallas kernels  166 us (41%)
  starting transfers between devices  110 us (27%)
  waiting for transfers between devices  89.2 us (22%)
  local copies, waits for them, and re-layouts  20.1 us (5%)
  other arithmetic  8.58 us (2%)
    pallas_call x19, Pallas kernels, kernel_call(): pl.pallas_call(run, out_shape=(*[pltpu.HBM(a.shape, a.dtype) for a in out...  152 us
    ppermute x13, starting transfers between devices, y_moved(): return lax.ppermute(x, 'y', [(i, (i + distance) % 4) for i in range(4)])  33.1 us
    all_to_all x5, waiting for transfers between devices, dealt(): return lax.all_to_all(x, axis, split_axis=0, concat_axis=0, tiled=True)  31.1 us
    ppermute x12, starting transfers between devices, across(): lax.ppermute(pieces[k], SPREAD, [(i, i ^ k) for i in range(4)])  26.7 us
    all_to_all x5, starting transfers between devices, dealt(): return lax.all_to_all(x, axis, split_axis=0, concat_axis=0, tiled=True)  21.4 us
    ppermute x12, waiting for transfers between devices, across(): lax.ppermute(pieces[k], SPREAD, [(i, i ^ k) for i in range(4)])  18.4 us
    ppermute x17, starting transfers between devices, swapped(): return lax.ppermute(x, axis, [(0, 1), (1, 0)])  14.6 us
    ppermute x13, waiting for transfers between devices, y_moved(): return lax.ppermute(x, 'y', [(i, (i + distance) % 4) for i in range(4)])  12.8 us
  transfers between devices with their start and end apart: 57, of which 28 were waited for; matrix products, arithmetic and copies ran while one was open for 4% of the time, Pallas kernels for 29%

profile of v3, /device:TPU:0, one launch (start us, length us, event | category | flops | bytes accessed | tf_op | source)
XLA Modules:
  0.0 398.5 jit_solution(14922393087174154312)
XLA Ops:
  5.6 7.9 %shard_map.203 = (bf16[512,2048]{1,0:T(8,128)(2,1)}, f32[512,128]{1,0:T(8,128)}, bf16[768,128]{1,0:T(8,128)(2,1)}, bf16[768,128]{1,0:T(8,128)(2,1)}, bf16[768,12...) custom-call(s32[5]{0:T(128)S(1)} %stack.38.refs_0_.place, ...), custom_call_target="tpu_custom_call" | custom-call | flops 1610612736 | bytes 8945664 | tf_op jit(solution)/shard_map/pallas_call | solution.py:127
  13.5 4.0 %collective-permute-start = (bf16[768,128]{1,0:T(8,128)(2,1)}, bf16[768,128]{1,0:T(8,128)(2,1)S(1)}, u32[]{:S(2)}, u32[]{:S(2)}) collective-permute-start(bf16[768,128]{1,0:T(8,128)(2,1)} %get-tuple-element.159), channel_id=1, source_target_pairs={{0,32},{32,0},{64,96},{96,64},{1,33},{33,1},{65,97},{97,65},{2,34}... | collective-permute-start | bytes 589832 | tf_op jit(solution)/shard_map/ppermute | solution.py:676
  17.5 3.0 collective-permute-start.1
  20.6 5.4 %shard_map.204.refs_11_ = f32[512,704]{1,0:T(8,128)} custom-call(bf16[512,2048]{1,0:T(8,128)(2,1)} %refs_12_.1, bf16[704,2048]{1,0:T(8,128)(2,1)} %refs_1_.3), custom_call_target="tpu_custom_call" | custom-call | flops 1476395008 | bytes 6422528 | tf_op jit(solution)/shard_map/pallas_call | solution.py:127
  33.7 13.0 %shard_map.205 = (f32[4,128,512]{2,1,0:T(8,128)}, f32[4,8,512]{2,1,0:T(8,128)}) custom-call(s32[5]{0:T(128)S(1)} %stack.38.refs_0_.place, bf16[4,512,128]{2,1,0:T(8,128)(2,1)} %copy-done.21, bf16[4,512,128]{2,1,0:T(8,128)(2,1)} %copy-done.46, bf16[768,128]{1,0:T(8,128)(2,1)} %get-tuple-element.162.refs_3_, bf16[768,128]{1,0:T(8,128)(2,1)} %copy-done.43, ...), custom_call_target="tpu_custom_call" | custom-call | flops 2684354560 | bytes 2490368 | tf_op jit(solution)/shard_map/pallas_call | solution.py:127
  49.7 14.3 %shard_map.206 = (bf16[256,128]{1,0:T(8,128)(2,1)}, bf16[256,128]{1,0:T(8,128)(2,1)}, bf16[256,128]{1,0:T(8,128)(2,1)}, bf16[256,128]{1,0:T(8,128)(2,1)}, f32[4,128,512]{2,1,0:T(8,128)}, /*index=5*/f32[4,8,512]{2,1,0:T(8,128)}) custom-call(s32[5]{0:T(128)S(1)} %stack.38.refs_0_.place, bf16[4,512,128]{2,1,0:T(8,128)(2,1)} %copy-done.47, ...), custom_call_target="tpu_custom_call" | custom-call | flops 2684354560 | bytes 3866624 | tf_op jit(solution)/shard_map/pallas_call | solution.py:127
  66.2 3.0 collective-permute-start.7
  72.2 5.4 %collective-permute-done.8.refs_4_ = bf16[256,128]{1,0:T(8,128)(2,1)S(1)} collective-permute-done((bf16[256,128]{1,0:T(8,128)(2,1)}, bf16[256,128]{1,0:T(8,128)(2,1)S(1)}, u32[]{:S(2)}, u32[]{:S(2)}) %collective-permute-start.8) | collective-permute-done | bytes 65568 | tf_op jit(solution)/shard_map/ppermute | solution.py:676
  78.2 4.2 %shard_map.207 = (bf16[512,256]{1,0:T(8,128)(2,1)}, bf16[128,2048]{1,0:T(8,128)(2,1)}, bf16[128,2048]{1,0:T(8,128)(2,1)}, bf16[64,2048]{1,0:T(8,128)(2,1)}, bf16...) custom-call(s32[5]{0:T(128)S(1)} %stack.38.refs_0_.place, ...), custom_call_target="tpu_custom_call" | custom-call | flops 536870912 | bytes 3670016 | tf_op jit(solution)/shard_map/pallas_call | solution.py:127
  86.4 6.0 %collective-permute-done.11.refs_3_ = bf16[64,2048]{1,0:T(8,128)(2,1)S(1)} collective-permute-done((bf16[64,2048]{1,0:T(8,128)(2,1)}, bf16[64,2048]{1,0:T(8,128)(2,1)S(1)}, u32[]{:S(2)}, u32[]{:S(2)}) %collective-permute-start.11) | collective-permute-done | bytes 262176 | tf_op jit(solution)/shard_map/ppermute | solution.py:671
  92.4 3.9 collective-permute-done.9.refs_1_
  97.3 3.0 shard_map.208
  103.7 3.2 collective-permute-done.12.refs_4_
  109.8 4.2 %shard_map.209 = (bf16[64,2048]{1,0:T(8,128)(2,1)}, f32[64,2048]{1,0:T(8,128)}, f32[64,2048]{1,0:T(8,128)}, f32[64,128]{1,0:T(8,128)}) custom-call(s32[5]{0:T(128)S(1)} %stack.38.refs_0_.place, bf16[128,2048]{1,0:T(8,128)(2,1)} %copy-done.8, bf16[128,2048]{1,0:T(8,128)(2,1)} %copy-done.9, bf16[64,2048]{1,0:T(8,128)(2,1)} %get-tuple-element.177.refs_3_, ...), custom_call_target="tpu_custom_call" | custom-call | bytes 3440640 | tf_op jit(solution)/shard_map/pallas_call | solution.py:127
  129.7 2.8 collective-permute-done.18.refs_6_.refs_7_
  133.9 12.7 %shard_map.210 = (bf16[512,704]{1,0:T(8,128)(2,1)}, bf16[512,704]{1,0:T(8,128)(2,1)}, bf16[512,704]{1,0:T(8,128)(2,1)}, bf16[512,2048]{1,0:T(8,128)(2,1)}) custom-call(s32[5]{0:T(128)S(1)} %stack.38.refs_0_.place, bf16[64,2048]{1,0:T(8,128)(2,1)} %get-tuple-element.184.refs_1_.refs_2_, bf16[64,2048]{1,0:T(8,128)(2,1)} %copy-done.34, ...), custom_call_target="tpu_custom_call" | custom-call | flops 5905580032 | bytes 13565952 | tf_op jit(solution)/shard_map/pallas_call | solution.py:127
  146.7 4.2 %all-to-all-start = ((bf16[8,64,2048]{2,1,0:T(8,128)(2,1)}), bf16[8,64,2048]{2,1,0:T(8,128)(2,1)S(1)}, u32[]{:S(2)}, u32[]{:S(2)}) async-start(bf16[8,64,2048]{2,1,0:T(8,128)(2,1)} %bitcast.62), calls=%async_computation | async-start | bytes 4194304 | tf_op jit(solution)/shard_map/all_to_all | solution.py:783
  150.9 12.2 %shard_map.211 = (bf16[8,2112,128]{2,1,0:T(8,128)(2,1)}, bf16[8,2112,128]{2,1,0:T(8,128)(2,1)}) custom-call(s32[5]{0:T(128)S(1)} %stack.38.refs_0_.place, bf16[512,704]{1,0:T(8,128)(2,1)} %get-tuple-element.187.refs_1_, bf16[64,2048]{1,0:T(8,128)(2,1)} %get-tuple-element.184.refs_1_.refs_2_, bf16[64,2048]{1,0:T(8,128)(2,1)} %copy-done.34, ...), custom_call_target="tpu_custom_call" | custom-call | tf_op jit(solution)/shard_map/pallas_call | solution.py:127
  163.1 11.2 %all-to-all-done.refs_0_ = bf16[8,64,2048]{2,1,0:T(8,128)(2,1)S(1)} async-done(((bf16[8,64,2048]{2,1,0:T(8,128)(2,1)}), bf16[8,64,2048]{2,1,0:T(8,128)(2,1)S(1)}, u32[]{:S(2)}, u32[]{:S(2)}) %all-to-all-start) | async-done | bytes 2097184 | tf_op jit(solution)/shard_map/all_to_all | solution.py:783
  174.3 3.7 shard_map.213
  178.0 3.6 all-to-all-start.1
  182.0 5.7 %shard_map.212 = (bf16[2,2112,128]{2,1,0:T(8,128)(2,1)}, bf16[2,2112,128]{2,1,0:T(8,128)(2,1)}, bf16[2,2112,128]{2,1,0:T(8,128)(2,1)}, bf16[2,2112,128]{2,1,0:T(8,128)(2,1)}) custom-call(s32[1]{0:T(128)} %bitcast.12.place, bf16[8,2112,128]{2,1,0:T(8,128)(2,1)} %get-tuple-element.192.mine, bf16[8,2112,128]{2,1,0:T(8,128)(2,1)} %collective-permute-done.21.received), custom_call_target="tpu_custom_call" | custom-call | tf_op jit(solution)/shard_map/pallas_call | solution.py:711
  191.2 3.1 convolution_convert_fusion
  194.3 15.2 %all-to-all-done.1 = bf16[8,64,2048]{2,1,0:T(8,128)(2,1)S(1)} async-done(((bf16[8,64,2048]{2,1,0:T(8,128)(2,1)}), bf16[8,64,2048]{2,1,0:T(8,128)(2,1)S(1)}, u32[]{:S(2)}, u32[]{:S(2)}) %all-to-all-start.1) | async-done | bytes 2097184 | tf_op jit(solution)/shard_map/all_to_all | solution.py:783
  209.5 3.5 shard_map.214
  216.2 4.4 %all-to-all-start.2 = ((bf16[4,128,2048]{2,1,0:T(8,128)(2,1)}), bf16[4,128,2048]{2,1,0:T(8,128)(2,1)S(1)}, u32[]{:S(2)}, u32[]{:S(2)}) async-start(bf16[4,128,2048]{2,1,0:T(8,128)(2,1)} %bitcast.61), calls=%async_computation.2 | async-start | bytes 4194304 | tf_op jit(solution)/shard_map/all_to_all | solution.py:783
  221.5 3.2 collective-permute-start.25
  227.2 5.6 %collective-permute-done.26.refs_10_ = bf16[256,128]{1,0:T(8,128)(2,1)S(1)} collective-permute-done((bf16[256,128]{1,0:T(8,128)(2,1)S(1)}, bf16[256,128]{1,0:T(8,128)(2,1)S(1)}, u32[]{:S(2)}, u32[]{:S(2)}) %collective-permute-start.26) | collective-permute-done | bytes 65568 | tf_op jit(solution)/shard_map/ppermute | solution.py:676
  234.3 20.3 %shard_map.215 = (f32[4,128,512]{2,1,0:T(8,128)}, bf16[4,512,128]{2,1,0:T(8,128)(2,1)}, bf16[4,512,128]{2,1,0:T(8,128)(2,1)}) custom-call(s32[5]{0:T(128)S(1)} %stack.38.refs_0_.place, bf16[4,512,128]{2,1,0:T(8,128)(2,1)} %copy-done.47, bf16[4,512,128]{2,1,0:T(8,128)(2,1)} %copy-done.48, bf16[768,128]{1,0:T(8,128)(2,1)} %get-tuple-element.162.refs_3_, ...), custom_call_target="tpu_custom_call" | custom-call | flops 6710886400 | bytes 4849664 | tf_op jit(solution)/shard_map/pallas_call | solution.py:127
  254.6 2.9 collective-permute-done.27
  257.5 2.9 shard_map.216.refs_0_
  263.0 21.2 %shard_map.217 = (bf16[256,128]{1,0:T(8,128)(2,1)}, bf16[256,128]{1,0:T(8,128)(2,1)}, bf16[256,128]{1,0:T(8,128)(2,1)}, bf16[256,128]{1,0:T(8,128)(2,1)}, bf16[4...) custom-call(s32[5]{0:T(128)S(1)} %stack.38.refs_0_.place, bf16[4,512,128]{2,1,0:T(8,128)(2,1)} %copy-done.21, ...), custom_call_target="tpu_custom_call" | custom-call | flops 6710886400 | bytes 5111808 | tf_op jit(solution)/shard_map/pallas_call | solution.py:127
  292.4 2.8 collective-permute-start.33
  297.7 4.6 %all-to-all-start.3 = ((bf16[4,128,2048]{2,1,0:T(8,128)(2,1)}), bf16[4,128,2048]{2,1,0:T(8,128)(2,1)S(1)}, u32[]{:S(2)}, u32[]{:S(2)}) async-start(bf16[4,128,2048]{2,1,0:T(8,128)(2,1)} %shard_map.219), calls=%async_computation.3 | async-start | bytes 4194304 | tf_op jit(solution)/shard_map/all_to_all | solution.py:783
  304.0 2.9 collective-permute-done.34.refs_4_
  309.3 7.0 %shard_map.220 = (bf16[512,768]{1,0:T(8,128)(2,1)}, bf16[512,2048]{1,0:T(8,128)(2,1)}, f32[1,2048]{1,0:T(1,128)S(1)}, f32[1,2048]{1,0:T(1,128)S(1)}, f32[3,256]{1,0:T(4,128)S(1)}) custom-call(s32[5]{0:T(128)S(1)} %stack.38.refs_0_.place, bf16[768,128]{1,0:T(8,128)(2,1)} %get-tuple-element.260.refs_1_, bf16[768,128]{1,0:T(8,128)(2,1)} %copy-done.41, ...), custom_call_target="tpu_custom_call" | custom-call | flops 1610612736 | bytes 9699328 | tf_op jit(solution)/shard_map/pallas_call | solution.py:127
  316.3 7.8 %shard_map.221 = (bf16[8,1024,128]{2,1,0:T(8,128)(2,1)}, bf16[8,1024,128]{2,1,0:T(8,128)(2,1)}) custom-call(s32[5]{0:T(128)S(1)} %stack.38.refs_0_.place, bf16[512,768]{1,0:T(8,128)(2,1)} %get-tuple-element.274.refs_1_, bf16[512,2048]{1,0:T(8,128)(2,1)} %get-tuple-element.275.refs_2_, bf16[512,256]{1,0:T(8,128)(2,1)} %get-tuple-element.276.refs_3_, ...), custom_call_target="tpu_custom_call" | custom-call | tf_op jit(solution)/shard_map/pallas_call | solution.py:127
  324.8 3.3 all-to-all-done.3.x
  328.2 4.6 %all-to-all-start.4 = ((bf16[8,64,2048]{2,1,0:T(8,128)(2,1)}), bf16[8,64,2048]{2,1,0:T(8,128)(2,1)}, u32[]{:S(2)}, u32[]{:S(2)}) async-start(bf16[8,64,2048]{2,1,0:T(8,128)(2,1)} %bitcast.60), calls=%async_computation.4 | async-start | bytes 4194304 | tf_op jit(solution)/shard_map/all_to_all | solution.py:783
  335.1 3.0 collective-permute-done.36
  340.7 2.9 collective-permute-done.37
  343.7 3.5 shard_map.222
  359.4 3.4 shard_map.224.refs_0_
  364.7 3.0 collective-permute-start.46
  367.7 8.4 %collective-permute-start.44 = (bf16[64,2176]{1,0:T(8,128)(2,1)}, bf16[64,2176]{1,0:T(8,128)(2,1)S(1)}, u32[]{:S(2)}, u32[]{:S(2)}) collective-permute-start(bf16[64,2176]{1,0:T(8,128)(2,1)} %shard_map.224.refs_0_), channel_id=1, source_target_pairs={{0,2},{2,4},{4,6},{6,0},{1,3},{3,5},{5,7},{7,1},{8,10},{10,12},{12... | collective-permute-start | bytes 835592 | tf_op jit(solution)/shard_map/ppermute | solution.py:791
  376.6 3.2 collective-permute-start.45
  379.9 3.2 collective-permute-start.48
  391.6 2.9 shard_map.225
  (248 shorter events, 110.7 us)
Async XLA Ops:
  13.5 14.5 %collective-permute-start = (bf16[768,128]{1,0:T(8,128)(2,1)}, bf16[768,128]{1,0:T(8,128)(2,1)S(1)}, u32[]{:S(2)}, u32[]{:S(2)}) collective-permute-start(bf16[768,128]{1,0:T(8,128)(2,1)} %get-tuple-element.159), channel_id=1, source_target_pairs={{0,32},{32,0},{64,96},{96,64},{1,33},{33,1},{65,97},{97,65},{2,34}... | collective-permute-start | bytes 589832 | tf_op jit(solution)/shard_map/ppermute | solution.py:676
  17.5 10.5 %collective-permute-start.1 = (bf16[768,128]{1,0:T(8,128)(2,1)}, bf16[768,128]{1,0:T(8,128)(2,1)S(1)}, u32[]{:S(2)}, u32[]{:S(2)}) collective-permute-start(bf16[768,128]{1,0:T(8,128)(2,1)} %get-tuple-element.160), channel_id=1, source_target_pairs={{0,64},{32,96},{64,0},{96,32},{1,65},{33,97},{65,1},{97,33},{2,66}... | collective-permute-start | bytes 589832 | tf_op jit(solution)/shard_map/ppermute | solution.py:676
  20.6 10.2 %collective-permute-start.2 = (bf16[768,128]{1,0:T(8,128)(2,1)}, bf16[768,128]{1,0:T(8,128)(2,1)S(1)}, u32[]{:S(2)}, u32[]{:S(2)}) collective-permute-start(bf16[768,128]{1,0:T(8,128)(2,1)} %get-tuple-element.161), channel_id=1, source_target_pairs={{0,96},{32,64},{64,32},{96,0},{1,97},{33,65},{65,33},{97,1},{2,98}... | collective-permute-start | bytes 589832 | tf_op jit(solution)/shard_map/ppermute | solution.py:676
  31.0 15.7 %collective-permute-start.4 = (bf16[4,512,128]{2,1,0:T(8,128)(2,1)S(1)}, bf16[4,512,128]{2,1,0:T(8,128)(2,1)S(1)}, u32[]{:S(2)}, u32[]{:S(2)}) collective-permute-start(bf16[4,512,128]{2,1,0:T(8,128)(2,1)S(1)} %pad_maximum_fusion.refs_1_), channel_id=1, source_target_pairs={{0,16},{16,0},{1,17},{17,1},{2,18},{18,2},{3,19},{19,3},{4,20},{20... | collective-permute-start | bytes 1572872 | tf_op jit(solution)/shard_map/ppermute | solution.py:671
  64.1 6.6 %collective-permute-start.6 = (bf16[256,128]{1,0:T(8,128)(2,1)}, bf16[256,128]{1,0:T(8,128)(2,1)S(1)}, u32[]{:S(2)}, u32[]{:S(2)}) collective-permute-start(bf16[256,128]{1,0:T(8,128)(2,1)} %get-tuple-element.172), channel_id=1, source_target_pairs={{0,32},{32,0},{64,96},{96,64},{1,33},{33,1},{65,97},{97,65},{2,34}... | collective-permute-start | bytes 196616 | tf_op jit(solution)/shard_map/ppermute | solution.py:676
  69.2 8.4 %collective-permute-start.8 = (bf16[256,128]{1,0:T(8,128)(2,1)}, bf16[256,128]{1,0:T(8,128)(2,1)S(1)}, u32[]{:S(2)}, u32[]{:S(2)}) collective-permute-start(bf16[256,128]{1,0:T(8,128)(2,1)} %get-tuple-element.174), channel_id=1, source_target_pairs={{0,96},{32,64},{64,32},{96,0},{1,97},{33,65},{65,33},{97,1},{2,98}... | collective-permute-start | bytes 196616 | tf_op jit(solution)/shard_map/ppermute | solution.py:676
  82.5 13.8 %collective-permute-start.9 = (bf16[128,2048]{1,0:T(8,128)(2,1)}, bf16[128,2048]{1,0:T(8,128)(2,1)S(1)}, u32[]{:S(2)}, u32[]{:S(2)}) collective-permute-start(bf16[128,2048]{1,0:T(8,128)(2,1)} %get-tuple-element.175), channel_id=1, source_target_pairs={{0,2},{2,4},{4,6},{6,0},{1,3},{3,5},{5,7},{7,1},{8,10},{10,12},{12... | collective-permute-start | bytes 1572872 | tf_op jit(solution)/shard_map/ppermute | solution.py:791
  84.1 12.2 %collective-permute-start.10 = (bf16[128,2048]{1,0:T(8,128)(2,1)}, bf16[128,2048]{1,0:T(8,128)(2,1)S(1)}, u32[]{:S(2)}, u32[]{:S(2)}) collective-permute-start(bf16[128,2048]{1,0:T(8,128)(2,1)} %get-tuple-element.176), channel_id=1, source_target_pairs={{0,6},{2,0},{4,2},{6,4},{1,7},{3,1},{5,3},{7,5},{8,14},{10,8},{12,... | collective-permute-start | bytes 1572872 | tf_op jit(solution)/shard_map/ppermute | solution.py:791
  85.8 6.6 %collective-permute-start.11 = (bf16[64,2048]{1,0:T(8,128)(2,1)}, bf16[64,2048]{1,0:T(8,128)(2,1)S(1)}, u32[]{:S(2)}, u32[]{:S(2)}) collective-permute-start(bf16[64,2048]{1,0:T(8,128)(2,1)} %get-tuple-element.178), channel_id=1, source_target_pairs={{0,1},{1,0},{2,3},{3,2},{4,5},{5,4},{6,7},{7,6},{8,9},{9,8},{10,11... | collective-permute-start | bytes 786440 | tf_op jit(solution)/shard_map/ppermute | solution.py:671
  100.3 6.7 %collective-permute-start.12 = (bf16[64,2048]{1,0:T(8,128)(2,1)}, bf16[64,2048]{1,0:T(8,128)(2,1)S(1)}, u32[]{:S(2)}, u32[]{:S(2)}) collective-permute-start(bf16[64,2048]{1,0:T(8,128)(2,1)} %get-tuple-element.181), channel_id=1, source_target_pairs={{0,1},{1,0},{2,3},{3,2},{4,5},{5,4},{6,7},{7,6},{8,9},{9,8},{10,11... | collective-permute-start | bytes 786440 | tf_op jit(solution)/shard_map/ppermute | solution.py:671
  100.9 8.1 %collective-permute-start.13 = (bf16[64,2048]{1,0:T(8,128)(2,1)}, bf16[64,2048]{1,0:T(8,128)(2,1)S(1)}, u32[]{:S(2)}, u32[]{:S(2)}) collective-permute-start(bf16[64,2048]{1,0:T(8,128)(2,1)} %get-tuple-element.182), channel_id=1, source_target_pairs={{0,4},{2,6},{4,0},{6,2},{1,5},{3,7},{5,1},{7,3},{8,12},{10,14},{12... | collective-permute-start | bytes 786440 | tf_op jit(solution)/shard_map/ppermute | solution.py:791
  114.0 7.5 %collective-permute-start.14 = (bf16[64,2048]{1,0:T(8,128)(2,1)}, bf16[64,2048]{1,0:T(8,128)(2,1)S(1)}, u32[]{:S(2)}, u32[]{:S(2)}) collective-permute-start(bf16[64,2048]{1,0:T(8,128)(2,1)} %get-tuple-element.184.refs_1_.refs_2_), channel_id=1, source_target_pairs={{0,1},{1,0},{2,3},{3,2},{4,5},{5,4},{6,7},{7,6},{8,9},{9,8},{10,11... | collective-permute-start | bytes 786440 | tf_op jit(solution)/shard_map/ppermute | solution.py:671
  115.5 11.0 %collective-permute-start.17 = (bf16[64,2048]{1,0:T(8,128)(2,1)}, bf16[64,2048]{1,0:T(8,128)(2,1)S(1)}, u32[]{:S(2)}, u32[]{:S(2)}) collective-permute-start(bf16[64,2048]{1,0:T(8,128)(2,1)} %get-tuple-element.184.refs_1_.refs_2_), channel_id=1, source_target_pairs={{0,4},{2,6},{4,0},{6,2},{1,5},{3,7},{5,1},{7,3},{8,12},{10,14},{12... | collective-permute-start | bytes 786440 | tf_op jit(solution)/shard_map/ppermute | solution.py:791
  118.3 11.4 %collective-permute-start.15 = (bf16[64,2048]{1,0:T(8,128)(2,1)}, bf16[64,2048]{1,0:T(8,128)(2,1)S(1)}, u32[]{:S(2)}, u32[]{:S(2)}) collective-permute-start(bf16[64,2048]{1,0:T(8,128)(2,1)} %get-tuple-element.184.refs_1_.refs_2_), channel_id=1, source_target_pairs={{0,2},{2,4},{4,6},{6,0},{1,3},{3,5},{5,7},{7,1},{8,10},{10,12},{12... | collective-permute-start | bytes 786440 | tf_op jit(solution)/shard_map/ppermute | solution.py:791
  119.2 10.5 %collective-permute-start.16 = (bf16[64,2048]{1,0:T(8,128)(2,1)}, bf16[64,2048]{1,0:T(8,128)(2,1)S(1)}, u32[]{:S(2)}, u32[]{:S(2)}) collective-permute-start(bf16[64,2048]{1,0:T(8,128)(2,1)} %get-tuple-element.184.refs_1_.refs_2_), channel_id=1, source_target_pairs={{0,6},{2,0},{4,2},{6,4},{1,7},{3,1},{5,3},{7,5},{8,14},{10,8},{12,... | collective-permute-start | bytes 786440 | tf_op jit(solution)/shard_map/ppermute | solution.py:791
  121.5 11.0 %collective-permute-start.18 = (bf16[64,2048]{1,0:T(8,128)(2,1)S(1)}, bf16[64,2048]{1,0:T(8,128)(2,1)S(1)}, u32[]{:S(2)}, u32[]{:S(2)}) collective-permute-start(bf16[64,2048]{1,0:T(8,128)(2,1)S(1)} %collective-permute-done.14.refs_2_.refs_3_), channel_id=1, source_target_pairs={{0,2},{2,4},{4,6},{6,0},{1,3},{3,5},{5,7},{7,1},{8,10},{10,12},{12... | collective-permute-start | bytes 786440 | tf_op jit(solution)/shard_map/ppermute | solution.py:791
  122.1 10.4 %collective-permute-start.19 = (bf16[64,2048]{1,0:T(8,128)(2,1)S(1)}, bf16[64,2048]{1,0:T(8,128)(2,1)S(1)}, u32[]{:S(2)}, u32[]{:S(2)}) collective-permute-start(bf16[64,2048]{1,0:T(8,128)(2,1)S(1)} %collective-permute-done.14.refs_2_.refs_3_), channel_id=1, source_target_pairs={{0,6},{2,0},{4,2},{6,4},{1,7},{3,1},{5,3},{7,5},{8,14},{10,8},{12,... | collective-permute-start | bytes 786440 | tf_op jit(solution)/shard_map/ppermute | solution.py:791
  126.5 6.8 %collective-permute-start.20 = (bf16[64,2048]{1,0:T(8,128)(2,1)S(1)}, bf16[64,2048]{1,0:T(8,128)(2,1)S(1)}, u32[]{:S(2)}, u32[]{:S(2)}) collective-permute-start(bf16[64,2048]{1,0:T(8,128)(2,1)S(1)} %collective-permute-done.17.refs_5_.refs_6_), channel_id=1, source_target_pairs={{0,1},{1,0},{2,3},{3,2},{4,5},{5,4},{6,7},{7,6},{8,9},{9,8},{10,11... | collective-permute-start | bytes 786440 | tf_op jit(solution)/shard_map/ppermute | solution.py:671
  146.7 27.6 %all-to-all-start = ((bf16[8,64,2048]{2,1,0:T(8,128)(2,1)}), bf16[8,64,2048]{2,1,0:T(8,128)(2,1)S(1)}, u32[]{:S(2)}, u32[]{:S(2)}) async-start(bf16[8,64,2048]{2,1,0:T(8,128)(2,1)} %bitcast.62), calls=%async_computation | async-start | bytes 4194304 | tf_op jit(solution)/shard_map/all_to_all | solution.py:783
  174.3 7.7 %collective-permute-start.21 = (bf16[8,2112,128]{2,1,0:T(8,128)(2,1)}, bf16[8,2112,128]{2,1,0:T(8,128)(2,1)}, u32[]{:S(2)}, u32[]{:S(2)}) collective-permute-start(bf16[8,2112,128]{2,1,0:T(8,128)(2,1)} %get-tuple-element.193), channel_id=1, source_target_pairs={{0,8},{8,0},{1,9},{9,1},{2,10},{10,2},{3,11},{11,3},{4,12},{12,4},... | collective-permute-start | bytes 12976136 | tf_op jit(solution)/shard_map/ppermute | solution.py:671
  178.0 31.5 %all-to-all-start.1 = ((bf16[8,64,2048]{2,1,0:T(8,128)(2,1)}), bf16[8,64,2048]{2,1,0:T(8,128)(2,1)S(1)}, u32[]{:S(2)}, u32[]{:S(2)}) async-start(bf16[8,64,2048]{2,1,0:T(8,128)(2,1)} %get-tuple-element.200), calls=%async_computation.1 | async-start | bytes 4194304 | tf_op jit(solution)/shard_map/all_to_all | solution.py:783
  187.7 27.5 %collective-permute-start.22 = (bf16[2,2112,128]{2,1,0:T(8,128)(2,1)}, bf16[2,2112,128]{2,1,0:T(8,128)(2,1)S(1)}, u32[]{:S(2)}, u32[]{:S(2)}) collective-permute-start(bf16[2,2112,128]{2,1,0:T(8,128)(2,1)} %get-tuple-element.194), channel_id=1, source_target_pairs={{0,16},{16,32},{32,48},{48,0},{1,17},{17,33},{33,49},{49,1},{2,18}... | collective-permute-start | bytes 3244040 | tf_op jit(solution)/shard_map/ppermute | solution.py:770
  188.8 26.4 %collective-permute-start.23 = (bf16[2,2112,128]{2,1,0:T(8,128)(2,1)}, bf16[2,2112,128]{2,1,0:T(8,128)(2,1)}, u32[]{:S(2)}, u32[]{:S(2)}) collective-permute-start(bf16[2,2112,128]{2,1,0:T(8,128)(2,1)} %get-tuple-element.195), channel_id=1, source_target_pairs={{0,48},{16,0},{32,16},{48,32},{1,49},{17,1},{33,17},{49,33},{2,50}... | collective-permute-start | bytes 3244040 | tf_op jit(solution)/shard_map/ppermute | solution.py:770
  216.2 41.3 %all-to-all-start.2 = ((bf16[4,128,2048]{2,1,0:T(8,128)(2,1)}), bf16[4,128,2048]{2,1,0:T(8,128)(2,1)S(1)}, u32[]{:S(2)}, u32[]{:S(2)}) async-start(bf16[4,128,2048]{2,1,0:T(8,128)(2,1)} %bitcast.61), calls=%async_computation.2 | async-start | bytes 4194304 | tf_op jit(solution)/shard_map/all_to_all | solution.py:783
  220.6 6.5 %collective-permute-start.24 = (bf16[256,128]{1,0:T(8,128)(2,1)S(1)}, bf16[256,128]{1,0:T(8,128)(2,1)S(1)}, u32[]{:S(2)}, u32[]{:S(2)}) collective-permute-start(bf16[256,128]{1,0:T(8,128)(2,1)S(1)} %copy-done.56), channel_id=1, source_target_pairs={{0,32},{32,0},{64,96},{96,64},{1,33},{33,1},{65,97},{97,65},{2,34}... | collective-permute-start | bytes 196616 | tf_op jit(solution)/shard_map/ppermute | solution.py:676
  224.6 8.2 %collective-permute-start.26 = (bf16[256,128]{1,0:T(8,128)(2,1)S(1)}, bf16[256,128]{1,0:T(8,128)(2,1)S(1)}, u32[]{:S(2)}, u32[]{:S(2)}) collective-permute-start(bf16[256,128]{1,0:T(8,128)(2,1)S(1)} %copy-done.53), channel_id=1, source_target_pairs={{0,96},{32,64},{64,32},{96,0},{1,97},{33,65},{65,33},{97,1},{2,98}... | collective-permute-start | bytes 196616 | tf_op jit(solution)/shard_map/ppermute | solution.py:676
  232.8 24.7 %collective-permute-start.27 = (bf16[2,2112,128]{2,1,0:T(8,128)(2,1)}, bf16[2,2112,128]{2,1,0:T(8,128)(2,1)}, u32[]{:S(2)}, u32[]{:S(2)}) collective-permute-start(bf16[2,2112,128]{2,1,0:T(8,128)(2,1)} %get-tuple-element.221), channel_id=1, source_target_pairs={{0,32},{16,48},{32,0},{48,16},{1,33},{17,49},{33,1},{49,17},{2,34}... | collective-permute-start | bytes 3244040 | tf_op jit(solution)/shard_map/ppermute | solution.py:770
  260.6 23.6 %collective-permute-start.29 = (bf16[4,512,128]{2,1,0:T(8,128)(2,1)S(1)}, bf16[4,512,128]{2,1,0:T(8,128)(2,1)S(1)}, u32[]{:S(2)}, u32[]{:S(2)}) collective-permute-start(bf16[4,512,128]{2,1,0:T(8,128)(2,1)S(1)} %add_convert_fusion.1), channel_id=1, source_target_pairs={{0,16},{16,0},{1,17},{17,1},{2,18},{18,2},{3,19},{19,3},{4,20},{20... | collective-permute-start | bytes 1572872 | tf_op jit(solution)/shard_map/ppermute | solution.py:671
  261.8 22.4 %collective-permute-start.30 = (bf16[128,2048]{1,0:T(8,128)(2,1)S(1)}, bf16[128,2048]{1,0:T(8,128)(2,1)S(1)}, u32[]{:S(2)}, u32[]{:S(2)}) collective-permute-start(bf16[128,2048]{1,0:T(8,128)(2,1)S(1)} %copy-done.10), channel_id=1, source_target_pairs={{0,1},{1,0},{2,3},{3,2},{4,5},{5,4},{6,7},{7,6},{8,9},{9,8},{10,11... | collective-permute-start | bytes 1572872 | tf_op jit(solution)/shard_map/ppermute | solution.py:671
  291.1 12.9 %collective-permute-start.32 = (bf16[768,128]{1,0:T(8,128)(2,1)}, bf16[768,128]{1,0:T(8,128)(2,1)S(1)}, u32[]{:S(2)}, u32[]{:S(2)}) collective-permute-start(bf16[768,128]{1,0:T(8,128)(2,1)} %get-tuple-element.253), channel_id=1, source_target_pairs={{0,32},{32,0},{64,96},{96,64},{1,33},{33,1},{65,97},{97,65},{2,34}... | collective-permute-start | bytes 589832 | tf_op jit(solution)/shard_map/ppermute | solution.py:676
  292.4 11.5 %collective-permute-start.33 = (bf16[768,128]{1,0:T(8,128)(2,1)}, bf16[768,128]{1,0:T(8,128)(2,1)}, u32[]{:S(2)}, u32[]{:S(2)}) collective-permute-start(bf16[768,128]{1,0:T(8,128)(2,1)} %get-tuple-element.254), channel_id=1, source_target_pairs={{0,64},{32,96},{64,0},{96,32},{1,65},{33,97},{65,1},{97,33},{2,66}... | collective-permute-start | bytes 589832 | tf_op jit(solution)/shard_map/ppermute | solution.py:676
  295.3 11.7 %collective-permute-start.34 = (bf16[768,128]{1,0:T(8,128)(2,1)}, bf16[768,128]{1,0:T(8,128)(2,1)}, u32[]{:S(2)}, u32[]{:S(2)}) collective-permute-start(bf16[768,128]{1,0:T(8,128)(2,1)} %get-tuple-element.255), channel_id=1, source_target_pairs={{0,96},{32,64},{64,32},{96,0},{1,97},{33,65},{65,33},{97,1},{2,98}... | collective-permute-start | bytes 589832 | tf_op jit(solution)/shard_map/ppermute | solution.py:676
  297.7 30.5 %all-to-all-start.3 = ((bf16[4,128,2048]{2,1,0:T(8,128)(2,1)}), bf16[4,128,2048]{2,1,0:T(8,128)(2,1)S(1)}, u32[]{:S(2)}, u32[]{:S(2)}) async-start(bf16[4,128,2048]{2,1,0:T(8,128)(2,1)} %shard_map.219), calls=%async_computation.3 | async-start | bytes 4194304 | tf_op jit(solution)/shard_map/all_to_all | solution.py:783
  306.9 17.1 %collective-permute-start.38 = (bf16[2112,128]{1,0:T(8,128)(2,1)S(1)}, bf16[2112,128]{1,0:T(8,128)(2,1)S(1)}, u32[]{:S(2)}, u32[]{:S(2)}) collective-permute-start(bf16[2112,128]{1,0:T(8,128)(2,1)S(1)} %fusion), channel_id=1, source_target_pairs={{0,64},{64,0},{1,65},{65,1},{2,66},{66,2},{3,67},{67,3},{4,68},{68... | collective-permute-start | bytes 1622024 | tf_op jit(solution)/shard_map/ppermute | solution.py:671
  324.8 18.9 %collective-permute-start.39 = (bf16[8,1024,128]{2,1,0:T(8,128)(2,1)}, bf16[8,1024,128]{2,1,0:T(8,128)(2,1)}, u32[]{:S(2)}, u32[]{:S(2)}) collective-permute-start(bf16[8,1024,128]{2,1,0:T(8,128)(2,1)} %get-tuple-element.281), channel_id=1, source_target_pairs={{0,8},{8,0},{1,9},{9,1},{2,10},{10,2},{3,11},{11,3},{4,12},{12,4},... | collective-permute-start | bytes 6291464 | tf_op jit(solution)/shard_map/ppermute | solution.py:671
  328.2 30.6 %all-to-all-start.4 = ((bf16[8,64,2048]{2,1,0:T(8,128)(2,1)}), bf16[8,64,2048]{2,1,0:T(8,128)(2,1)}, u32[]{:S(2)}, u32[]{:S(2)}) async-start(bf16[8,64,2048]{2,1,0:T(8,128)(2,1)} %bitcast.60), calls=%async_computation.4 | async-start | bytes 4194304 | tf_op jit(solution)/shard_map/all_to_all | solution.py:783
  347.3 10.1 %collective-permute-start.40 = (f32[35,256]{1,0:T(8,128)S(1)}, f32[35,256]{1,0:T(8,128)S(1)}, u32[]{:S(2)}, u32[]{:S(2)}) collective-permute-start(f32[35,256]{1,0:T(8,128)S(1)} %add.157), channel_id=1, source_target_pairs={{0,64},{64,0},{1,65},{65,1},{2,66},{66,2},{3,67},{67,3},{4,68},{68... | collective-permute-start | bytes 107528 | tf_op jit(solution)/shard_map/ppermute | solution.py:806
  349.6 18.1 %collective-permute-start.42 = (bf16[2,1024,128]{2,1,0:T(8,128)(2,1)}, bf16[2,1024,128]{2,1,0:T(8,128)(2,1)}, u32[]{:S(2)}, u32[]{:S(2)}) collective-permute-start(bf16[2,1024,128]{2,1,0:T(8,128)(2,1)} %get-tuple-element.295), channel_id=1, source_target_pairs={{0,16},{16,32},{32,48},{48,0},{1,17},{17,33},{33,49},{49,1},{2,18}... | collective-permute-start | bytes 1572872 | tf_op jit(solution)/shard_map/ppermute | solution.py:770
  353.8 22.9 %collective-permute-start.43 = (bf16[2,1024,128]{2,1,0:T(8,128)(2,1)}, bf16[2,1024,128]{2,1,0:T(8,128)(2,1)}, u32[]{:S(2)}, u32[]{:S(2)}) collective-permute-start(bf16[2,1024,128]{2,1,0:T(8,128)(2,1)} %get-tuple-element.296), channel_id=1, source_target_pairs={{0,48},{16,0},{32,16},{48,32},{1,49},{17,1},{33,17},{49,33},{2,50}... | collective-permute-start | bytes 1572872 | tf_op jit(solution)/shard_map/ppermute | solution.py:770
  362.8 20.3 %collective-permute-start.50 = (bf16[2,1024,128]{2,1,0:T(8,128)(2,1)S(1)}, bf16[2,1024,128]{2,1,0:T(8,128)(2,1)S(1)}, u32[]{:S(2)}, u32[]{:S(2)}) collective-permute-start(bf16[2,1024,128]{2,1,0:T(8,128)(2,1)S(1)} %copy-done.49), channel_id=1, source_target_pairs={{0,32},{16,48},{32,0},{48,16},{1,33},{17,49},{33,1},{49,17},{2,34}... | collective-permute-start | bytes 1572872 | tf_op jit(solution)/shard_map/ppermute | solution.py:770
  364.0 15.8 %collective-permute-start.41 = (bf16[64,2176]{1,0:T(8,128)(2,1)}, bf16[64,2176]{1,0:T(8,128)(2,1)S(1)}, u32[]{:S(2)}, u32[]{:S(2)}) collective-permute-start(bf16[64,2176]{1,0:T(8,128)(2,1)} %shard_map.224.refs_0_), channel_id=1, source_target_pairs={{0,1},{1,0},{2,3},{3,2},{4,5},{5,4},{6,7},{7,6},{8,9},{9,8},{10,11... | collective-permute-start | bytes 835592 | tf_op jit(solution)/shard_map/ppermute | solution.py:671
  364.7 15.1 %collective-permute-start.46 = (bf16[64,2176]{1,0:T(8,128)(2,1)}, bf16[64,2176]{1,0:T(8,128)(2,1)S(1)}, u32[]{:S(2)}, u32[]{:S(2)}) collective-permute-start(bf16[64,2176]{1,0:T(8,128)(2,1)} %shard_map.224.refs_0_), channel_id=1, source_target_pairs={{0,4},{2,6},{4,0},{6,2},{1,5},{3,7},{5,1},{7,3},{8,12},{10,14},{12... | collective-permute-start | bytes 835592 | tf_op jit(solution)/shard_map/ppermute | solution.py:791
  367.7 17.4 %collective-permute-start.44 = (bf16[64,2176]{1,0:T(8,128)(2,1)}, bf16[64,2176]{1,0:T(8,128)(2,1)S(1)}, u32[]{:S(2)}, u32[]{:S(2)}) collective-permute-start(bf16[64,2176]{1,0:T(8,128)(2,1)} %shard_map.224.refs_0_), channel_id=1, source_target_pairs={{0,2},{2,4},{4,6},{6,0},{1,3},{3,5},{5,7},{7,1},{8,10},{10,12},{12... | collective-permute-start | bytes 835592 | tf_op jit(solution)/shard_map/ppermute | solution.py:791
  376.6 13.4 %collective-permute-start.45 = (bf16[64,2176]{1,0:T(8,128)(2,1)}, bf16[64,2176]{1,0:T(8,128)(2,1)S(1)}, u32[]{:S(2)}, u32[]{:S(2)}) collective-permute-start(bf16[64,2176]{1,0:T(8,128)(2,1)} %shard_map.224.refs_0_), channel_id=1, source_target_pairs={{0,6},{2,0},{4,2},{6,4},{1,7},{3,1},{5,3},{7,5},{8,14},{10,8},{12,... | collective-permute-start | bytes 835592 | tf_op jit(solution)/shard_map/ppermute | solution.py:791
  379.8 10.2 %collective-permute-start.47 = (bf16[64,2176]{1,0:T(8,128)(2,1)S(1)}, bf16[64,2176]{1,0:T(8,128)(2,1)S(1)}, u32[]{:S(2)}, u32[]{:S(2)}) collective-permute-start(bf16[64,2176]{1,0:T(8,128)(2,1)S(1)} %collective-permute-done.41.refs_1_), channel_id=1, source_target_pairs={{0,2},{2,4},{4,6},{6,0},{1,3},{3,5},{5,7},{7,1},{8,10},{10,12},{12... | collective-permute-start | bytes 835592 | tf_op jit(solution)/shard_map/ppermute | solution.py:791
  379.9 10.2 %collective-permute-start.48 = (bf16[64,2176]{1,0:T(8,128)(2,1)S(1)}, bf16[64,2176]{1,0:T(8,128)(2,1)S(1)}, u32[]{:S(2)}, u32[]{:S(2)}) collective-permute-start(bf16[64,2176]{1,0:T(8,128)(2,1)S(1)} %collective-permute-done.41.refs_1_), channel_id=1, source_target_pairs={{0,6},{2,0},{4,2},{6,4},{1,7},{3,1},{5,3},{7,5},{8,14},{10,8},{12,... | collective-permute-start | bytes 835592 | tf_op jit(solution)/shard_map/ppermute | solution.py:791
  383.1 7.0 %collective-permute-start.49 = (bf16[64,2176]{1,0:T(8,128)(2,1)S(1)}, bf16[64,2176]{1,0:T(8,128)(2,1)S(1)}, u32[]{:S(2)}, u32[]{:S(2)}) collective-permute-start(bf16[64,2176]{1,0:T(8,128)(2,1)S(1)} %collective-permute-done.46.refs_4_), channel_id=1, source_target_pairs={{0,1},{1,0},{2,3},{3,2},{4,5},{5,4},{6,7},{7,6},{8,9},{9,8},{10,11... | collective-permute-start | bytes 835592 | tf_op jit(solution)/shard_map/ppermute | solution.py:671
  385.2 10.0 %collective-permute-start.51 = (bf16[1024,128]{1,0:T(8,128)(2,1)S(1)}, bf16[1024,128]{1,0:T(8,128)(2,1)S(1)}, u32[]{:S(2)}, u32[]{:S(2)}) collective-permute-start(bf16[1024,128]{1,0:T(8,128)(2,1)S(1)} %fusion.1), channel_id=1, source_target_pairs={{0,64},{64,0},{1,65},{65,1},{2,66},{66,2},{3,67},{67,3},{4,68},{68... | collective-permute-start | bytes 786440 | tf_op jit(solution)/shard_map/ppermute | solution.py:671
  (68 other events, 344.0 us)

commit v4 on v2

--- a/solution.py
+++ b/solution.py
@@ -643,7 +643,7 @@
             theirs[n, at, :] = jnp.where(first_core, second, first).astype(LOW)
             return carry
 
-        lax.fori_loop(0, 8, one, 0, unroll=4)
+        lax.fori_loop(0, 8, one, 0, unroll=8)
         start += width
 
 
@@ -982,7 +982,7 @@
         exps=20 * BLOCK * BLOCK,
         mib=28,
     )
-    acc, send1, feed_parts, feed_2 = tied((acc, send1, feed_parts, feed_2))
+    acc, send1, feed_parts = tied((acc, send1, feed_parts))
     (feed_half,) = kernel_call(
         feed_sum_kernel,
         (shape_of(128, 2048),),
@@ -991,7 +991,7 @@
         moved=1,
     )
     far = (keep1.astype(WIDE) + swapped(send1, "core").astype(WIDE)).astype(LOW)
-    acc, far, feed_half = tied((acc, far, feed_half))
+    acc, far, feed_half, feed_2 = tied((acc, far, feed_half, feed_2))
     near = kernel_call(
         functools.partial(backward_kernel, (0, 1), False),
         (*[quarter] * 4, blocks, blocks),

time: 406 us -> 403 us (level)
    unnamed x118 -> x120, local copies, waits for them, and re-layouts: 10.8 us -> 11.3 us
  transfers between devices with their start and end apart: 57 -> 57, of which waited for: 31 -> 31; matrix products, arithmetic and copies ran while one was open for 4% -> 4% of each run, Pallas kernels for 29% -> 28%
where the time goes in v4:
time: 403 us; the launch traced here: 395 us
  Pallas kernels  164 us (41%)
  starting transfers between devices  99.1 us (25%)
  waiting for transfers between devices  98.2 us (24%)
  local copies, waits for them, and re-layouts  20.6 us (5%)
  other arithmetic  8.57 us (2%)
    pallas_call x19, Pallas kernels, kernel_call(): pl.pallas_call(run, out_shape=(*[pltpu.HBM(a.shape, a.dtype) for a in out...  150 us
    ppermute x12, starting transfers between devices, across(): lax.ppermute(pieces[k], SPREAD, [(i, i ^ k) for i in range(4)])  26.7 us
    all_to_all x5, waiting for transfers between devices, dealt(): return lax.all_to_all(x, axis, split_axis=0, concat_axis=0, tiled=True)  26.6 us
    all_to_all x5, starting transfers between devices, dealt(): return lax.all_to_all(x, axis, split_axis=0, concat_axis=0, tiled=True)  25.8 us
    ppermute x12, waiting for transfers between devices, across(): lax.ppermute(pieces[k], SPREAD, [(i, i ^ k) for i in range(4)])  18.3 us
    ppermute x17, waiting for transfers between devices, swapped(): return lax.ppermute(x, axis, [(0, 1), (1, 0)])  17.7 us
    ppermute x13, starting transfers between devices, y_moved(): return lax.ppermute(x, 'y', [(i, (i + distance) % 4) for i in range(4)])  16.9 us
    ppermute x13, waiting for transfers between devices, y_moved(): return lax.ppermute(x, 'y', [(i, (i + distance) % 4) for i in range(4)])  15.8 us
  transfers between devices with their start and end apart: 57, of which 31 were waited for; matrix products, arithmetic and copies ran while one was open for 4% of the time, Pallas kernels for 28%

profile of v4, /device:TPU:8, one launch (start us, length us, event | category | flops | bytes accessed | tf_op | source)
XLA Modules:
  0.0 395.1 jit_solution(4841613586188478593)
XLA Ops:
  5.6 7.9 %shard_map.203 = (bf16[512,2048]{1,0:T(8,128)(2,1)}, f32[512,128]{1,0:T(8,128)}, bf16[768,128]{1,0:T(8,128)(2,1)}, bf16[768,128]{1,0:T(8,128)(2,1)}, bf16[768,12...) custom-call(s32[5]{0:T(128)S(1)} %stack.38.refs_0_.place, ...), custom_call_target="tpu_custom_call" | custom-call | flops 1610612736 | bytes 8945664 | tf_op jit(solution)/shard_map/pallas_call | solution.py:127
  13.5 4.0 %collective-permute-start = (bf16[768,128]{1,0:T(8,128)(2,1)}, bf16[768,128]{1,0:T(8,128)(2,1)S(1)}, u32[]{:S(2)}, u32[]{:S(2)}) collective-permute-start(bf16[768,128]{1,0:T(8,128)(2,1)} %get-tuple-element.157), channel_id=1, source_target_pairs={{0,32},{32,0},{64,96},{96,64},{1,33},{33,1},{65,97},{97,65},{2,34}... | collective-permute-start | bytes 589832 | tf_op jit(solution)/shard_map/ppermute | solution.py:676
  17.5 3.0 collective-permute-start.1
  20.5 5.4 %shard_map.204.refs_11_ = f32[512,704]{1,0:T(8,128)} custom-call(bf16[512,2048]{1,0:T(8,128)(2,1)} %refs_12_.1, bf16[704,2048]{1,0:T(8,128)(2,1)} %refs_1_.3), custom_call_target="tpu_custom_call" | custom-call | flops 1476395008 | bytes 6422528 | tf_op jit(solution)/shard_map/pallas_call | solution.py:127
  27.9 2.7 collective-permute-done.2.refs_6_
  33.6 13.0 %shard_map.205 = (f32[4,128,512]{2,1,0:T(8,128)}, f32[4,8,512]{2,1,0:T(8,128)}) custom-call(s32[5]{0:T(128)S(1)} %stack.38.refs_0_.place, bf16[4,512,128]{2,1,0:T(8,128)(2,1)} %copy-done.23, bf16[4,512,128]{2,1,0:T(8,128)(2,1)} %copy-done.48, bf16[768,128]{1,0:T(8,128)(2,1)} %get-tuple-element.160.refs_3_, bf16[768,128]{1,0:T(8,128)(2,1)} %copy-done.45, ...), custom_call_target="tpu_custom_call" | custom-call | flops 2684354560 | bytes 2490368 | tf_op jit(solution)/shard_map/pallas_call | solution.py:127
  49.7 14.3 %shard_map.206 = (bf16[256,128]{1,0:T(8,128)(2,1)}, bf16[256,128]{1,0:T(8,128)(2,1)}, bf16[256,128]{1,0:T(8,128)(2,1)}, bf16[256,128]{1,0:T(8,128)(2,1)}, f32[4,128,512]{2,1,0:T(8,128)}, /*index=5*/f32[4,8,512]{2,1,0:T(8,128)}) custom-call(s32[5]{0:T(128)S(1)} %stack.38.refs_0_.place, bf16[4,512,128]{2,1,0:T(8,128)(2,1)} %copy-done.49, ...), custom_call_target="tpu_custom_call" | custom-call | flops 2684354560 | bytes 3866624 | tf_op jit(solution)/shard_map/pallas_call | solution.py:127
  66.1 3.0 collective-permute-start.7
  72.1 5.4 %collective-permute-done.8.refs_4_ = bf16[256,128]{1,0:T(8,128)(2,1)S(1)} collective-permute-done((bf16[256,128]{1,0:T(8,128)(2,1)}, bf16[256,128]{1,0:T(8,128)(2,1)S(1)}, u32[]{:S(2)}, u32[]{:S(2)}) %collective-permute-start.8) | collective-permute-done | bytes 65568 | tf_op jit(solution)/shard_map/ppermute | solution.py:676
  78.2 4.2 %shard_map.207 = (bf16[512,256]{1,0:T(8,128)(2,1)}, bf16[128,2048]{1,0:T(8,128)(2,1)}, bf16[128,2048]{1,0:T(8,128)(2,1)}, bf16[64,2048]{1,0:T(8,128)(2,1)}, bf16...) custom-call(s32[5]{0:T(128)S(1)} %stack.38.refs_0_.place, ...), custom_call_target="tpu_custom_call" | custom-call | flops 536870912 | bytes 3670016 | tf_op jit(solution)/shard_map/pallas_call | solution.py:127
  85.1 6.0 %collective-permute-done.11.refs_3_ = bf16[64,2048]{1,0:T(8,128)(2,1)S(1)} collective-permute-done((bf16[64,2048]{1,0:T(8,128)(2,1)}, bf16[64,2048]{1,0:T(8,128)(2,1)S(1)}, u32[]{:S(2)}, u32[]{:S(2)}) %collective-permute-start.11) | collective-permute-done | bytes 262176 | tf_op jit(solution)/shard_map/ppermute | solution.py:671
  91.1 3.9 collective-permute-done.9.refs_1_
  97.0 3.0 shard_map.208
  103.0 3.7 collective-permute-done.12.refs_4_
  109.5 4.3 %shard_map.209 = (bf16[64,2048]{1,0:T(8,128)(2,1)}, f32[64,2048]{1,0:T(8,128)}, f32[64,2048]{1,0:T(8,128)}, f32[64,128]{1,0:T(8,128)}) custom-call(s32[5]{0:T(128)S(1)} %stack.38.refs_0_.place, bf16[128,2048]{1,0:T(8,128)(2,1)} %copy-done.8, bf16[128,2048]{1,0:T(8,128)(2,1)} %copy-done.9, bf16[64,2048]{1,0:T(8,128)(2,1)} %get-tuple-element.175.refs_3_, ...), custom_call_target="tpu_custom_call" | custom-call | bytes 3440640 | tf_op jit(solution)/shard_map/pallas_call | solution.py:127
  122.5 3.8 collective-permute-done.17.refs_5_.refs_6_
  133.8 12.7 %shard_map.210 = (bf16[512,704]{1,0:T(8,128)(2,1)}, bf16[512,704]{1,0:T(8,128)(2,1)}, bf16[512,704]{1,0:T(8,128)(2,1)}, bf16[512,2048]{1,0:T(8,128)(2,1)}) custom-call(s32[5]{0:T(128)S(1)} %stack.38.refs_0_.place, bf16[64,2048]{1,0:T(8,128)(2,1)} %get-tuple-element.182.refs_1_.refs_2_, bf16[64,2048]{1,0:T(8,128)(2,1)} %copy-done.36, ...), custom_call_target="tpu_custom_call" | custom-call | flops 5905580032 | bytes 13565952 | tf_op jit(solution)/shard_map/pallas_call | solution.py:127
  146.5 4.8 %all-to-all-start = ((bf16[8,64,2048]{2,1,0:T(8,128)(2,1)}), bf16[8,64,2048]{2,1,0:T(8,128)(2,1)S(1)}, u32[]{:S(2)}, u32[]{:S(2)}) async-start(bf16[8,64,2048]{2,1,0:T(8,128)(2,1)} %bitcast.62), calls=%async_computation | async-start | bytes 4194304 | tf_op jit(solution)/shard_map/all_to_all | solution.py:783
  151.3 10.8 %shard_map.211 = (bf16[8,2112,128]{2,1,0:T(8,128)(2,1)}, bf16[8,2112,128]{2,1,0:T(8,128)(2,1)}) custom-call(s32[5]{0:T(128)S(1)} %stack.38.refs_0_.place, bf16[512,704]{1,0:T(8,128)(2,1)} %get-tuple-element.185.refs_1_, bf16[64,2048]{1,0:T(8,128)(2,1)} %get-tuple-element.182.refs_1_.refs_2_, bf16[64,2048]{1,0:T(8,128)(2,1)} %copy-done.36, ...), custom_call_target="tpu_custom_call" | custom-call | tf_op jit(solution)/shard_map/pallas_call | solution.py:127
  162.1 10.7 %all-to-all-done.refs_0_ = bf16[8,64,2048]{2,1,0:T(8,128)(2,1)S(1)} async-done(((bf16[8,64,2048]{2,1,0:T(8,128)(2,1)}), bf16[8,64,2048]{2,1,0:T(8,128)(2,1)S(1)}, u32[]{:S(2)}, u32[]{:S(2)}) %all-to-all-start) | async-done | bytes 2097184 | tf_op jit(solution)/shard_map/all_to_all | solution.py:783
  172.7 3.7 shard_map.213
  176.4 5.7 %all-to-all-start.1 = ((bf16[8,64,2048]{2,1,0:T(8,128)(2,1)}), bf16[8,64,2048]{2,1,0:T(8,128)(2,1)S(1)}, u32[]{:S(2)}, u32[]{:S(2)}) async-start(bf16[8,64,2048]{2,1,0:T(8,128)(2,1)} %get-tuple-element.198), calls=%async_computation.1 | async-start | bytes 4194304 | tf_op jit(solution)/shard_map/all_to_all | solution.py:783
  182.2 5.7 %shard_map.212 = (bf16[2,2112,128]{2,1,0:T(8,128)(2,1)}, bf16[2,2112,128]{2,1,0:T(8,128)(2,1)}, bf16[2,2112,128]{2,1,0:T(8,128)(2,1)}, bf16[2,2112,128]{2,1,0:T(8,128)(2,1)}) custom-call(s32[1]{0:T(128)} %bitcast.12.place, bf16[8,2112,128]{2,1,0:T(8,128)(2,1)} %get-tuple-element.190.mine, bf16[8,2112,128]{2,1,0:T(8,128)(2,1)} %collective-permute-done.21.received), custom_call_target="tpu_custom_call" | custom-call | tf_op jit(solution)/shard_map/pallas_call | solution.py:711
  191.2 3.1 convolution_convert_fusion
  194.3 13.9 %all-to-all-done.1 = bf16[8,64,2048]{2,1,0:T(8,128)(2,1)S(1)} async-done(((bf16[8,64,2048]{2,1,0:T(8,128)(2,1)}), bf16[8,64,2048]{2,1,0:T(8,128)(2,1)S(1)}, u32[]{:S(2)}, u32[]{:S(2)}) %all-to-all-start.1) | async-done | bytes 2097184 | tf_op jit(solution)/shard_map/all_to_all | solution.py:783
  208.2 3.5 shard_map.214
  211.8 3.6 collective-permute-done.22
  216.4 4.8 %all-to-all-start.2 = ((bf16[4,128,2048]{2,1,0:T(8,128)(2,1)}), bf16[4,128,2048]{2,1,0:T(8,128)(2,1)S(1)}, u32[]{:S(2)}, u32[]{:S(2)}) async-start(bf16[4,128,2048]{2,1,0:T(8,128)(2,1)} %bitcast.61), calls=%async_computation.2 | async-start | bytes 4194304 | tf_op jit(solution)/shard_map/all_to_all | solution.py:783
  221.9 3.2 collective-permute-start.25
  227.7 5.6 %collective-permute-done.26.refs_10_ = bf16[256,128]{1,0:T(8,128)(2,1)S(1)} collective-permute-done((bf16[256,128]{1,0:T(8,128)(2,1)S(1)}, bf16[256,128]{1,0:T(8,128)(2,1)S(1)}, u32[]{:S(2)}, u32[]{:S(2)}) %collective-permute-start.26) | collective-permute-done | bytes 65568 | tf_op jit(solution)/shard_map/ppermute | solution.py:676
  234.9 20.3 %shard_map.215 = (f32[4,128,512]{2,1,0:T(8,128)}, bf16[4,512,128]{2,1,0:T(8,128)(2,1)}, bf16[4,512,128]{2,1,0:T(8,128)(2,1)}) custom-call(s32[5]{0:T(128)S(1)} %stack.38.refs_0_.place, bf16[4,512,128]{2,1,0:T(8,128)(2,1)} %copy-done.49, bf16[4,512,128]{2,1,0:T(8,128)(2,1)} %copy-done.50, bf16[768,128]{1,0:T(8,128)(2,1)} %get-tuple-element.160.refs_3_, ...), custom_call_target="tpu_custom_call" | custom-call | flops 6710886400 | bytes 4849664 | tf_op jit(solution)/shard_map/pallas_call | solution.py:127
  255.3 2.9 shard_map.216.refs_0_
  260.3 21.2 %shard_map.217 = (bf16[256,128]{1,0:T(8,128)(2,1)}, bf16[256,128]{1,0:T(8,128)(2,1)}, bf16[256,128]{1,0:T(8,128)(2,1)}, bf16[256,128]{1,0:T(8,128)(2,1)}, bf16[4...) custom-call(s32[5]{0:T(128)S(1)} %stack.38.refs_0_.place, bf16[4,512,128]{2,1,0:T(8,128)(2,1)} %copy-done.23, ...), custom_call_target="tpu_custom_call" | custom-call | flops 6710886400 | bytes 5111808 | tf_op jit(solution)/shard_map/pallas_call | solution.py:127
  282.4 2.7 shard_map.219
  288.4 3.0 collective-permute-start.32
  291.4 2.8 collective-permute-start.33
  295.0 4.8 %all-to-all-start.3 = ((bf16[4,128,2048]{2,1,0:T(8,128)(2,1)}), bf16[4,128,2048]{2,1,0:T(8,128)(2,1)S(1)}, u32[]{:S(2)}, u32[]{:S(2)}) async-start(bf16[4,128,2048]{2,1,0:T(8,128)(2,1)} %shard_map.219), calls=%async_computation.3 | async-start | bytes 4194304 | tf_op jit(solution)/shard_map/all_to_all | solution.py:783
  301.5 3.1 collective-permute-done.34.refs_4_
  307.2 7.0 %shard_map.220 = (bf16[512,768]{1,0:T(8,128)(2,1)}, bf16[512,2048]{1,0:T(8,128)(2,1)}, f32[1,2048]{1,0:T(1,128)S(1)}, f32[1,2048]{1,0:T(1,128)S(1)}, f32[3,256]{1,0:T(4,128)S(1)}) custom-call(s32[5]{0:T(128)S(1)} %stack.38.refs_0_.place, bf16[768,128]{1,0:T(8,128)(2,1)} %get-tuple-element.258.refs_1_, bf16[768,128]{1,0:T(8,128)(2,1)} %copy-done.43, ...), custom_call_target="tpu_custom_call" | custom-call | flops 1610612736 | bytes 9699328 | tf_op jit(solution)/shard_map/pallas_call | solution.py:127
  314.2 7.1 %shard_map.221 = (bf16[8,1024,128]{2,1,0:T(8,128)(2,1)}, bf16[8,1024,128]{2,1,0:T(8,128)(2,1)}) custom-call(s32[5]{0:T(128)S(1)} %stack.38.refs_0_.place, bf16[512,768]{1,0:T(8,128)(2,1)} %get-tuple-element.272.refs_1_, bf16[512,2048]{1,0:T(8,128)(2,1)} %get-tuple-element.273.refs_2_, bf16[512,256]{1,0:T(8,128)(2,1)} %get-tuple-element.274.refs_3_, ...), custom_call_target="tpu_custom_call" | custom-call | tf_op jit(solution)/shard_map/pallas_call | solution.py:127
  324.2 5.7 %all-to-all-start.4 = ((bf16[8,64,2048]{2,1,0:T(8,128)(2,1)}), bf16[8,64,2048]{2,1,0:T(8,128)(2,1)}, u32[]{:S(2)}, u32[]{:S(2)}) async-start(bf16[8,64,2048]{2,1,0:T(8,128)(2,1)} %bitcast.60), calls=%async_computation.4 | async-start | bytes 4194304 | tf_op jit(solution)/shard_map/all_to_all | solution.py:783
  332.2 3.0 collective-permute-done.36
  340.8 3.5 shard_map.222
  344.3 2.8 collective-permute-start.40
  355.6 3.3 shard_map.224.refs_0_
  363.1 7.9 %collective-permute-done.43 = bf16[2,1024,128]{2,1,0:T(8,128)(2,1)} collective-permute-done((bf16[2,1024,128]{2,1,0:T(8,128)(2,1)}, bf16[2,1024,128]{2,1,0:T(8,128)(2,1)}, u32[]{:S(2)}, u32[]{:S(2)}) %collective-permute-start.43) | collective-permute-done | bytes 524320 | tf_op jit(solution)/shard_map/ppermute | solution.py:770
  378.4 3.6 collective-permute-done.51
  391.1 2.9 shard_map.225
  (248 shorter events, 106.0 us)
Async XLA Ops:
  13.5 14.4 %collective-permute-start = (bf16[768,128]{1,0:T(8,128)(2,1)}, bf16[768,128]{1,0:T(8,128)(2,1)S(1)}, u32[]{:S(2)}, u32[]{:S(2)}) collective-permute-start(bf16[768,128]{1,0:T(8,128)(2,1)} %get-tuple-element.157), channel_id=1, source_target_pairs={{0,32},{32,0},{64,96},{96,64},{1,33},{33,1},{65,97},{97,65},{2,34}... | collective-permute-start | bytes 589832 | tf_op jit(solution)/shard_map/ppermute | solution.py:676
  17.5 10.5 %collective-permute-start.1 = (bf16[768,128]{1,0:T(8,128)(2,1)}, bf16[768,128]{1,0:T(8,128)(2,1)S(1)}, u32[]{:S(2)}, u32[]{:S(2)}) collective-permute-start(bf16[768,128]{1,0:T(8,128)(2,1)} %get-tuple-element.158), channel_id=1, source_target_pairs={{0,64},{32,96},{64,0},{96,32},{1,65},{33,97},{65,1},{97,33},{2,66}... | collective-permute-start | bytes 589832 | tf_op jit(solution)/shard_map/ppermute | solution.py:676
  20.5 10.2 %collective-permute-start.2 = (bf16[768,128]{1,0:T(8,128)(2,1)}, bf16[768,128]{1,0:T(8,128)(2,1)S(1)}, u32[]{:S(2)}, u32[]{:S(2)}) collective-permute-start(bf16[768,128]{1,0:T(8,128)(2,1)} %get-tuple-element.159), channel_id=1, source_target_pairs={{0,96},{32,64},{64,32},{96,0},{1,97},{33,65},{65,33},{97,1},{2,98}... | collective-permute-start | bytes 589832 | tf_op jit(solution)/shard_map/ppermute | solution.py:676
  30.9 15.7 %collective-permute-start.4 = (bf16[4,512,128]{2,1,0:T(8,128)(2,1)S(1)}, bf16[4,512,128]{2,1,0:T(8,128)(2,1)S(1)}, u32[]{:S(2)}, u32[]{:S(2)}) collective-permute-start(bf16[4,512,128]{2,1,0:T(8,128)(2,1)S(1)} %pad_maximum_fusion.refs_1_), channel_id=1, source_target_pairs={{0,16},{16,0},{1,17},{17,1},{2,18},{18,2},{3,19},{19,3},{4,20},{20... | collective-permute-start | bytes 1572872 | tf_op jit(solution)/shard_map/ppermute | solution.py:671
  64.0 6.6 %collective-permute-start.6 = (bf16[256,128]{1,0:T(8,128)(2,1)}, bf16[256,128]{1,0:T(8,128)(2,1)S(1)}, u32[]{:S(2)}, u32[]{:S(2)}) collective-permute-start(bf16[256,128]{1,0:T(8,128)(2,1)} %get-tuple-element.170), channel_id=1, source_target_pairs={{0,32},{32,0},{64,96},{96,64},{1,33},{33,1},{65,97},{97,65},{2,34}... | collective-permute-start | bytes 196616 | tf_op jit(solution)/shard_map/ppermute | solution.py:676
  69.2 8.4 %collective-permute-start.8 = (bf16[256,128]{1,0:T(8,128)(2,1)}, bf16[256,128]{1,0:T(8,128)(2,1)S(1)}, u32[]{:S(2)}, u32[]{:S(2)}) collective-permute-start(bf16[256,128]{1,0:T(8,128)(2,1)} %get-tuple-element.172), channel_id=1, source_target_pairs={{0,96},{32,64},{64,32},{96,0},{1,97},{33,65},{65,33},{97,1},{2,98}... | collective-permute-start | bytes 196616 | tf_op jit(solution)/shard_map/ppermute | solution.py:676
  82.4 12.5 %collective-permute-start.9 = (bf16[128,2048]{1,0:T(8,128)(2,1)}, bf16[128,2048]{1,0:T(8,128)(2,1)S(1)}, u32[]{:S(2)}, u32[]{:S(2)}) collective-permute-start(bf16[128,2048]{1,0:T(8,128)(2,1)} %get-tuple-element.173), channel_id=1, source_target_pairs={{0,2},{2,4},{4,6},{6,0},{1,3},{3,5},{5,7},{7,1},{8,10},{10,12},{12... | collective-permute-start | bytes 1572872 | tf_op jit(solution)/shard_map/ppermute | solution.py:791
  84.0 12.2 %collective-permute-start.10 = (bf16[128,2048]{1,0:T(8,128)(2,1)}, bf16[128,2048]{1,0:T(8,128)(2,1)S(1)}, u32[]{:S(2)}, u32[]{:S(2)}) collective-permute-start(bf16[128,2048]{1,0:T(8,128)(2,1)} %get-tuple-element.174), channel_id=1, source_target_pairs={{0,6},{2,0},{4,2},{6,4},{1,7},{3,1},{5,3},{7,5},{8,14},{10,8},{12,... | collective-permute-start | bytes 1572872 | tf_op jit(solution)/shard_map/ppermute | solution.py:791
  84.5 6.6 %collective-permute-start.11 = (bf16[64,2048]{1,0:T(8,128)(2,1)}, bf16[64,2048]{1,0:T(8,128)(2,1)S(1)}, u32[]{:S(2)}, u32[]{:S(2)}) collective-permute-start(bf16[64,2048]{1,0:T(8,128)(2,1)} %get-tuple-element.176), channel_id=1, source_target_pairs={{0,1},{1,0},{2,3},{3,2},{4,5},{5,4},{6,7},{7,6},{8,9},{9,8},{10,11... | collective-permute-start | bytes 786440 | tf_op jit(solution)/shard_map/ppermute | solution.py:671
  100.0 6.7 %collective-permute-start.12 = (bf16[64,2048]{1,0:T(8,128)(2,1)}, bf16[64,2048]{1,0:T(8,128)(2,1)S(1)}, u32[]{:S(2)}, u32[]{:S(2)}) collective-permute-start(bf16[64,2048]{1,0:T(8,128)(2,1)} %get-tuple-element.179), channel_id=1, source_target_pairs={{0,1},{1,0},{2,3},{3,2},{4,5},{5,4},{6,7},{7,6},{8,9},{9,8},{10,11... | collective-permute-start | bytes 786440 | tf_op jit(solution)/shard_map/ppermute | solution.py:671
  100.7 8.1 %collective-permute-start.13 = (bf16[64,2048]{1,0:T(8,128)(2,1)}, bf16[64,2048]{1,0:T(8,128)(2,1)S(1)}, u32[]{:S(2)}, u32[]{:S(2)}) collective-permute-start(bf16[64,2048]{1,0:T(8,128)(2,1)} %get-tuple-element.180), channel_id=1, source_target_pairs={{0,4},{2,6},{4,0},{6,2},{1,5},{3,7},{5,1},{7,3},{8,12},{10,14},{12... | collective-permute-start | bytes 786440 | tf_op jit(solution)/shard_map/ppermute | solution.py:791
  113.8 6.7 %collective-permute-start.14 = (bf16[64,2048]{1,0:T(8,128)(2,1)}, bf16[64,2048]{1,0:T(8,128)(2,1)S(1)}, u32[]{:S(2)}, u32[]{:S(2)}) collective-permute-start(bf16[64,2048]{1,0:T(8,128)(2,1)} %get-tuple-element.182.refs_1_.refs_2_), channel_id=1, source_target_pairs={{0,1},{1,0},{2,3},{3,2},{4,5},{5,4},{6,7},{7,6},{8,9},{9,8},{10,11... | collective-permute-start | bytes 786440 | tf_op jit(solution)/shard_map/ppermute | solution.py:671
  115.3 11.0 %collective-permute-start.17 = (bf16[64,2048]{1,0:T(8,128)(2,1)}, bf16[64,2048]{1,0:T(8,128)(2,1)S(1)}, u32[]{:S(2)}, u32[]{:S(2)}) collective-permute-start(bf16[64,2048]{1,0:T(8,128)(2,1)} %get-tuple-element.182.refs_1_.refs_2_), channel_id=1, source_target_pairs={{0,4},{2,6},{4,0},{6,2},{1,5},{3,7},{5,1},{7,3},{8,12},{10,14},{12... | collective-permute-start | bytes 786440 | tf_op jit(solution)/shard_map/ppermute | solution.py:791
  117.6 11.4 %collective-permute-start.15 = (bf16[64,2048]{1,0:T(8,128)(2,1)}, bf16[64,2048]{1,0:T(8,128)(2,1)S(1)}, u32[]{:S(2)}, u32[]{:S(2)}) collective-permute-start(bf16[64,2048]{1,0:T(8,128)(2,1)} %get-tuple-element.182.refs_1_.refs_2_), channel_id=1, source_target_pairs={{0,2},{2,4},{4,6},{6,0},{1,3},{3,5},{5,7},{7,1},{8,10},{10,12},{12... | collective-permute-start | bytes 786440 | tf_op jit(solution)/shard_map/ppermute | solution.py:791
  117.6 11.6 %collective-permute-start.16 = (bf16[64,2048]{1,0:T(8,128)(2,1)}, bf16[64,2048]{1,0:T(8,128)(2,1)S(1)}, u32[]{:S(2)}, u32[]{:S(2)}) collective-permute-start(bf16[64,2048]{1,0:T(8,128)(2,1)} %get-tuple-element.182.refs_1_.refs_2_), channel_id=1, source_target_pairs={{0,6},{2,0},{4,2},{6,4},{1,7},{3,1},{5,3},{7,5},{8,14},{10,8},{12,... | collective-permute-start | bytes 786440 | tf_op jit(solution)/shard_map/ppermute | solution.py:791
  120.5 11.4 %collective-permute-start.18 = (bf16[64,2048]{1,0:T(8,128)(2,1)S(1)}, bf16[64,2048]{1,0:T(8,128)(2,1)S(1)}, u32[]{:S(2)}, u32[]{:S(2)}) collective-permute-start(bf16[64,2048]{1,0:T(8,128)(2,1)S(1)} %collective-permute-done.14.refs_2_.refs_3_), channel_id=1, source_target_pairs={{0,2},{2,4},{4,6},{6,0},{1,3},{3,5},{5,7},{7,1},{8,10},{10,12},{12... | collective-permute-start | bytes 786440 | tf_op jit(solution)/shard_map/ppermute | solution.py:791
  121.8 10.2 %collective-permute-start.19 = (bf16[64,2048]{1,0:T(8,128)(2,1)S(1)}, bf16[64,2048]{1,0:T(8,128)(2,1)S(1)}, u32[]{:S(2)}, u32[]{:S(2)}) collective-permute-start(bf16[64,2048]{1,0:T(8,128)(2,1)S(1)} %collective-permute-done.14.refs_2_.refs_3_), channel_id=1, source_target_pairs={{0,6},{2,0},{4,2},{6,4},{1,7},{3,1},{5,3},{7,5},{8,14},{10,8},{12,... | collective-permute-start | bytes 786440 | tf_op jit(solution)/shard_map/ppermute | solution.py:791
  126.3 6.8 %collective-permute-start.20 = (bf16[64,2048]{1,0:T(8,128)(2,1)S(1)}, bf16[64,2048]{1,0:T(8,128)(2,1)S(1)}, u32[]{:S(2)}, u32[]{:S(2)}) collective-permute-start(bf16[64,2048]{1,0:T(8,128)(2,1)S(1)} %collective-permute-done.17.refs_5_.refs_6_), channel_id=1, source_target_pairs={{0,1},{1,0},{2,3},{3,2},{4,5},{5,4},{6,7},{7,6},{8,9},{9,8},{10,11... | collective-permute-start | bytes 786440 | tf_op jit(solution)/shard_map/ppermute | solution.py:671
  146.5 26.2 %all-to-all-start = ((bf16[8,64,2048]{2,1,0:T(8,128)(2,1)}), bf16[8,64,2048]{2,1,0:T(8,128)(2,1)S(1)}, u32[]{:S(2)}, u32[]{:S(2)}) async-start(bf16[8,64,2048]{2,1,0:T(8,128)(2,1)} %bitcast.62), calls=%async_computation | async-start | bytes 4194304 | tf_op jit(solution)/shard_map/all_to_all | solution.py:783
  172.7 9.4 %collective-permute-start.21 = (bf16[8,2112,128]{2,1,0:T(8,128)(2,1)}, bf16[8,2112,128]{2,1,0:T(8,128)(2,1)}, u32[]{:S(2)}, u32[]{:S(2)}) collective-permute-start(bf16[8,2112,128]{2,1,0:T(8,128)(2,1)} %get-tuple-element.191), channel_id=1, source_target_pairs={{0,8},{8,0},{1,9},{9,1},{2,10},{10,2},{3,11},{11,3},{4,12},{12,4},... | collective-permute-start | bytes 12976136 | tf_op jit(solution)/shard_map/ppermute | solution.py:671
  176.4 31.8 %all-to-all-start.1 = ((bf16[8,64,2048]{2,1,0:T(8,128)(2,1)}), bf16[8,64,2048]{2,1,0:T(8,128)(2,1)S(1)}, u32[]{:S(2)}, u32[]{:S(2)}) async-start(bf16[8,64,2048]{2,1,0:T(8,128)(2,1)} %get-tuple-element.198), calls=%async_computation.1 | async-start | bytes 4194304 | tf_op jit(solution)/shard_map/all_to_all | solution.py:783
  187.9 27.5 %collective-permute-start.22 = (bf16[2,2112,128]{2,1,0:T(8,128)(2,1)}, bf16[2,2112,128]{2,1,0:T(8,128)(2,1)S(1)}, u32[]{:S(2)}, u32[]{:S(2)}) collective-permute-start(bf16[2,2112,128]{2,1,0:T(8,128)(2,1)} %get-tuple-element.192), channel_id=1, source_target_pairs={{0,16},{16,32},{32,48},{48,0},{1,17},{17,33},{33,49},{49,1},{2,18}... | collective-permute-start | bytes 3244040 | tf_op jit(solution)/shard_map/ppermute | solution.py:770
  189.0 26.4 %collective-permute-start.23 = (bf16[2,2112,128]{2,1,0:T(8,128)(2,1)}, bf16[2,2112,128]{2,1,0:T(8,128)(2,1)}, u32[]{:S(2)}, u32[]{:S(2)}) collective-permute-start(bf16[2,2112,128]{2,1,0:T(8,128)(2,1)} %get-tuple-element.193), channel_id=1, source_target_pairs={{0,48},{16,0},{32,16},{48,32},{1,49},{17,1},{33,17},{49,33},{2,50}... | collective-permute-start | bytes 3244040 | tf_op jit(solution)/shard_map/ppermute | solution.py:770
  216.4 38.9 %all-to-all-start.2 = ((bf16[4,128,2048]{2,1,0:T(8,128)(2,1)}), bf16[4,128,2048]{2,1,0:T(8,128)(2,1)S(1)}, u32[]{:S(2)}, u32[]{:S(2)}) async-start(bf16[4,128,2048]{2,1,0:T(8,128)(2,1)} %bitcast.61), calls=%async_computation.2 | async-start | bytes 4194304 | tf_op jit(solution)/shard_map/all_to_all | solution.py:783
  221.2 6.5 %collective-permute-start.24 = (bf16[256,128]{1,0:T(8,128)(2,1)}, bf16[256,128]{1,0:T(8,128)(2,1)S(1)}, u32[]{:S(2)}, u32[]{:S(2)}) collective-permute-start(bf16[256,128]{1,0:T(8,128)(2,1)} %get-tuple-element.206), channel_id=1, source_target_pairs={{0,32},{32,0},{64,96},{96,64},{1,33},{33,1},{65,97},{97,65},{2,34}... | collective-permute-start | bytes 196616 | tf_op jit(solution)/shard_map/ppermute | solution.py:676
  225.1 8.2 %collective-permute-start.26 = (bf16[256,128]{1,0:T(8,128)(2,1)S(1)}, bf16[256,128]{1,0:T(8,128)(2,1)S(1)}, u32[]{:S(2)}, u32[]{:S(2)}) collective-permute-start(bf16[256,128]{1,0:T(8,128)(2,1)S(1)} %copy-done.54), channel_id=1, source_target_pairs={{0,96},{32,64},{64,32},{96,0},{1,97},{33,65},{65,33},{97,1},{2,98}... | collective-permute-start | bytes 196616 | tf_op jit(solution)/shard_map/ppermute | solution.py:676
  233.3 25.1 %collective-permute-start.28 = (bf16[2,2112,128]{2,1,0:T(8,128)(2,1)}, bf16[2,2112,128]{2,1,0:T(8,128)(2,1)S(1)}, u32[]{:S(2)}, u32[]{:S(2)}) collective-permute-start(bf16[2,2112,128]{2,1,0:T(8,128)(2,1)} %get-tuple-element.224), channel_id=1, source_target_pairs={{0,32},{16,48},{32,0},{48,16},{1,33},{17,49},{33,1},{49,17},{2,34}... | collective-permute-start | bytes 3244040 | tf_op jit(solution)/shard_map/ppermute | solution.py:770
  258.4 23.1 %collective-permute-start.29 = (bf16[4,512,128]{2,1,0:T(8,128)(2,1)S(1)}, bf16[4,512,128]{2,1,0:T(8,128)(2,1)S(1)}, u32[]{:S(2)}, u32[]{:S(2)}) collective-permute-start(bf16[4,512,128]{2,1,0:T(8,128)(2,1)S(1)} %add_convert_fusion.1), channel_id=1, source_target_pairs={{0,16},{16,0},{1,17},{17,1},{2,18},{18,2},{3,19},{19,3},{4,20},{20... | collective-permute-start | bytes 1572872 | tf_op jit(solution)/shard_map/ppermute | solution.py:671
  259.3 22.3 %collective-permute-start.30 = (bf16[128,2048]{1,0:T(8,128)(2,1)S(1)}, bf16[128,2048]{1,0:T(8,128)(2,1)S(1)}, u32[]{:S(2)}, u32[]{:S(2)}) collective-permute-start(bf16[128,2048]{1,0:T(8,128)(2,1)S(1)} %copy-done.10), channel_id=1, source_target_pairs={{0,1},{1,0},{2,3},{3,2},{4,5},{5,4},{6,7},{7,6},{8,9},{9,8},{10,11... | collective-permute-start | bytes 1572872 | tf_op jit(solution)/shard_map/ppermute | solution.py:671
  288.4 13.1 %collective-permute-start.32 = (bf16[768,128]{1,0:T(8,128)(2,1)}, bf16[768,128]{1,0:T(8,128)(2,1)S(1)}, u32[]{:S(2)}, u32[]{:S(2)}) collective-permute-start(bf16[768,128]{1,0:T(8,128)(2,1)} %get-tuple-element.251), channel_id=1, source_target_pairs={{0,32},{32,0},{64,96},{96,64},{1,33},{33,1},{65,97},{97,65},{2,34}... | collective-permute-start | bytes 589832 | tf_op jit(solution)/shard_map/ppermute | solution.py:676
  291.4 10.1 %collective-permute-start.33 = (bf16[768,128]{1,0:T(8,128)(2,1)}, bf16[768,128]{1,0:T(8,128)(2,1)}, u32[]{:S(2)}, u32[]{:S(2)}) collective-permute-start(bf16[768,128]{1,0:T(8,128)(2,1)} %get-tuple-element.252), channel_id=1, source_target_pairs={{0,64},{32,96},{64,0},{96,32},{1,65},{33,97},{65,1},{97,33},{2,66}... | collective-permute-start | bytes 589832 | tf_op jit(solution)/shard_map/ppermute | solution.py:676
  294.1 10.4 %collective-permute-start.34 = (bf16[768,128]{1,0:T(8,128)(2,1)}, bf16[768,128]{1,0:T(8,128)(2,1)}, u32[]{:S(2)}, u32[]{:S(2)}) collective-permute-start(bf16[768,128]{1,0:T(8,128)(2,1)} %get-tuple-element.253), channel_id=1, source_target_pairs={{0,96},{32,64},{64,32},{96,0},{1,97},{33,65},{65,33},{97,1},{2,98}... | collective-permute-start | bytes 589832 | tf_op jit(solution)/shard_map/ppermute | solution.py:676
  295.0 29.2 %all-to-all-start.3 = ((bf16[4,128,2048]{2,1,0:T(8,128)(2,1)}), bf16[4,128,2048]{2,1,0:T(8,128)(2,1)S(1)}, u32[]{:S(2)}, u32[]{:S(2)}) async-start(bf16[4,128,2048]{2,1,0:T(8,128)(2,1)} %shard_map.219), calls=%async_computation.3 | async-start | bytes 4194304 | tf_op jit(solution)/shard_map/all_to_all | solution.py:783
  304.5 16.7 %collective-permute-start.38 = (bf16[2112,128]{1,0:T(8,128)(2,1)S(1)}, bf16[2112,128]{1,0:T(8,128)(2,1)S(1)}, u32[]{:S(2)}, u32[]{:S(2)}) collective-permute-start(bf16[2112,128]{1,0:T(8,128)(2,1)S(1)} %fusion), channel_id=1, source_target_pairs={{0,64},{64,0},{1,65},{65,1},{2,66},{66,2},{3,67},{67,3},{4,68},{68... | collective-permute-start | bytes 1622024 | tf_op jit(solution)/shard_map/ppermute | solution.py:671
  322.1 18.7 %collective-permute-start.39 = (bf16[8,1024,128]{2,1,0:T(8,128)(2,1)}, bf16[8,1024,128]{2,1,0:T(8,128)(2,1)}, u32[]{:S(2)}, u32[]{:S(2)}) collective-permute-start(bf16[8,1024,128]{2,1,0:T(8,128)(2,1)} %get-tuple-element.279), channel_id=1, source_target_pairs={{0,8},{8,0},{1,9},{9,1},{2,10},{10,2},{3,11},{11,3},{4,12},{12,4},... | collective-permute-start | bytes 6291464 | tf_op jit(solution)/shard_map/ppermute | solution.py:671
  324.2 30.8 %all-to-all-start.4 = ((bf16[8,64,2048]{2,1,0:T(8,128)(2,1)}), bf16[8,64,2048]{2,1,0:T(8,128)(2,1)}, u32[]{:S(2)}, u32[]{:S(2)}) async-start(bf16[8,64,2048]{2,1,0:T(8,128)(2,1)} %bitcast.60), calls=%async_computation.4 | async-start | bytes 4194304 | tf_op jit(solution)/shard_map/all_to_all | solution.py:783
  344.3 10.6 %collective-permute-start.40 = (f32[35,256]{1,0:T(8,128)S(1)}, f32[35,256]{1,0:T(8,128)S(1)}, u32[]{:S(2)}, u32[]{:S(2)}) collective-permute-start(f32[35,256]{1,0:T(8,128)S(1)} %add.157), channel_id=1, source_target_pairs={{0,64},{64,0},{1,65},{65,1},{2,66},{66,2},{3,67},{67,3},{4,68},{68... | collective-permute-start | bytes 107528 | tf_op jit(solution)/shard_map/ppermute | solution.py:806
  347.2 15.9 %collective-permute-start.42 = (bf16[2,1024,128]{2,1,0:T(8,128)(2,1)}, bf16[2,1024,128]{2,1,0:T(8,128)(2,1)}, u32[]{:S(2)}, u32[]{:S(2)}) collective-permute-start(bf16[2,1024,128]{2,1,0:T(8,128)(2,1)} %get-tuple-element.291), channel_id=1, source_target_pairs={{0,16},{16,32},{32,48},{48,0},{1,17},{17,33},{33,49},{49,1},{2,18}... | collective-permute-start | bytes 1572872 | tf_op jit(solution)/shard_map/ppermute | solution.py:770
  348.2 22.9 %collective-permute-start.43 = (bf16[2,1024,128]{2,1,0:T(8,128)(2,1)}, bf16[2,1024,128]{2,1,0:T(8,128)(2,1)}, u32[]{:S(2)}, u32[]{:S(2)}) collective-permute-start(bf16[2,1024,128]{2,1,0:T(8,128)(2,1)} %get-tuple-element.292), channel_id=1, source_target_pairs={{0,48},{16,0},{32,16},{48,32},{1,49},{17,1},{33,17},{49,33},{2,50}... | collective-permute-start | bytes 1572872 | tf_op jit(solution)/shard_map/ppermute | solution.py:770
  350.4 21.8 %collective-permute-start.50 = (bf16[2,1024,128]{2,1,0:T(8,128)(2,1)}, bf16[2,1024,128]{2,1,0:T(8,128)(2,1)}, u32[]{:S(2)}, u32[]{:S(2)}) collective-permute-start(bf16[2,1024,128]{2,1,0:T(8,128)(2,1)} %get-tuple-element.298), channel_id=1, source_target_pairs={{0,32},{16,48},{32,0},{48,16},{1,33},{17,49},{33,1},{49,17},{2,34}... | collective-permute-start | bytes 1572872 | tf_op jit(solution)/shard_map/ppermute | solution.py:770
  358.9 12.1 %collective-permute-start.41 = (bf16[64,2176]{1,0:T(8,128)(2,1)}, bf16[64,2176]{1,0:T(8,128)(2,1)S(1)}, u32[]{:S(2)}, u32[]{:S(2)}) collective-permute-start(bf16[64,2176]{1,0:T(8,128)(2,1)} %shard_map.224.refs_0_), channel_id=1, source_target_pairs={{0,1},{1,0},{2,3},{3,2},{4,5},{5,4},{6,7},{7,6},{8,9},{9,8},{10,11... | collective-permute-start | bytes 835592 | tf_op jit(solution)/shard_map/ppermute | solution.py:671
  359.8 18.2 %collective-permute-start.46 = (bf16[64,2176]{1,0:T(8,128)(2,1)}, bf16[64,2176]{1,0:T(8,128)(2,1)S(1)}, u32[]{:S(2)}, u32[]{:S(2)}) collective-permute-start(bf16[64,2176]{1,0:T(8,128)(2,1)} %shard_map.224.refs_0_), channel_id=1, source_target_pairs={{0,4},{2,6},{4,0},{6,2},{1,5},{3,7},{5,1},{7,3},{8,12},{10,14},{12... | collective-permute-start | bytes 835592 | tf_op jit(solution)/shard_map/ppermute | solution.py:791
  373.5 8.6 %collective-permute-start.51 = (bf16[1024,128]{1,0:T(8,128)(2,1)S(1)}, bf16[1024,128]{1,0:T(8,128)(2,1)S(1)}, u32[]{:S(2)}, u32[]{:S(2)}) collective-permute-start(bf16[1024,128]{1,0:T(8,128)(2,1)S(1)} %fusion.1), channel_id=1, source_target_pairs={{0,64},{64,0},{1,65},{65,1},{2,66},{66,2},{3,67},{67,3},{4,68},{68... | collective-permute-start | bytes 786440 | tf_op jit(solution)/shard_map/ppermute | solution.py:671
  374.3 15.0 %collective-permute-start.44 = (bf16[64,2176]{1,0:T(8,128)(2,1)}, bf16[64,2176]{1,0:T(8,128)(2,1)S(1)}, u32[]{:S(2)}, u32[]{:S(2)}) collective-permute-start(bf16[64,2176]{1,0:T(8,128)(2,1)} %shard_map.224.refs_0_), channel_id=1, source_target_pairs={{0,2},{2,4},{4,6},{6,0},{1,3},{3,5},{5,7},{7,1},{8,10},{10,12},{12... | collective-permute-start | bytes 835592 | tf_op jit(solution)/shard_map/ppermute | solution.py:791
  376.0 13.3 %collective-permute-start.45 = (bf16[64,2176]{1,0:T(8,128)(2,1)}, bf16[64,2176]{1,0:T(8,128)(2,1)S(1)}, u32[]{:S(2)}, u32[]{:S(2)}) collective-permute-start(bf16[64,2176]{1,0:T(8,128)(2,1)} %shard_map.224.refs_0_), channel_id=1, source_target_pairs={{0,6},{2,0},{4,2},{6,4},{1,7},{3,1},{5,3},{7,5},{8,14},{10,8},{12,... | collective-permute-start | bytes 835592 | tf_op jit(solution)/shard_map/ppermute | solution.py:791
  376.3 13.0 %collective-permute-start.47 = (bf16[64,2176]{1,0:T(8,128)(2,1)S(1)}, bf16[64,2176]{1,0:T(8,128)(2,1)S(1)}, u32[]{:S(2)}, u32[]{:S(2)}) collective-permute-start(bf16[64,2176]{1,0:T(8,128)(2,1)S(1)} %collective-permute-done.41.refs_1_), channel_id=1, source_target_pairs={{0,2},{2,4},{4,6},{6,0},{1,3},{3,5},{5,7},{7,1},{8,10},{10,12},{12... | collective-permute-start | bytes 835592 | tf_op jit(solution)/shard_map/ppermute | solution.py:791
  378.1 11.3 %collective-permute-start.48 = (bf16[64,2176]{1,0:T(8,128)(2,1)S(1)}, bf16[64,2176]{1,0:T(8,128)(2,1)S(1)}, u32[]{:S(2)}, u32[]{:S(2)}) collective-permute-start(bf16[64,2176]{1,0:T(8,128)(2,1)S(1)} %collective-permute-done.41.refs_1_), channel_id=1, source_target_pairs={{0,6},{2,0},{4,2},{6,4},{1,7},{3,1},{5,3},{7,5},{8,14},{10,8},{12,... | collective-permute-start | bytes 835592 | tf_op jit(solution)/shard_map/ppermute | solution.py:791
  382.0 7.4 %collective-permute-start.49 = (bf16[64,2176]{1,0:T(8,128)(2,1)S(1)}, bf16[64,2176]{1,0:T(8,128)(2,1)S(1)}, u32[]{:S(2)}, u32[]{:S(2)}) collective-permute-start(bf16[64,2176]{1,0:T(8,128)(2,1)S(1)} %collective-permute-done.46.refs_4_), channel_id=1, source_target_pairs={{0,1},{1,0},{2,3},{3,2},{4,5},{5,4},{6,7},{7,6},{8,9},{9,8},{10,11... | collective-permute-start | bytes 835592 | tf_op jit(solution)/shard_map/ppermute | solution.py:671
  (68 other events, 374.2 us)
